TPU v7x, 32 devices: a whole 2x2x4 slice. The times are simulated.
32 devices in a mesh: groups: 1, expert: 32 (over z, y, x, core).
Axes of the slice: x: 2, y: 2, z: 4, core: 2. Of those that a mesh axis runs over, the one named last changes fastest.
Arguments:
- hidden: bfloat16 [384, 4096], P(('groups', 'expert')), may hold values from -6 to 6
- expert_ids: int32 [384, 8], P(('groups', 'expert')), may hold values from 0 to 15, all different within a row; in each aligned block of 12 rows (0 to 11, 12 to 23, ...) at most 9 rows name the same one
- gate_raw: float32 [384, 8], P(('groups', 'expert')), may hold values from 0.05 to 1
- w_gate: bfloat16 [32, 4096, 384], P('expert'), may hold values from -0.09375 to 0.09375
- w_up: bfloat16 [32, 4096, 384], P('expert'), may hold values from -0.09375 to 0.09375
- w_down: bfloat16 [32, 384, 4096], P('expert'), may hold values from -0.21875 to 0.21875
Outputs:
- moe_out: bfloat16 [384, 4096], P(('groups', 'expert'))
Inputs may be any that keep to these rules, and one draw needn't show every extreme that they name: `expert_ids`: each row names 8 different experts. Among the 12 rows of one device (aligned blocks) no expert is named by more than 9 rows, a bound that some block reaches of some device in every draw.
All inputs are finite; a program needn't handle non-finite values.
Results may differ from a plain program's by a relative error of at most 0.0085.
Values may be sent and summed in bfloat16 or wider, within the bound.
No kernel may reach another device: no remote copies, remote signals or barrier semaphores. Data moves between devices by JAX's collectives and lax.ppermute only.
A program may use at most 128 MiB of HBM per device.

v0:
```python
import jax
import jax.numpy as jnp
from jax import lax
from jax.sharding import PartitionSpec as P


def slot_table(ids):
    rows, top = ids.shape
    flat = ids.reshape(rows * top)
    same = flat[:, None] == flat[None, :]
    order = jnp.arange(rows * top)
    earlier = order[None, :] < order[:, None]
    return jnp.sum(same & earlier, axis=1).reshape(rows, top)


def expert_return(buffer, w_gate, w_up, w_down):
    count, slots, width = buffer.shape
    flat = buffer.reshape(count * slots, width)
    gate = jnp.dot(flat, w_gate[0], preferred_element_type=jnp.float32)
    upper = jnp.dot(flat, w_up[0], preferred_element_type=jnp.float32)
    inner = (jax.nn.silu(gate) * upper).astype(jnp.bfloat16)
    partial_value = jnp.dot(inner, w_down[0], preferred_element_type=jnp.float32).astype(
        jnp.bfloat16
    )
    partial_value = partial_value.reshape(count, slots, width)
    return lax.all_to_all(partial_value, "expert", split_axis=0, concat_axis=0, tiled=True)


def per_device(hidden, expert_ids, gate_raw, w_gate, w_up, w_down):
    devices = lax.axis_size("expert")
    experts = devices // 2
    rows, top = expert_ids.shape
    width = hidden.shape[1]
    capacity = min(rows, max(2, 3 * rows * top // (2 * experts)))
    slot_range = jnp.arange(capacity)
    own_slots = slot_table(expert_ids)
    gathered, all_ids = (
        lax.all_gather(hidden, "expert", axis=0, tiled=True),
        lax.all_gather(expert_ids, "expert", axis=0, tiled=True),
    )
    blocks = all_ids.reshape(devices, rows, top)
    slots = jax.vmap(slot_table)(blocks)
    mine = lax.axis_index("expert") // 2
    named = (blocks == mine).astype(jnp.float32)
    slot_hit = (slots[..., None] == slot_range).astype(jnp.float32)
    select = jnp.einsum("srt,srtk->skr", named, slot_hit).astype(jnp.bfloat16)
    received = jnp.einsum(
        "skr,srd->skd",
        select,
        gathered.reshape(devices, rows, width),
        preferred_element_type=jnp.float32,
    ).astype(jnp.bfloat16)
    results = expert_return(received, w_gate, w_up, w_down)
    weight = gate_raw / jnp.sum(gate_raw, axis=1, keepdims=True)
    owner_expert = jnp.arange(devices) // 2
    device_hit = (expert_ids[:, :, None] == owner_expert).astype(jnp.float32)
    own_hit = (own_slots[:, :, None] == slot_range).astype(jnp.float32)
    combine = jnp.einsum("rt,rtj,rtk->rjk", weight, device_hit, own_hit)
    mixed = jnp.einsum(
        "rjk,jkd->rd", combine, results.astype(jnp.float32), precision=lax.Precision.HIGHEST
    )
    return mixed.astype(jnp.bfloat16)


def solution(mesh):
    placed = (
        P(("groups", "expert"), None),
        P(("groups", "expert"), None),
        P(("groups", "expert"), None),
        P("expert", None, None),
        P("expert", None, None),
        P("expert", None, None),
    )
    return jax.shard_map(
        per_device,
        mesh=mesh,
        in_specs=placed,
        out_specs=P(("groups", "expert"), None),
        check_vma=False,
    )
```

profile of v0, /device:TPU:0, one launch (start us, length us, event | category | flops | bytes accessed | tf_op | source)
XLA Modules:
  0.0 211.3 jit_solution(17803977916793229158)
XLA Ops:
  6.5 0.0 copy-start
  6.5 0.0 all-gather.4.cloned.1.call-start
  6.5 0.7 all-gather.4.cloned.1.call-update
  7.3 44.1 %all-gather = s32[32,12,8]{1,2,0:T(8,128)S(1)} all-gather(s32[1,12,8]{1,2,0:T(8,128)} %bitcast.30), channel_id=1, replica_groups=mesh['groups'=1,'expert'=32] {'expert'}, dimensions={0}, use_global_device_ids=true | all-gather | bytes 12672 | tf_op jit(solution)/shard_map/all_gather | solution.py:39
  51.4 0.1 copy.31
  51.5 0.1 copy.43
  51.7 0.1 copy.32
  51.8 1.2 convert_reduce_fusion
  53.0 0.1 copy.34
  53.0 0.2 select_reduce_fusion
  53.2 0.2 copy.42
  53.4 21.6 %all-gather.4.cloned.1.call-done = bf16[32,12,4096]{2,1,0:T(8,128)(2,1)} async-done(((bf16[1,12,4096]{2,1,0:T(8,128)(2,1)}), bf16[32,12,4096]{2,1,0:T(8,128)(2,1)}) %all-gather.4.cloned.1.call-update) | async-done | bytes 3145744 | tf_op jit(solution)/shard_map/all_gather | solution.py:38
  75.1 5.3 %convolution_convert_fusion = bf16[32,9,4096]{2,1,0:T(8,128)(2,1)} fusion(bf16[32,12,4096]{2,1,0:T(8,128)(2,1)} %all-gather.4.cloned.1.call-done, bf16[32,12,9]{1,2,0:T(8,128)(2,1)S(1)} %copy.42), kind=kOutput, calls=%fused_computation | convolution fusion | flops 29491200 | bytes 5511936 | tf_op jit(solution)/shard_map/skr,srd->skd/dot_general | solution.py:47
  80.4 4.7 %reshape.47 = bf16[288,4096]{1,0:T(8,128)(2,1)} reshape(bf16[32,9,4096]{2,1,0:T(8,128)(2,1)} %convolution_convert_fusion) | data formatting | bytes 4718592 | tf_op jit(solution)/shard_map/reshape | solution.py:18
  85.1 4.8 %fusion.4 = f32[288,384]{1,0:T(8,128)} fusion(bf16[288,4096]{1,0:T(8,128)(2,1)} %reshape.47, bf16[1,4096,384]{2,1,0:T(8,128)(2,1)} %param.9), kind=kOutput, calls=%fused_computation.7 | convolution fusion | flops 905969664 | bytes 5947392 | tf_op jit(solution)/shard_map/dot_general | solution.py:19
  89.8 0.0 copy-done
  89.9 6.8 %convolution_convert_fusion.1 = bf16[288,4096]{1,0:T(8,128)(2,1)} fusion(bf16[1,384,4096]{2,1,0:T(8,128)(2,1)S(1)} %copy-done, bf16[288,4096]{1,0:T(8,128)(2,1)} %reshape.47, bf16[1,4096,384]{2,1,0:T(8,128)(2,1)} %param.10, f32[288,384]{1,0:T(8,128)} %fusion.4), kind=kOutput, calls=%fused_computation.1 | convolution fusion | flops 1813782528 | bytes 11452416 | tf_op jit(solution)/shard_map/dot_general | solution.py:22
  96.7 4.6 %reshape.48 = bf16[32,9,4096]{2,1,0:T(8,128)(2,1)} reshape(bf16[288,4096]{1,0:T(8,128)(2,1)} %convolution_convert_fusion.1) | data formatting | bytes 4718592 | tf_op jit(solution)/shard_map/reshape | solution.py:25
  101.3 0.0 copy-start.1
  101.3 0.0 copy-start.2
  101.3 3.7 %all-to-all-start = ((bf16[32,9,4096]{2,1,0:T(8,128)(2,1)}), bf16[32,9,4096]{2,1,0:T(8,128)(2,1)}, u32[]{:S(2)}, u32[]{:S(2)}) async-start(bf16[32,9,4096]{2,1,0:T(8,128)(2,1)} %reshape.48), calls=%async_computation | async-start | bytes 8388608 | tf_op jit(solution)/shard_map/all_to_all | solution.py:26
  105.0 0.0 copy-done.1
  105.0 0.1 copy.28
  105.1 0.1 eq.85
  105.2 0.2 convert_reduce_fusion.1
  105.4 0.1 eq.89
  105.4 0.0 copy-done.2
  105.5 0.1 copy.30
  105.6 0.4 fusion.23
  106.0 93.0 %all-to-all-done = bf16[32,9,4096]{2,1,0:T(8,128)(2,1)} async-done(((bf16[32,9,4096]{2,1,0:T(8,128)(2,1)}), bf16[32,9,4096]{2,1,0:T(8,128)(2,1)}, u32[]{:S(2)}, u32[]{:S(2)}) %all-to-all-start) | async-done | bytes 2359328 | tf_op jit(solution)/shard_map/all_to_all | solution.py:26
  199.0 5.4 %fusion = bf16[12,4096]{1,0:T(8,128)(2,1)} fusion(bf16[32,9,4096]{2,1,0:T(8,128)(2,1)} %all-to-all-done, f32[12,32,9]{1,2,0:T(8,128)S(1)} %fusion.23), kind=kOutput, calls=%fused_computation.3 | convolution fusion | flops 169918464 | bytes 2471424 | tf_op jit(solution)/shard_map/rjk,jkd->rd/dot_general | solution.py:59
  (5 shorter events, 0.1 us)
Async XLA Ops:
  6.5 83.3 %copy-start = (bf16[1,384,4096]{2,1,0:T(8,128)(2,1)S(1)}, bf16[1,384,4096]{2,1,0:T(8,128)(2,1)}, u32[]{:S(2)}) copy-start(bf16[1,384,4096]{2,1,0:T(8,128)(2,1)} %param.11) | copy-start | bytes 9437188
  6.5 68.5 %all-gather.4.cloned.1.call-start = ((), (), s32[]{:S(2)}) async-start(), calls=%async_computation.1 | async-start | bytes 4325376 | tf_op jit(solution)/shard_map/all_gather | solution.py:38
  101.3 3.7 %copy-start.1 = (s32[12,8]{0,1:T(8,128)S(1)}, s32[12,8]{0,1:T(8,128)}, u32[]{:S(2)}) copy-start(s32[12,8]{0,1:T(8,128)} %param.7) | copy-start | bytes 1156
  101.3 4.2 %copy-start.2 = (f32[12,8]{0,1:T(8,128)S(1)}, f32[12,8]{0,1:T(8,128)}, u32[]{:S(2)}) copy-start(f32[12,8]{0,1:T(8,128)} %param.8) | copy-start | bytes 1156
  101.3 97.7 %all-to-all-start = ((bf16[32,9,4096]{2,1,0:T(8,128)(2,1)}), bf16[32,9,4096]{2,1,0:T(8,128)(2,1)}, u32[]{:S(2)}, u32[]{:S(2)}) async-start(bf16[32,9,4096]{2,1,0:T(8,128)(2,1)} %reshape.48), calls=%async_computation | async-start | bytes 8388608 | tf_op jit(solution)/shard_map/all_to_all | solution.py:26
Sparse Core Ops, SparseCore 0:
  10.2 64.8 all-gather.3
where the time goes:
time: 212 us; the launch traced here: 211 us
  waiting for transfers between devices  115 us (54%)
  blocking collectives  44.1 us (21%)
  matrix products  22.7 us (11%)
  between operations  13.5 us (6%)
  local copies, waits for them, and re-layouts  10.3 us (5%)
  starting transfers between devices  3.7 us (2%)
    all_to_all x1, waiting for transfers between devices, expert_return(): lax.all_to_all(partial_value, 'expert', split_axis=0, concat_axis=0, tile...  93 us
    all_gather x1, blocking collectives, per_device(): lax.all_gather(expert_ids, 'expert', axis=0, tiled=True)  44.1 us
    all_gather x1, waiting for transfers between devices, per_device(): lax.all_gather(hidden, 'expert', axis=0, tiled=True)  21.6 us
    dot_general x1, matrix products, expert_return(): jnp.dot(inner, w_down[0], preferred_element_type=jnp.float32)  6.81 us
    dot_general x1, matrix products, per_device(): jnp.einsum('rjk,jkd->rd', combine, results.astype(jnp.float32), precision...  5.44 us
    dot_general x1, matrix products, per_device(): jnp.einsum('skr,srd->skd', select, gathered.reshape(devices, rows, width)...  5.34 us
    dot_general x1, matrix products, expert_return(): gate = jnp.dot(flat, w_gate[0], preferred_element_type=jnp.float32)  4.75 us
    reshape x1, local copies, waits for them, and re-layouts, expert_return(): flat = buffer.reshape(count * slots, width)  4.69 us
  transfers between devices with their start and end apart: 2, of which 2 were waited for; matrix products, arithmetic and copies ran while one was open for 1% of the time, Pallas kernels for 0%

commit v1 on v0

v1 whole, which is shorter than its diff:
```python
import jax
import jax.numpy as jnp
from jax import lax
from jax.sharding import PartitionSpec as P

BF16 = jnp.bfloat16
F32 = jnp.float32
TILE = 8


def permute(value, devices, flip_of):
    pairs = [(device, device ^ flip_of(device)) for device in range(devices)]
    return lax.ppermute(value, "expert", pairs)


def first_flip(device):
    return 2 if device % 2 == 0 else 4


def second_flip(device):
    return 4 if device % 2 == 0 else 2


def fold(rows):
    half = rows.shape[1] // 2
    rest = rows[TILE:]
    return jnp.concatenate(
        [rows[:TILE], jnp.concatenate([rest[:, :half], rest[:, half:]], axis=0)], axis=1
    )


def unfold(block, width):
    half = width // 2
    part = TILE // 2
    rest = jnp.concatenate([block[:part, width:], block[part:, width:]], axis=1)
    return jnp.concatenate([block[:, :width], rest], axis=0)


def side_of(weight, expert_ids, experts):
    hit = expert_ids[:, :, None] == jnp.arange(experts)
    dense = jnp.sum(jnp.where(hit, weight[:, :, None], 0.0), axis=1)
    high = lax.reduce_precision(dense, 8, 7)
    low = dense - high
    return jnp.concatenate([high, low], axis=1).astype(BF16)


def expert_rows(blocks, width, experts, mine, weights):
    count = blocks.shape[0] // TILE
    part = TILE // 2
    half = width // 2
    main = blocks[:, :width]
    rest = blocks[:, width : width + half].reshape(count, 2, part, half)
    rest = rest.transpose(0, 2, 1, 3).reshape(count * part, width)
    flat = jnp.concatenate([main, rest], axis=0)
    side = blocks[:, width + half :].astype(F32)
    lane = jnp.arange(side.shape[1])
    pick = (lane == mine) | (lane == mine + experts)
    pick_rest = (lane == mine + 2 * experts) | (lane == mine + 3 * experts)
    scale = jnp.sum(jnp.where(pick, side, 0.0), axis=1)
    scale_rest = jnp.sum(jnp.where(pick_rest, side, 0.0), axis=1)
    scale_rest = scale_rest.reshape(count, TILE)[:, :part].reshape(count * part)
    scale = jnp.concatenate([scale, scale_rest])[:, None]
    total = 0.0
    for gate_mat, up_mat, down_mat in weights:
        gate = jnp.dot(flat, gate_mat, preferred_element_type=F32)
        upper = jnp.dot(flat, up_mat, preferred_element_type=F32)
        inner = (jax.nn.silu(gate) * upper * scale).astype(BF16)
        total = total + jnp.dot(inner, down_mat, preferred_element_type=F32)
    out = total.astype(BF16)
    rest = out[count * TILE :].reshape(count, part, 2, half).transpose(0, 2, 1, 3)
    return jnp.concatenate([out[: count * TILE], rest.reshape(count * TILE, half)], axis=1)


def add(a, b):
    return (a.astype(F32) + b.astype(F32)).astype(BF16)


def per_device(hidden, expert_ids, gate_raw, w_gate, w_up, w_down):
    devices = lax.axis_size("expert")
    experts = devices // 2
    levels = devices // 8
    rows, top = expert_ids.shape
    width = hidden.shape[1]
    mine = lax.axis_index("expert") // 2
    go = lambda value, flip: permute(value, devices, flip)

    weight = gate_raw / jnp.sum(gate_raw, axis=1, keepdims=True)
    side = side_of(weight, expert_ids, experts)
    spare = -(4 * experts) % 128
    side = jnp.concatenate(
        [side[:TILE], jnp.pad(side[TILE:], ((0, 2 * TILE - rows), (0, 0))), jnp.zeros((TILE, spare), BF16)],
        axis=1,
    )
    own = jnp.concatenate([fold(hidden), side], axis=1)

    level = [own] + [None] * (levels - 1)
    for step in reversed(range(1, levels)):
        level[step] = go(own, lambda device, s=step: 8 * s)
    weights = [(w_gate[0], w_up[0], w_down[0])]
    weights.append(tuple(go(w, lambda device: 1) for w in weights[0]))

    half = levels // 2
    results = []
    for group in (level[:half], level[half:]):
        here = jnp.concatenate(group, axis=0)
        pair = jnp.concatenate([here, go(here, first_flip)], axis=0)
        blocks = jnp.concatenate([pair, go(pair, second_flip)], axis=0)
        results.append(expert_rows(blocks, width, experts, mine, weights))

    sums = []
    for partial in reversed(results):
        count = partial.shape[0] // 2
        pair = add(partial[:count], go(partial[count:], second_flip))
        count = count // 2
        here = add(pair[:count], go(pair[count:], first_flip))
        sums.append(here.reshape(half, TILE, -1))
    far, near = sums
    total = near[0].astype(F32)
    for step in reversed(range(1, levels)):
        block = near[step] if step < half else far[step - half]
        total = total + go(block, lambda device, s=step: 8 * s).astype(F32)
    return unfold(total.astype(BF16), width)


def solution(mesh):
    placed = (
        P(("groups", "expert"), None),
        P(("groups", "expert"), None),
        P(("groups", "expert"), None),
        P("expert", None, None),
        P("expert", None, None),
        P("expert", None, None),
    )
    return jax.shard_map(
        per_device,
        mesh=mesh,
        in_specs=placed,
        out_specs=P(("groups", "expert"), None),
        check_vma=False,
    )
```

time: 212 us -> 101 us (0.48)
  waiting for transfers between devices: 115 us -> 41.5 us
  blocking collectives: 44.1 us -> 0 us
  starting transfers between devices: 3.7 us -> 19.5 us
  between operations: 13.5 us -> 0.36 us
  matrix products: 22.7 us -> 29 us
  local copies, waits for them, and re-layouts: 10.3 us -> 7.06 us
    all_to_all x1 -> x0, waiting for transfers between devices: 93 us -> none  [expert_return(): lax.all_to_all(partial_value, 'expert', split_axis=0, concat_axis=0, tile...]
    all_gather x1 -> x0, blocking collectives: 44.1 us -> none  [per_device(): lax.all_gather(expert_ids, 'expert', axis=0, tiled=True)]
    ppermute x0 -> x17, waiting for transfers between devices: none -> 41.5 us  [permute(): return lax.ppermute(value, 'expert', pairs)]
    all_gather x1 -> x0, waiting for transfers between devices: 21.6 us -> none  [per_device(): lax.all_gather(hidden, 'expert', axis=0, tiled=True)]
    ppermute x0 -> x17, starting transfers between devices: none -> 19.5 us  [permute(): return lax.ppermute(value, 'expert', pairs)]
    reshape x2 -> x11, local copies, waits for them, and re-layouts: 9.32 us -> 1.17 us  [the longest x3 0.5 us: expert_rows(): out[count * TILE:].reshape(count, part, 2, half).transpose(0, 2, 1, 3)]
    dot_general x5 -> x8, matrix products: 22.7 us -> 29 us  [the longest x4 20.6 us: expert_rows(): total = total + jnp.dot(inner, down_mat, preferred_element_type=F32)]
    slice x0 -> x17, local copies, waits for them, and re-layouts: none -> 4 us  [the longest x2 2.19 us: expert_rows(): out[:count * TILE]]
  transfers between devices with their start and end apart: 2 -> 17, of which waited for: 2 -> 11; matrix products, arithmetic and copies ran while one was open for 1% -> 18% of each run, Pallas kernels for 0% -> 0%
where the time goes in v1:
time: 101 us
  waiting for transfers between devices  41.5 us (41%)
  matrix products  29 us (29%)
  starting transfers between devices  19.5 us (19%)
  local copies, waits for them, and re-layouts  7.06 us (7%)
  other arithmetic  3.05 us (3%)
    ppermute x17, waiting for transfers between devices, permute(): return lax.ppermute(value, 'expert', pairs)  41.5 us
    dot_general x4, matrix products, expert_rows(): total = total + jnp.dot(inner, down_mat, preferred_element_type=F32)  20.6 us
    ppermute x17, starting transfers between devices, permute(): return lax.ppermute(value, 'expert', pairs)  19.5 us
    dot_general x2, matrix products, expert_rows(): upper = jnp.dot(flat, up_mat, preferred_element_type=F32)  5.05 us
    dot_general x2, matrix products, expert_rows(): gate = jnp.dot(flat, gate_mat, preferred_element_type=F32)  3.39 us
    slice x2, local copies, waits for them, and re-layouts, expert_rows(): out[:count * TILE]  2.19 us
  transfers between devices with their start and end apart: 17, of which 11 were waited for; matrix products, arithmetic and copies ran while one was open for 18% of the time, Pallas kernels for 0%

profile of v1, /device:TPU:0, one launch (start us, length us, event | category | flops | bytes accessed | tf_op | source)
XLA Modules:
  0.0 100.5 jit_solution(8642043065627062429)
XLA Ops:
  0.0 0.8 fusion.56
  0.8 0.8 slice.103
  1.6 0.7 reduce_sum.54
  3.1 0.8 copy.19
  4.2 5.0 %collective-permute-start.9 = (bf16[8,6272]{1,0:T(8,128)(2,1)S(1)}, bf16[8,6272]{1,0:T(8,128)(2,1)S(1)}, u32[]{:S(2)}, u32[]{:S(2)}) collective-permute-start(bf16[8,6272]{1,0:T(8,128)(2,1)S(1)} %concatenate.58), channel_id=1, source_target_pairs={{0,24},{1,25},{2,26},{3,27},{4,28},{5,29},{6,30},{7,31},{8,16},{9,... | collective-permute-start | bytes 301064 | tf_op jit(solution)/shard_map/ppermute | solution.py:13
  10.4 2.6 %collective-permute-done.9 = bf16[8,6272]{1,0:T(8,128)(2,1)S(1)} collective-permute-done((bf16[8,6272]{1,0:T(8,128)(2,1)S(1)}, bf16[8,6272]{1,0:T(8,128)(2,1)S(1)}, u32[]{:S(2)}, u32[]{:S(2)}) %collective-permute-start.9) | collective-permute-done | bytes 100384 | tf_op jit(solution)/shard_map/ppermute | solution.py:13
  13.0 4.7 %collective-permute-done.8 = bf16[8,6272]{1,0:T(8,128)(2,1)S(1)} collective-permute-done((bf16[8,6272]{1,0:T(8,128)(2,1)S(1)}, bf16[8,6272]{1,0:T(8,128)(2,1)S(1)}, u32[]{:S(2)}, u32[]{:S(2)}) %collective-permute-start.8) | collective-permute-done | bytes 100384 | tf_op jit(solution)/shard_map/ppermute | solution.py:13
  17.7 1.6 %collective-permute-start.10 = (bf16[16,6272]{1,0:T(8,128)(2,1)S(1)}, bf16[16,6272]{1,0:T(8,128)(2,1)S(1)}, u32[]{:S(2)}, u32[]{:S(2)}) collective-permute-start(bf16[16,6272]{1,0:T(8,128)(2,1)S(1)} %pad_maximum_fusion.9), channel_id=1, source_target_pairs={{0,2},{1,5},{2,0},{3,7},{4,6},{5,1},{6,4},{7,3},{8,10},{9,13},{10,... | collective-permute-start | bytes 602120 | tf_op jit(solution)/shard_map/ppermute | solution.py:13
  19.9 3.6 %collective-permute-done.10 = bf16[16,6272]{1,0:T(8,128)(2,1)S(1)} collective-permute-done((bf16[16,6272]{1,0:T(8,128)(2,1)S(1)}, bf16[16,6272]{1,0:T(8,128)(2,1)S(1)}, u32[]{:S(2)}, u32[]{:S(2)}) %collective-permute-start.10) | collective-permute-done | bytes 200736 | tf_op jit(solution)/shard_map/ppermute | solution.py:13
  23.5 1.6 %collective-permute-start.11 = (bf16[32,6272]{1,0:T(8,128)(2,1)S(1)}, bf16[32,6272]{1,0:T(8,128)(2,1)S(1)}, u32[]{:S(2)}, u32[]{:S(2)}) collective-permute-start(bf16[32,6272]{1,0:T(8,128)(2,1)S(1)} %pad_maximum_fusion.4), channel_id=1, source_target_pairs={{0,4},{1,3},{2,6},{3,1},{4,0},{5,7},{6,2},{7,5},{8,12},{9,11},{10,... | collective-permute-start | bytes 1204232 | tf_op jit(solution)/shard_map/ppermute | solution.py:13
  25.1 1.6 %collective-permute-done.1 = bf16[16,6272]{1,0:T(8,128)(2,1)S(1)} collective-permute-done((bf16[16,6272]{1,0:T(8,128)(2,1)S(1)}, bf16[16,6272]{1,0:T(8,128)(2,1)S(1)}, u32[]{:S(2)}, u32[]{:S(2)}) %collective-permute-start.1) | collective-permute-done | bytes 200736 | tf_op jit(solution)/shard_map/ppermute | solution.py:13
  26.8 1.6 %collective-permute-start.2 = (bf16[32,6272]{1,0:T(8,128)(2,1)S(1)}, bf16[32,6272]{1,0:T(8,128)(2,1)S(1)}, u32[]{:S(2)}, u32[]{:S(2)}) collective-permute-start(bf16[32,6272]{1,0:T(8,128)(2,1)S(1)} %pad_maximum_fusion.3), channel_id=1, source_target_pairs={{0,4},{1,3},{2,6},{3,1},{4,0},{5,7},{6,2},{7,5},{8,12},{9,11},{10,... | collective-permute-start | bytes 1204232 | tf_op jit(solution)/shard_map/ppermute | solution.py:13
  28.4 3.1 %collective-permute-done.11 = bf16[32,6272]{1,0:T(8,128)(2,1)S(1)} collective-permute-done((bf16[32,6272]{1,0:T(8,128)(2,1)S(1)}, bf16[32,6272]{1,0:T(8,128)(2,1)S(1)}, u32[]{:S(2)}, u32[]{:S(2)}) %collective-permute-start.11) | collective-permute-done | bytes 401440 | tf_op jit(solution)/shard_map/ppermute | solution.py:13
  31.6 4.2 %collective-permute-done.2 = bf16[32,6272]{1,0:T(8,128)(2,1)S(1)} collective-permute-done((bf16[32,6272]{1,0:T(8,128)(2,1)S(1)}, bf16[32,6272]{1,0:T(8,128)(2,1)S(1)}, u32[]{:S(2)}, u32[]{:S(2)}) %collective-permute-start.2) | collective-permute-done | bytes 401440 | tf_op jit(solution)/shard_map/ppermute | solution.py:13
  37.4 2.8 %fusion.45 = f32[96,384]{1,0:T(8,128)S(1)} fusion(bf16[1,4096,384]{2,1,0:T(8,128)(2,1)} %param.9, bf16[32,4096]{1,0:T(8,128)(2,1)S(1)} %bitcast.40, bf16[64,4096]{1,0:T(8,128)(2,1)S(1)} %slice.137), kind=kOutput, calls=%fused_computation.92 | convolution fusion | flops 303562752 | bytes 4079616 | tf_op jit(solution)/shard_map/dot_general | solution.py:65
  40.8 4.3 %fusion.6 = f32[96,4096]{1,0:T(8,128)S(1)} fusion(f32[96,384]{1,0:T(8,128)S(1)} %fusion.43, f32[96]{0:T(128)S(1)} %get-tuple-element.22, bf16[1,384,4096]{2,1,0:T(8,128)(2,1)} %param.11, bf16[1,4096,384]{2,1,0:T(8,128)(2,1)} %param.10, bf16[32,4096]{1,0:T(8,128)(2,1)S(1)} %bitcast.45, bf16[64,4096]{1,0:T(8,128)(2,1)S(1)} %slice.145), kind=kOutput, calls=%fused_computation.10 | convolution fusion | flops 605810688 | bytes 8798592 | tf_op jit(solution)/shard_map/dot_general | solution.py:68
  45.1 5.4 %fusion.7 = f32[96,4096]{1,0:T(8,128)} fusion(f32[96,384]{1,0:T(8,128)S(1)} %fusion.45, f32[96]{0:T(128)S(1)} %get-tuple-element.21, bf16[1,384,4096]{2,1,0:T(8,128)(2,1)} %param.11, bf16[1,4096,384]{2,1,0:T(8,128)(2,1)} %param.10, bf16[32,4096]{1,0:T(8,128)(2,1)S(1)} %bitcast.41, bf16[64,4096]{1,0:T(8,128)(2,1)S(1)} %slice.137), kind=kOutput, calls=%fused_computation.11 | convolution fusion | flops 605810688 | bytes 8798592 | tf_op jit(solution)/shard_map/dot_general | solution.py:68
  50.6 2.5 %fusion.53 = f32[96,384]{1,0:T(8,128)S(1)} fusion(bf16[4096,384]{1,0:T(8,128)(2,1)} %collective-permute-done.4, bf16[32,4096]{1,0:T(8,128)(2,1)S(1)} %bitcast.42, bf16[64,4096]{1,0:T(8,128)(2,1)S(1)} %slice.137), kind=kOutput, calls=%fused_computation.100 | convolution fusion | flops 303562752 | bytes 4079616 | tf_op jit(solution)/shard_map/dot_general | solution.py:66
  53.1 5.6 %fusion = bf16[96,4096]{1,0:T(8,128)(2,1)} fusion(f32[96,4096]{1,0:T(8,128)} %fusion.7, bf16[384,4096]{1,0:T(8,128)(2,1)} %collective-permute-done.5, f32[96,384]{1,0:T(8,128)S(1)} %fusion.53, f32[96]{0:T(128)S(1)} %get-tuple-element.21, bf16[4096,384]{1,0:T(8,128)(2,1)} %collective-permute-done.3, bf16[32,4096]{1,0:T(8,128)(2,1)S(1)} %bitcast.43, ...), kind=kOutput, calls=%fused_computation.2 | convolution fusion | flops 606597120 | bytes 9585024 | tf_op jit(solution)/shard_map/dot_general | solution.py:68
  58.7 1.1 %slice.138 = bf16[64,4096]{1,0:T(8,128)(2,1)S(1)} slice(bf16[96,4096]{1,0:T(8,128)(2,1)} %fusion), slice={[0:64], [0:4096]} | slice | bytes 1048576 | tf_op jit(solution)/shard_map/slice | solution.py:71
  59.8 2.5 %fusion.51 = f32[96,384]{1,0:T(8,128)S(1)} fusion(bf16[4096,384]{1,0:T(8,128)(2,1)} %collective-permute-done.4, bf16[32,4096]{1,0:T(8,128)(2,1)S(1)} %bitcast.46, bf16[64,4096]{1,0:T(8,128)(2,1)S(1)} %slice.145), kind=kOutput, calls=%fused_computation.98 | convolution fusion | flops 303562752 | bytes 4079616 | tf_op jit(solution)/shard_map/dot_general | solution.py:66
  62.4 5.3 %fusion.1 = bf16[96,4096]{1,0:T(8,128)(2,1)} fusion(f32[96,4096]{1,0:T(8,128)S(1)} %fusion.6, bf16[384,4096]{1,0:T(8,128)(2,1)} %collective-permute-done.5, f32[96,384]{1,0:T(8,128)S(1)} %fusion.51, f32[96]{0:T(128)S(1)} %get-tuple-element.22, bf16[4096,384]{1,0:T(8,128)(2,1)} %collective-permute-done.3, bf16[32,4096]{1,0:T(8,128)(2,1)S(1)} %bitcast.47, ...), kind=kOutput, calls=%fused_computation.3 | convolution fusion | flops 606597120 | bytes 9585024 | tf_op jit(solution)/shard_map/dot_general | solution.py:68
  67.6 1.1 %slice.148 = bf16[64,4096]{1,0:T(8,128)(2,1)S(1)} slice(bf16[96,4096]{1,0:T(8,128)(2,1)} %fusion.1), slice={[0:64], [0:4096]} | slice | bytes 1048576 | tf_op jit(solution)/shard_map/slice | solution.py:71
  69.6 1.7 %collective-permute-start.6 = (bf16[32,6144]{1,0:T(8,128)(2,1)S(1)}, bf16[32,6144]{1,0:T(8,128)(2,1)S(1)}, u32[]{:S(2)}, u32[]{:S(2)}) collective-permute-start(bf16[32,6144]{1,0:T(8,128)(2,1)S(1)} %pad_maximum_fusion.6), channel_id=1, source_target_pairs={{0,4},{1,3},{2,6},{3,1},{4,0},{5,7},{6,2},{7,5},{8,12},{9,11},{10,... | collective-permute-start | bytes 1179656 | tf_op jit(solution)/shard_map/ppermute | solution.py:13
  71.8 5.7 %collective-permute-done.6 = bf16[32,6144]{1,0:T(8,128)(2,1)S(1)} collective-permute-done((bf16[32,6144]{1,0:T(8,128)(2,1)S(1)}, bf16[32,6144]{1,0:T(8,128)(2,1)S(1)}, u32[]{:S(2)}, u32[]{:S(2)}) %collective-permute-start.6) | collective-permute-done | bytes 393248 | tf_op jit(solution)/shard_map/ppermute | solution.py:13
  77.6 1.6 %collective-permute-start.7 = (bf16[16,6144]{1,0:T(8,128)(2,1)S(1)}, bf16[16,6144]{1,0:T(8,128)(2,1)S(1)}, u32[]{:S(2)}, u32[]{:S(2)}) collective-permute-start(bf16[16,6144]{1,0:T(8,128)(2,1)S(1)} %slice.143), channel_id=1, source_target_pairs={{0,2},{1,5},{2,0},{3,7},{4,6},{5,1},{6,4},{7,3},{8,10},{9,13},{10,... | collective-permute-start | bytes 589832 | tf_op jit(solution)/shard_map/ppermute | solution.py:13
  79.1 6.1 %collective-permute-done.12 = bf16[32,6144]{1,0:T(8,128)(2,1)S(1)} collective-permute-done((bf16[32,6144]{1,0:T(8,128)(2,1)S(1)}, bf16[32,6144]{1,0:T(8,128)(2,1)S(1)}, u32[]{:S(2)}, u32[]{:S(2)}) %collective-permute-start.12) | collective-permute-done | bytes 393248 | tf_op jit(solution)/shard_map/ppermute | solution.py:13
  85.4 1.6 %collective-permute-start.13 = (bf16[16,6144]{1,0:T(8,128)(2,1)S(1)}, bf16[16,6144]{1,0:T(8,128)(2,1)S(1)}, u32[]{:S(2)}, u32[]{:S(2)}) collective-permute-start(bf16[16,6144]{1,0:T(8,128)(2,1)S(1)} %slice.153), channel_id=1, source_target_pairs={{0,2},{1,5},{2,0},{3,7},{4,6},{5,1},{6,4},{7,3},{8,10},{9,13},{10,... | collective-permute-start | bytes 589832 | tf_op jit(solution)/shard_map/ppermute | solution.py:13
  87.1 4.0 %collective-permute-done.13 = bf16[16,6144]{1,0:T(8,128)(2,1)S(1)} collective-permute-done((bf16[16,6144]{1,0:T(8,128)(2,1)S(1)}, bf16[16,6144]{1,0:T(8,128)(2,1)S(1)}, u32[]{:S(2)}, u32[]{:S(2)}) %collective-permute-start.13) | collective-permute-done | bytes 196640 | tf_op jit(solution)/shard_map/ppermute | solution.py:13
  91.2 2.6 %collective-permute-start.14 = (bf16[8,6144]{1,0:T(8,128)(2,1)S(1)}, bf16[8,6144]{1,0:T(8,128)(2,1)S(1)}, u32[]{:S(2)}, u32[]{:S(2)}) collective-permute-start(bf16[8,6144]{1,0:T(8,128)(2,1)S(1)} %get-tuple-element.11), channel_id=1, source_target_pairs={{0,24},{1,25},{2,26},{3,27},{4,28},{5,29},{6,30},{7,31},{8,16},{9,... | collective-permute-start | bytes 294920 | tf_op jit(solution)/shard_map/ppermute | solution.py:13
  93.8 3.9 %collective-permute-done.14 = bf16[8,6144]{1,0:T(8,128)(2,1)S(1)} collective-permute-done((bf16[8,6144]{1,0:T(8,128)(2,1)S(1)}, bf16[8,6144]{1,0:T(8,128)(2,1)S(1)}, u32[]{:S(2)}, u32[]{:S(2)}) %collective-permute-start.14) | collective-permute-done | bytes 98336 | tf_op jit(solution)/shard_map/ppermute | solution.py:13
  97.7 2.1 %collective-permute-done.15 = bf16[8,6144]{1,0:T(8,128)(2,1)S(1)} collective-permute-done((bf16[8,6144]{1,0:T(8,128)(2,1)S(1)}, bf16[8,6144]{1,0:T(8,128)(2,1)S(1)}, u32[]{:S(2)}, u32[]{:S(2)}) %collective-permute-start.15) | collective-permute-done | bytes 98336 | tf_op jit(solution)/shard_map/ppermute | solution.py:13
  (77 shorter events, 7.8 us)
Async XLA Ops:
  4.2 8.8 %collective-permute-start.9 = (bf16[8,6272]{1,0:T(8,128)(2,1)S(1)}, bf16[8,6272]{1,0:T(8,128)(2,1)S(1)}, u32[]{:S(2)}, u32[]{:S(2)}) collective-permute-start(bf16[8,6272]{1,0:T(8,128)(2,1)S(1)} %concatenate.58), channel_id=1, source_target_pairs={{0,24},{1,25},{2,26},{3,27},{4,28},{5,29},{6,30},{7,31},{8,16},{9,... | collective-permute-start | bytes 301064 | tf_op jit(solution)/shard_map/ppermute | solution.py:13
  9.3 8.4 %collective-permute-start.8 = (bf16[8,6272]{1,0:T(8,128)(2,1)S(1)}, bf16[8,6272]{1,0:T(8,128)(2,1)S(1)}, u32[]{:S(2)}, u32[]{:S(2)}) collective-permute-start(bf16[8,6272]{1,0:T(8,128)(2,1)S(1)} %concatenate.58), channel_id=1, source_target_pairs={{0,16},{1,17},{2,18},{3,19},{4,20},{5,21},{6,22},{7,23},{8,24},{9,... | collective-permute-start | bytes 301064 | tf_op jit(solution)/shard_map/ppermute | solution.py:13
  9.3 10.0 %collective-permute-start = (bf16[8,6272]{1,0:T(8,128)(2,1)S(1)}, bf16[8,6272]{1,0:T(8,128)(2,1)S(1)}, u32[]{:S(2)}, u32[]{:S(2)}) collective-permute-start(bf16[8,6272]{1,0:T(8,128)(2,1)S(1)} %concatenate.58), channel_id=1, source_target_pairs={{0,8},{1,9},{2,10},{3,11},{4,12},{5,13},{6,14},{7,15},{8,0},{9,1},... | collective-permute-start | bytes 301064 | tf_op jit(solution)/shard_map/ppermute | solution.py:13
  9.9 43.2 %collective-permute-start.5 = (bf16[384,4096]{1,0:T(8,128)(2,1)}, bf16[384,4096]{1,0:T(8,128)(2,1)}, u32[]{:S(2)}, u32[]{:S(2)}) collective-permute-start(bf16[384,4096]{1,0:T(8,128)(2,1)} %bitcast.38), channel_id=1, source_target_pairs={{0,1},{1,0},{2,3},{3,2},{4,5},{5,4},{6,7},{7,6},{8,9},{9,8},{10,11... | collective-permute-start | bytes 9437192 | tf_op jit(solution)/shard_map/ppermute | solution.py:13
  9.9 40.7 %collective-permute-start.4 = (bf16[4096,384]{1,0:T(8,128)(2,1)}, bf16[4096,384]{1,0:T(8,128)(2,1)}, u32[]{:S(2)}, u32[]{:S(2)}) collective-permute-start(bf16[4096,384]{1,0:T(8,128)(2,1)} %bitcast.37), channel_id=1, source_target_pairs={{0,1},{1,0},{2,3},{3,2},{4,5},{5,4},{6,7},{7,6},{8,9},{9,8},{10,11... | collective-permute-start | bytes 9437192 | tf_op jit(solution)/shard_map/ppermute | solution.py:13
  13.0 40.1 %collective-permute-start.3 = (bf16[4096,384]{1,0:T(8,128)(2,1)}, bf16[4096,384]{1,0:T(8,128)(2,1)}, u32[]{:S(2)}, u32[]{:S(2)}) collective-permute-start(bf16[4096,384]{1,0:T(8,128)(2,1)} %bitcast.39), channel_id=1, source_target_pairs={{0,1},{1,0},{2,3},{3,2},{4,5},{5,4},{6,7},{7,6},{8,9},{9,8},{10,11... | collective-permute-start | bytes 9437192 | tf_op jit(solution)/shard_map/ppermute | solution.py:13
  17.7 5.8 %collective-permute-start.10 = (bf16[16,6272]{1,0:T(8,128)(2,1)S(1)}, bf16[16,6272]{1,0:T(8,128)(2,1)S(1)}, u32[]{:S(2)}, u32[]{:S(2)}) collective-permute-start(bf16[16,6272]{1,0:T(8,128)(2,1)S(1)} %pad_maximum_fusion.9), channel_id=1, source_target_pairs={{0,2},{1,5},{2,0},{3,7},{4,6},{5,1},{6,4},{7,3},{8,10},{9,13},{10,... | collective-permute-start | bytes 602120 | tf_op jit(solution)/shard_map/ppermute | solution.py:13
  19.3 7.4 %collective-permute-start.1 = (bf16[16,6272]{1,0:T(8,128)(2,1)S(1)}, bf16[16,6272]{1,0:T(8,128)(2,1)S(1)}, u32[]{:S(2)}, u32[]{:S(2)}) collective-permute-start(bf16[16,6272]{1,0:T(8,128)(2,1)S(1)} %pad_maximum_fusion.8), channel_id=1, source_target_pairs={{0,2},{1,5},{2,0},{3,7},{4,6},{5,1},{6,4},{7,3},{8,10},{9,13},{10,... | collective-permute-start | bytes 602120 | tf_op jit(solution)/shard_map/ppermute | solution.py:13
  23.5 7.9 %collective-permute-start.11 = (bf16[32,6272]{1,0:T(8,128)(2,1)S(1)}, bf16[32,6272]{1,0:T(8,128)(2,1)S(1)}, u32[]{:S(2)}, u32[]{:S(2)}) collective-permute-start(bf16[32,6272]{1,0:T(8,128)(2,1)S(1)} %pad_maximum_fusion.4), channel_id=1, source_target_pairs={{0,4},{1,3},{2,6},{3,1},{4,0},{5,7},{6,2},{7,5},{8,12},{9,11},{10,... | collective-permute-start | bytes 1204232 | tf_op jit(solution)/shard_map/ppermute | solution.py:13
  26.8 9.0 %collective-permute-start.2 = (bf16[32,6272]{1,0:T(8,128)(2,1)S(1)}, bf16[32,6272]{1,0:T(8,128)(2,1)S(1)}, u32[]{:S(2)}, u32[]{:S(2)}) collective-permute-start(bf16[32,6272]{1,0:T(8,128)(2,1)S(1)} %pad_maximum_fusion.3), channel_id=1, source_target_pairs={{0,4},{1,3},{2,6},{3,1},{4,0},{5,7},{6,2},{7,5},{8,12},{9,11},{10,... | collective-permute-start | bytes 1204232 | tf_op jit(solution)/shard_map/ppermute | solution.py:13
  37.0 3.2 %copy-start = (bf16[1,4096,384]{2,1,0:T(8,128)(2,1)S(1)}, bf16[1,4096,384]{2,1,0:T(8,128)(2,1)}, u32[]{:S(2)}) copy-start(bf16[1,4096,384]{2,1,0:T(8,128)(2,1)} %param.9) | copy-start | bytes 9437188
  62.4 6.4 %slice-start.1 = ((bf16[96,4096]{1,0:T(8,128)(2,1)}), bf16[32,4096]{1,0:T(8,128)(2,1)S(1)}, s32[]{:S(2)}) async-start(bf16[96,4096]{1,0:T(8,128)(2,1)} %fusion), calls=%async_computation.1 | async-start | bytes 524288 | tf_op jit(solution)/shard_map/slice | solution.py:70
  67.6 1.5 %slice-start = ((bf16[96,4096]{1,0:T(8,128)(2,1)}), bf16[32,4096]{1,0:T(8,128)(2,1)S(1)}, s32[]{:S(2)}) async-start(bf16[96,4096]{1,0:T(8,128)(2,1)} %fusion.1), calls=%async_computation | async-start | bytes 524288 | tf_op jit(solution)/shard_map/slice | solution.py:70
  69.6 7.8 %collective-permute-start.6 = (bf16[32,6144]{1,0:T(8,128)(2,1)S(1)}, bf16[32,6144]{1,0:T(8,128)(2,1)S(1)}, u32[]{:S(2)}, u32[]{:S(2)}) collective-permute-start(bf16[32,6144]{1,0:T(8,128)(2,1)S(1)} %pad_maximum_fusion.6), channel_id=1, source_target_pairs={{0,4},{1,3},{2,6},{3,1},{4,0},{5,7},{6,2},{7,5},{8,12},{9,11},{10,... | collective-permute-start | bytes 1179656 | tf_op jit(solution)/shard_map/ppermute | solution.py:13
  71.3 14.0 %collective-permute-start.12 = (bf16[32,6144]{1,0:T(8,128)(2,1)S(1)}, bf16[32,6144]{1,0:T(8,128)(2,1)S(1)}, u32[]{:S(2)}, u32[]{:S(2)}) collective-permute-start(bf16[32,6144]{1,0:T(8,128)(2,1)S(1)} %pad_maximum_fusion.5), channel_id=1, source_target_pairs={{0,4},{1,3},{2,6},{3,1},{4,0},{5,7},{6,2},{7,5},{8,12},{9,11},{10,... | collective-permute-start | bytes 1179656 | tf_op jit(solution)/shard_map/ppermute | solution.py:13
  77.6 9.4 %collective-permute-start.7 = (bf16[16,6144]{1,0:T(8,128)(2,1)S(1)}, bf16[16,6144]{1,0:T(8,128)(2,1)S(1)}, u32[]{:S(2)}, u32[]{:S(2)}) collective-permute-start(bf16[16,6144]{1,0:T(8,128)(2,1)S(1)} %slice.143), channel_id=1, source_target_pairs={{0,2},{1,5},{2,0},{3,7},{4,6},{5,1},{6,4},{7,3},{8,10},{9,13},{10,... | collective-permute-start | bytes 589832 | tf_op jit(solution)/shard_map/ppermute | solution.py:13
  85.4 5.7 %collective-permute-start.13 = (bf16[16,6144]{1,0:T(8,128)(2,1)S(1)}, bf16[16,6144]{1,0:T(8,128)(2,1)S(1)}, u32[]{:S(2)}, u32[]{:S(2)}) collective-permute-start(bf16[16,6144]{1,0:T(8,128)(2,1)S(1)} %slice.153), channel_id=1, source_target_pairs={{0,2},{1,5},{2,0},{3,7},{4,6},{5,1},{6,4},{7,3},{8,10},{9,13},{10,... | collective-permute-start | bytes 589832 | tf_op jit(solution)/shard_map/ppermute | solution.py:13
  87.0 6.8 %collective-permute-start.16 = (bf16[8,6144]{1,0:T(8,128)(2,1)S(1)}, bf16[8,6144]{1,0:T(8,128)(2,1)S(1)}, u32[]{:S(2)}, u32[]{:S(2)}) collective-permute-start(bf16[8,6144]{1,0:T(8,128)(2,1)S(1)} %slice.156), channel_id=1, source_target_pairs={{0,8},{1,9},{2,10},{3,11},{4,12},{5,13},{6,14},{7,15},{8,0},{9,1},... | collective-permute-start | bytes 294920 | tf_op jit(solution)/shard_map/ppermute | solution.py:13
  91.2 6.5 %collective-permute-start.14 = (bf16[8,6144]{1,0:T(8,128)(2,1)S(1)}, bf16[8,6144]{1,0:T(8,128)(2,1)S(1)}, u32[]{:S(2)}, u32[]{:S(2)}) collective-permute-start(bf16[8,6144]{1,0:T(8,128)(2,1)S(1)} %get-tuple-element.11), channel_id=1, source_target_pairs={{0,24},{1,25},{2,26},{3,27},{4,28},{5,29},{6,30},{7,31},{8,16},{9,... | collective-permute-start | bytes 294920 | tf_op jit(solution)/shard_map/ppermute | solution.py:13
  93.8 6.0 %collective-permute-start.15 = (bf16[8,6144]{1,0:T(8,128)(2,1)S(1)}, bf16[8,6144]{1,0:T(8,128)(2,1)S(1)}, u32[]{:S(2)}, u32[]{:S(2)}) collective-permute-start(bf16[8,6144]{1,0:T(8,128)(2,1)S(1)} %get-tuple-element.12), channel_id=1, source_target_pairs={{0,16},{1,17},{2,18},{3,19},{4,20},{5,21},{6,22},{7,23},{8,24},{9,... | collective-permute-start | bytes 294920 | tf_op jit(solution)/shard_map/ppermute | solution.py:13

commit v2 on v1

v2 whole, which is shorter than its diff:
```python
import functools

import jax
import jax.numpy as jnp
from jax import lax
from jax.experimental import pallas as pl
from jax.experimental.pallas import tpu as pltpu
from jax.sharding import PartitionSpec as P

BF16 = jnp.bfloat16
F32 = jnp.float32
TILE = 8
STEP = 512
NSTEP = 512


def permute(value, devices, flip_of):
    pairs = [(device, device ^ flip_of(device)) for device in range(devices)]
    return lax.ppermute(value, "expert", pairs)


def first_flip(device):
    return 2 if device % 2 == 0 else 4


def second_flip(device):
    return 4 if device % 2 == 0 else 2


def fold(rows):
    half = rows.shape[1] // 2
    rest = rows[TILE:]
    return jnp.concatenate(
        [rows[:TILE], jnp.concatenate([rest[:, :half], rest[:, half:]], axis=0)], axis=1
    )


def unfold(block, width):
    half = width // 2
    part = TILE // 2
    rest = jnp.concatenate([block[:part, width:], block[part:, width:]], axis=1)
    return jnp.concatenate([block[:, :width], rest], axis=0)


def side_of(weight, expert_ids, experts):
    hit = expert_ids[:, :, None] == jnp.arange(experts)
    dense = jnp.sum(jnp.where(hit, weight[:, :, None], 0.0), axis=1)
    high = lax.reduce_precision(dense, 8, 7)
    low = dense - high
    return jnp.concatenate([high, low], axis=1).astype(BF16)


def swap_halves(value):
    rows, width = value.shape
    tiles = value.reshape(rows // TILE, TILE, width)
    return pltpu.roll(tiles, TILE // 2, 1).reshape(rows, width)


def expert_kernel(experts, width, mine, here, first, second, *refs):
    weights, (keep, send), inner = refs[:6], refs[6:8], refs[8]
    half = width // 2
    parts = (here, first, second)
    rows = sum(part.shape[0] for part in parts)
    upper = lax.broadcasted_iota(jnp.int32, (rows, 1), 0) % TILE < TILE // 2

    side = jnp.concatenate([part[:, width + half :] for part in parts], axis=0).astype(F32)
    lane = lax.broadcasted_iota(jnp.int32, side.shape, 1)
    turn = lane - mine[0]
    scale = jnp.sum(jnp.where((turn == 0) | (turn == experts), side, 0.0), axis=1, keepdims=True)
    turn = turn - 2 * experts
    scale_rest = jnp.sum(jnp.where((turn == 0) | (turn == experts), side, 0.0), axis=1, keepdims=True)

    def columns(start, size):
        return [part[:, start : start + size] for part in parts]

    def product(mat):
        low = high = None
        for start in range(0, half, STEP):
            rest = columns(width + start, STEP)
            a = jnp.concatenate(columns(start, STEP) + rest, axis=0)
            b = jnp.concatenate(columns(half + start, STEP) + rest, axis=0)
            u = jnp.dot(a, mat[start : start + STEP], preferred_element_type=F32)
            v = jnp.dot(b, mat[half + start : half + start + STEP], preferred_element_type=F32)
            low = u if low is None else low + u
            high = v if high is None else high + v
        rest = jnp.where(upper, low[rows:], high[rows:])
        return low[:rows] + high[:rows], rest + swap_halves(rest)

    hidden_units = weights[0].shape[1]
    for side_of_chip in range(2):
        gate, gate_rest = product(weights[3 * side_of_chip])
        up, up_rest = product(weights[3 * side_of_chip + 1])
        at = side_of_chip * hidden_units
        inner[:rows, at : at + hidden_units] = (jax.nn.silu(gate) * up * scale).astype(BF16)
        inner[rows:, at : at + hidden_units] = (jax.nn.silu(gate_rest) * up_rest * scale_rest).astype(BF16)

    def down(start):
        return sum(
            jnp.dot(
                inner[:, at * hidden_units : (at + 1) * hidden_units],
                weights[3 * at + 2][:, start : start + NSTEP],
                preferred_element_type=F32,
            )
            for at in range(2)
        )

    kept = keep.shape[0]
    for start in range(0, half, NSTEP):
        low, high = down(start), down(half + start)
        rest = jnp.where(upper, low[rows:], high[rows:])
        for value, at in ((low, start), (high, half + start), (rest, width + start)):
            value = value[:rows].astype(BF16)
            keep[:, at : at + NSTEP] = value[:kept]
            send[:, at : at + NSTEP] = value[kept:]


def expert_rows(parts, width, mine, experts, weights):
    rows = sum(part.shape[0] for part in parts)
    out = jax.ShapeDtypeStruct((rows // 2, width + width // 2), BF16)
    flat = [pltpu.with_memory_space_constraint(w, pltpu.VMEM) for half in weights for w in half]
    units = flat[0].shape[1]
    vmem = pl.BlockSpec(memory_space=pltpu.VMEM)
    return pl.pallas_call(
        functools.partial(expert_kernel, experts, width),
        out_shape=(out, out),
        in_specs=[pl.BlockSpec(memory_space=pltpu.SMEM)] + [vmem] * (3 + len(flat)),
        out_specs=(vmem, vmem),
        scratch_shapes=[pltpu.VMEM((2 * rows, 2 * units), BF16)],
        compiler_params=pltpu.CompilerParams(vmem_limit_bytes=24 << 20),
    )(mine, *parts, *flat)


def add(a, b):
    return (a.astype(F32) + b.astype(F32)).astype(BF16)


def per_device(hidden, expert_ids, gate_raw, w_gate, w_up, w_down):
    devices = lax.axis_size("expert")
    experts = devices // 2
    levels = devices // 8
    rows, top = expert_ids.shape
    width = hidden.shape[1]
    mine = (lax.axis_index("expert") // 2).reshape(1)
    go = lambda value, flip: permute(value, devices, flip)

    weight = gate_raw / jnp.sum(gate_raw, axis=1, keepdims=True)
    side = side_of(weight, expert_ids, experts)
    spare = -(4 * experts) % 128
    side = jnp.concatenate(
        [side[:TILE], jnp.concatenate([side[TILE:]] * 2, axis=0), jnp.zeros((TILE, spare), BF16)],
        axis=1,
    )
    own = jnp.concatenate([fold(hidden), side], axis=1)

    level = [own] + [None] * (levels - 1)
    for step in reversed(range(1, levels)):
        level[step] = go(own, lambda device, s=step: 8 * s)
    weights = [(w_gate[0], w_up[0], w_down[0])]
    weights.append(tuple(go(w, lambda device: 1) for w in weights[0]))

    half = levels // 2
    results = []
    for group in (level[:half], level[half:]):
        here = jnp.concatenate(group, axis=0)
        first = go(here, first_flip)
        second = go(jnp.concatenate([here, first], axis=0), second_flip)
        results.append(expert_rows((here, first, second), width, mine, experts, weights))

    sums = []
    for keep, send in reversed(results):
        pair = add(keep, go(send, second_flip))
        count = pair.shape[0] // 2
        here = add(pair[:count], go(pair[count:], first_flip))
        sums.append(here.reshape(half, TILE, -1))
    far, near = sums
    total = near[0].astype(F32)
    for step in reversed(range(1, levels)):
        block = near[step] if step < half else far[step - half]
        total = total + go(block, lambda device, s=step: 8 * s).astype(F32)
    return unfold(total.astype(BF16), width)


def solution(mesh):
    placed = (
        P(("groups", "expert"), None),
        P(("groups", "expert"), None),
        P(("groups", "expert"), None),
        P("expert", None, None),
        P("expert", None, None),
        P("expert", None, None),
    )
    return jax.shard_map(
        per_device,
        mesh=mesh,
        in_specs=placed,
        out_specs=P(("groups", "expert"), None),
        check_vma=False,
    )
```

time: 101 us -> 75.2 us (0.74)
  matrix products: 29 us -> 0 us
  waiting for transfers between devices: 41.5 us -> 22.4 us
  Pallas kernels: 0 us -> 13.2 us
  starting transfers between devices: 19.5 us -> 23.5 us
  local copies, waits for them, and re-layouts: 7.06 us -> 10.2 us
  other arithmetic: 3.05 us -> 5.23 us
    dot_general x8 -> x0, matrix products: 29 us -> none  [the longest x4 20.6 us: expert_rows(): total = total + jnp.dot(inner, down_mat, preferred_element_type=F32)]
    ppermute x17, waiting for transfers between devices: 41.5 us -> 22.4 us  [permute(): return lax.ppermute(value, 'expert', pairs)]
    pallas_call x0 -> x2, Pallas kernels: none -> 13.2 us  [expert_rows(): pl.pallas_call(functools.partial(expert_kernel, experts, width), out_shap...]
    unnamed x8 -> x20, local copies, waits for them, and re-layouts: 0.99 us -> 8.31 us
    ppermute x17, starting transfers between devices: 19.5 us -> 23.5 us  [permute(): return lax.ppermute(value, 'expert', pairs)]
    slice x9 -> x0, local copies, waits for them, and re-layouts: 2.29 us -> none  [the longest x2 2.19 us: expert_rows(): out[:count * TILE]]
    concatenate x6 -> x2, other arithmetic: 0.27 us -> 2.51 us  [per_device(): second = go(jnp.concatenate([here, first], axis=0), second_flip)]
    reshape x11 -> x0, local copies, waits for them, and re-layouts: 1.17 us -> none  [the longest x3 0.5 us: expert_rows(): out[count * TILE:].reshape(count, part, 2, half).transpose(0, 2, 1, 3)]
  transfers between devices with their start and end apart: 17 -> 17, of which waited for: 11 -> 6; matrix products, arithmetic and copies ran while one was open for 18% -> 4% of each run, Pallas kernels for 0% -> 18%
where the time goes in v2:
time: 75.2 us; the launch traced here: 74.7 us
  starting transfers between devices  23.5 us (31%)
  waiting for transfers between devices  22.4 us (30%)
  Pallas kernels  13.2 us (18%)
  local copies, waits for them, and re-layouts  10.2 us (14%)
  other arithmetic  5.23 us (7%)
    ppermute x17, starting transfers between devices, permute(): return lax.ppermute(value, 'expert', pairs)  23.5 us
    ppermute x17, waiting for transfers between devices, permute(): return lax.ppermute(value, 'expert', pairs)  22.4 us
    pallas_call x2, Pallas kernels, expert_rows(): pl.pallas_call(functools.partial(expert_kernel, experts, width), out_shap...  13.2 us
    unnamed x20, local copies, waits for them, and re-layouts  8.31 us
    concatenate x2, other arithmetic, per_device(): second = go(jnp.concatenate([here, first], axis=0), second_flip)  2.51 us
  transfers between devices with their start and end apart: 17, of which 6 were waited for; matrix products, arithmetic and copies ran while one was open for 4% of the time, Pallas kernels for 18%

profile of v2, /device:TPU:0, one launch (start us, length us, event | category | flops | bytes accessed | tf_op | source)
XLA Modules:
  0.0 74.7 jit_solution(14956739553642274034)
XLA Ops:
  0.0 0.8 %fusion.3 = (bf16[4,2048]{1,0:T(4,128)(2,1)S(1)}, bf16[4,2048]{1,0:T(4,128)(2,1)S(1)}) fusion(bf16[12,4096]{1,0:T(8,128)(2,1)} %param.6), kind=kLoop, calls=%fused_computation.24 | loop fusion | bytes 65536 | tf_op jit(solution)/shard_map/slice | solution.py:34
  0.8 0.8 %slice.55 = bf16[8,4096]{1,0:T(8,128)(2,1)S(1)} slice(bf16[12,4096]{1,0:T(8,128)(2,1)} %param.6), slice={[0:8], [0:4096]} | slice | bytes 131072 | tf_op jit(solution)/shard_map/slice | solution.py:34
  1.6 0.7 reduce_sum.18
  2.3 0.7 broadcast_divide_fusion
  3.1 0.8 %copy.9 = s32[12,8]{1,0:T(8,128)S(1)} copy(s32[12,8]{0,1:T(8,128)} %param.7) | data formatting | bytes 768 | tf_op args[1]
  4.3 4.0 %collective-permute-start.8 = (bf16[8,6272]{1,0:T(8,128)(2,1)S(1)}, bf16[8,6272]{1,0:T(8,128)(2,1)S(1)}, u32[]{:S(2)}, u32[]{:S(2)}) collective-permute-start(bf16[8,6272]{1,0:T(8,128)(2,1)S(1)} %concatenate.36), channel_id=1, source_target_pairs={{0,16},{1,17},{2,18},{3,19},{4,20},{5,21},{6,22},{7,23},{8,24},{9,... | collective-permute-start | bytes 301064 | tf_op jit(solution)/shard_map/ppermute | solution.py:19
  8.3 1.3 %collective-permute-start.9 = (bf16[8,6272]{1,0:T(8,128)(2,1)S(1)}, bf16[8,6272]{1,0:T(8,128)(2,1)S(1)}, u32[]{:S(2)}, u32[]{:S(2)}) collective-permute-start(bf16[8,6272]{1,0:T(8,128)(2,1)S(1)} %concatenate.36), channel_id=1, source_target_pairs={{0,24},{1,25},{2,26},{3,27},{4,28},{5,29},{6,30},{7,31},{8,16},{9,... | collective-permute-start | bytes 301064 | tf_op jit(solution)/shard_map/ppermute | solution.py:19
  10.4 5.9 %collective-permute-done.8 = bf16[8,6272]{1,0:T(8,128)(2,1)S(1)} collective-permute-done((bf16[8,6272]{1,0:T(8,128)(2,1)S(1)}, bf16[8,6272]{1,0:T(8,128)(2,1)S(1)}, u32[]{:S(2)}, u32[]{:S(2)}) %collective-permute-start.8) | collective-permute-done | bytes 100384 | tf_op jit(solution)/shard_map/ppermute | solution.py:19
  16.4 1.8 %collective-permute-start.10 = (bf16[16,6272]{1,0:T(8,128)(2,1)S(1)}, bf16[16,6272]{1,0:T(8,128)(2,1)S(1)}, u32[]{:S(2)}, u32[]{:S(2)}) collective-permute-start(bf16[16,6272]{1,0:T(8,128)(2,1)S(1)} %constant_dynamic-update-slice_fusion.here), channel_id=1, source_target_pairs={{0,2},{1,5},{2,0},{3,7},{4,6},{5,1},{6,4},{7,3},{8,10},{9,13},{10,... | collective-permute-start | bytes 602120 | tf_op jit(solution)/shard_map/ppermute | solution.py:19
  18.8 3.4 %collective-permute-done.10.first = bf16[16,6272]{1,0:T(8,128)(2,1)S(1)} collective-permute-done((bf16[16,6272]{1,0:T(8,128)(2,1)S(1)}, bf16[16,6272]{1,0:T(8,128)(2,1)S(1)}, u32[]{:S(2)}, u32[]{:S(2)}) %collective-permute-start.10) | collective-permute-done | bytes 200736 | tf_op jit(solution)/shard_map/ppermute | solution.py:19
  22.2 0.8 %pad_maximum_fusion.1 = bf16[32,6272]{1,0:T(8,128)(2,1)} fusion(bf16[16,6272]{1,0:T(8,128)(2,1)S(1)} %collective-permute-done.10.first, bf16[8,6272]{1,0:T(8,128)(2,1)S(1)} %collective-permute-done.9, bf16[8,6272]{1,0:T(8,128)(2,1)S(1)} %collective-permute-done.8), kind=kLoop, calls=%fused_computation.3 | loop fusion | flops 1204224 | bytes 802816 | tf_op jit(solution)/shard_map/concatenate | solution.py:166
  23.0 1.8 %collective-permute-start.11 = (bf16[32,6272]{1,0:T(8,128)(2,1)}, bf16[32,6272]{1,0:T(8,128)(2,1)}, u32[]{:S(2)}, u32[]{:S(2)}) collective-permute-start(bf16[32,6272]{1,0:T(8,128)(2,1)} %pad_maximum_fusion.1), channel_id=1, source_target_pairs={{0,4},{1,3},{2,6},{3,1},{4,0},{5,7},{6,2},{7,5},{8,12},{9,11},{10,... | collective-permute-start | bytes 1204232 | tf_op jit(solution)/shard_map/ppermute | solution.py:19
  24.8 1.7 %pad_maximum_fusion = bf16[32,6272]{1,0:T(8,128)(2,1)} fusion(bf16[16,6272]{1,0:T(8,128)(2,1)S(1)} %collective-permute-done.1.first, bf16[8,6272]{1,0:T(8,128)(2,1)S(1)} %collective-permute-done, bf16[8,6272]{1,0:T(8,128)(2,1)} %copy-done.8), kind=kLoop, calls=%fused_computation.2 | loop fusion | flops 1204224 | bytes 802816 | tf_op jit(solution)/shard_map/concatenate | solution.py:166
  26.5 1.3 %collective-permute-start.2 = (bf16[32,6272]{1,0:T(8,128)(2,1)}, bf16[32,6272]{1,0:T(8,128)(2,1)}, u32[]{:S(2)}, u32[]{:S(2)}) collective-permute-start(bf16[32,6272]{1,0:T(8,128)(2,1)} %pad_maximum_fusion), channel_id=1, source_target_pairs={{0,4},{1,3},{2,6},{3,1},{4,0},{5,7},{6,2},{7,5},{8,12},{9,11},{10,... | collective-permute-start | bytes 1204232 | tf_op jit(solution)/shard_map/ppermute | solution.py:19
  27.8 3.4 %collective-permute-done.11.second = bf16[32,6272]{1,0:T(8,128)(2,1)} collective-permute-done((bf16[32,6272]{1,0:T(8,128)(2,1)}, bf16[32,6272]{1,0:T(8,128)(2,1)}, u32[]{:S(2)}, u32[]{:S(2)}) %collective-permute-start.11) | collective-permute-done | bytes 401440 | tf_op jit(solution)/shard_map/ppermute | solution.py:19
  31.2 1.9 %copy-done = bf16[1,4096,384]{2,1,0:T(8,128)(2,1)S(1)} copy-done((bf16[1,4096,384]{2,1,0:T(8,128)(2,1)S(1)}, bf16[1,4096,384]{2,1,0:T(8,128)(2,1)}, u32[]{:S(2)}) %copy-start) | copy-done | bytes 3145752
  33.1 1.9 %copy-done.2 = bf16[1,4096,384]{2,1,0:T(8,128)(2,1)S(1)} copy-done((bf16[1,4096,384]{2,1,0:T(8,128)(2,1)S(1)}, bf16[1,4096,384]{2,1,0:T(8,128)(2,1)}, u32[]{:S(2)}) %copy-start.2) | copy-done | bytes 3145752
  35.0 1.9 %copy-done.3 = bf16[1,384,4096]{2,1,0:T(8,128)(2,1)S(1)} copy-done((bf16[1,384,4096]{2,1,0:T(8,128)(2,1)S(1)}, bf16[1,384,4096]{2,1,0:T(8,128)(2,1)}, u32[]{:S(2)}) %copy-start.3) | copy-done | bytes 3145752
  36.9 0.9 %copy-done.5 = bf16[16,6272]{1,0:T(8,128)(2,1)S(1)} copy-done((bf16[16,6272]{1,0:T(8,128)(2,1)S(1)}, bf16[16,6272]{1,0:T(8,128)(2,1)}, u32[]{:S(2)}) %copy-start.5) | copy-done | bytes 200728
  37.8 0.9 %copy-done.7 = bf16[16,6272]{1,0:T(8,128)(2,1)S(1)} copy-done((bf16[16,6272]{1,0:T(8,128)(2,1)S(1)}, bf16[16,6272]{1,0:T(8,128)(2,1)}, u32[]{:S(2)}) %copy-start.7) | copy-done | bytes 200728
  38.8 6.7 %shard_map.65 = (bf16[32,6144]{1,0:T(8,128)(2,1)S(1)}, bf16[32,6144]{1,0:T(8,128)(2,1)S(1)}) custom-call(s32[1]{0:T(128)} %bitcast.mine, bf16[16,6272]{1,0:T(8,128)(2,1)S(1)} %copy-done.7, bf16[16,6272]{1,0:T(8,128)(2,1)S(1)} %copy-done.5, bf16[32,6272]{1,0:T(8,128)(2,1)} %collective-permute-done.11.second, bf16[4096,384]{1,0:T(8,128)(2,1)S(1)} %bitcast.5, ...), custom_call_target="tpu_custom_call" | custom-call | tf_op jit(solution)/shard_map/pallas_call | solution.py:123
  45.4 1.8 %collective-permute-start.12 = (bf16[32,6144]{1,0:T(8,128)(2,1)S(1)}, bf16[32,6144]{1,0:T(8,128)(2,1)S(1)}, u32[]{:S(2)}, u32[]{:S(2)}) collective-permute-start(bf16[32,6144]{1,0:T(8,128)(2,1)S(1)} %get-tuple-element.12), channel_id=1, source_target_pairs={{0,4},{1,3},{2,6},{3,1},{4,0},{5,7},{6,2},{7,5},{8,12},{9,11},{10,... | collective-permute-start | bytes 1179656 | tf_op jit(solution)/shard_map/ppermute | solution.py:19
  47.3 6.5 %shard_map.64 = (bf16[32,6144]{1,0:T(8,128)(2,1)S(1)}, bf16[32,6144]{1,0:T(8,128)(2,1)S(1)}) custom-call(s32[1]{0:T(128)} %bitcast.mine, bf16[16,6272]{1,0:T(8,128)(2,1)S(1)} %pad_maximum_fusion.2.here, bf16[16,6272]{1,0:T(8,128)(2,1)S(1)} %collective-permute-done.1.first, bf16[32,6272]{1,0:T(8,128)(2,1)} %collective-permute-done.2.second, ...), custom_call_target="tpu_custom_call" | custom-call | tf_op jit(solution)/shard_map/pallas_call | solution.py:123
  54.3 1.8 %collective-permute-start.13 = (bf16[16,6144]{1,0:T(8,128)(2,1)S(1)}, bf16[16,6144]{1,0:T(8,128)(2,1)S(1)}, u32[]{:S(2)}, u32[]{:S(2)}) collective-permute-start(bf16[16,6144]{1,0:T(8,128)(2,1)S(1)} %slice.77), channel_id=1, source_target_pairs={{0,2},{1,5},{2,0},{3,7},{4,6},{5,1},{6,4},{7,3},{8,10},{9,13},{10,... | collective-permute-start | bytes 589832 | tf_op jit(solution)/shard_map/ppermute | solution.py:19
  56.1 5.6 %collective-permute-done.6 = bf16[32,6144]{1,0:T(8,128)(2,1)S(1)} collective-permute-done((bf16[32,6144]{1,0:T(8,128)(2,1)S(1)}, bf16[32,6144]{1,0:T(8,128)(2,1)S(1)}, u32[]{:S(2)}, u32[]{:S(2)}) %collective-permute-start.6) | collective-permute-done | bytes 393248 | tf_op jit(solution)/shard_map/ppermute | solution.py:19
  61.8 2.0 %collective-permute-start.7 = (bf16[16,6144]{1,0:T(8,128)(2,1)S(1)}, bf16[16,6144]{1,0:T(8,128)(2,1)S(1)}, u32[]{:S(2)}, u32[]{:S(2)}) collective-permute-start(bf16[16,6144]{1,0:T(8,128)(2,1)S(1)} %slice.74), channel_id=1, source_target_pairs={{0,2},{1,5},{2,0},{3,7},{4,6},{5,1},{6,4},{7,3},{8,10},{9,13},{10,... | collective-permute-start | bytes 589832 | tf_op jit(solution)/shard_map/ppermute | solution.py:19
  63.8 2.8 %collective-permute-start.14 = (bf16[8,6144]{1,0:T(8,128)(2,1)S(1)}, bf16[8,6144]{1,0:T(8,128)(2,1)S(1)}, u32[]{:S(2)}, u32[]{:S(2)}) collective-permute-start(bf16[8,6144]{1,0:T(8,128)(2,1)S(1)} %get-tuple-element.13), channel_id=1, source_target_pairs={{0,24},{1,25},{2,26},{3,27},{4,28},{5,29},{6,30},{7,31},{8,16},{9,... | collective-permute-start | bytes 294920 | tf_op jit(solution)/shard_map/ppermute | solution.py:19
  66.7 1.5 %collective-permute-start.15 = (bf16[8,6144]{1,0:T(8,128)(2,1)S(1)}, bf16[8,6144]{1,0:T(8,128)(2,1)S(1)}, u32[]{:S(2)}, u32[]{:S(2)}) collective-permute-start(bf16[8,6144]{1,0:T(8,128)(2,1)S(1)} %get-tuple-element.14), channel_id=1, source_target_pairs={{0,16},{1,17},{2,18},{3,19},{4,20},{5,21},{6,22},{7,23},{8,24},{9,... | collective-permute-start | bytes 294920 | tf_op jit(solution)/shard_map/ppermute | solution.py:19
  68.3 1.6 %collective-permute-start.16 = (bf16[8,6144]{1,0:T(8,128)(2,1)S(1)}, bf16[8,6144]{1,0:T(8,128)(2,1)S(1)}, u32[]{:S(2)}, u32[]{:S(2)}) collective-permute-start(bf16[8,6144]{1,0:T(8,128)(2,1)S(1)} %slice.80), channel_id=1, source_target_pairs={{0,8},{1,9},{2,10},{3,11},{4,12},{5,13},{6,14},{7,15},{8,0},{9,1},... | collective-permute-start | bytes 294920 | tf_op jit(solution)/shard_map/ppermute | solution.py:19
  69.9 1.0 %collective-permute-done.14 = bf16[8,6144]{1,0:T(8,128)(2,1)S(1)} collective-permute-done((bf16[8,6144]{1,0:T(8,128)(2,1)S(1)}, bf16[8,6144]{1,0:T(8,128)(2,1)S(1)}, u32[]{:S(2)}, u32[]{:S(2)}) %collective-permute-start.14) | collective-permute-done | bytes 98336 | tf_op jit(solution)/shard_map/ppermute | solution.py:19
  70.9 3.1 %collective-permute-done.15 = bf16[8,6144]{1,0:T(8,128)(2,1)S(1)} collective-permute-done((bf16[8,6144]{1,0:T(8,128)(2,1)S(1)}, bf16[8,6144]{1,0:T(8,128)(2,1)S(1)}, u32[]{:S(2)}, u32[]{:S(2)}) %collective-permute-start.15) | collective-permute-done | bytes 98336 | tf_op jit(solution)/shard_map/ppermute | solution.py:19
  74.0 0.7 maximum_maximum_fusion
  (52 shorter events, 2.6 us)
Async XLA Ops:
  4.3 13.9 %copy-start.8 = (bf16[8,6272]{1,0:T(8,128)(2,1)}, bf16[8,6272]{1,0:T(8,128)(2,1)S(1)}, u32[]{:S(2)}) copy-start(bf16[8,6272]{1,0:T(8,128)(2,1)S(1)} %concatenate.36) | copy-start | bytes 301060
  4.3 12.1 %collective-permute-start.8 = (bf16[8,6272]{1,0:T(8,128)(2,1)S(1)}, bf16[8,6272]{1,0:T(8,128)(2,1)S(1)}, u32[]{:S(2)}, u32[]{:S(2)}) collective-permute-start(bf16[8,6272]{1,0:T(8,128)(2,1)S(1)} %concatenate.36), channel_id=1, source_target_pairs={{0,16},{1,17},{2,18},{3,19},{4,20},{5,21},{6,22},{7,23},{8,24},{9,... | collective-permute-start | bytes 301064 | tf_op jit(solution)/shard_map/ppermute | solution.py:19
  8.3 8.0 %collective-permute-start.9 = (bf16[8,6272]{1,0:T(8,128)(2,1)S(1)}, bf16[8,6272]{1,0:T(8,128)(2,1)S(1)}, u32[]{:S(2)}, u32[]{:S(2)}) collective-permute-start(bf16[8,6272]{1,0:T(8,128)(2,1)S(1)} %concatenate.36), channel_id=1, source_target_pairs={{0,24},{1,25},{2,26},{3,27},{4,28},{5,29},{6,30},{7,31},{8,16},{9,... | collective-permute-start | bytes 301064 | tf_op jit(solution)/shard_map/ppermute | solution.py:19
  9.7 8.5 %collective-permute-start = (bf16[8,6272]{1,0:T(8,128)(2,1)S(1)}, bf16[8,6272]{1,0:T(8,128)(2,1)S(1)}, u32[]{:S(2)}, u32[]{:S(2)}) collective-permute-start(bf16[8,6272]{1,0:T(8,128)(2,1)S(1)} %concatenate.36), channel_id=1, source_target_pairs={{0,8},{1,9},{2,10},{3,11},{4,12},{5,13},{6,14},{7,15},{8,0},{9,1},... | collective-permute-start | bytes 301064 | tf_op jit(solution)/shard_map/ppermute | solution.py:19
  9.9 21.3 %collective-permute-start.3 = (bf16[4096,384]{1,0:T(8,128)(2,1)}, bf16[4096,384]{1,0:T(8,128)(2,1)S(1)}, u32[]{:S(2)}, u32[]{:S(2)}) collective-permute-start(bf16[4096,384]{1,0:T(8,128)(2,1)} %bitcast.4), channel_id=1, source_target_pairs={{0,1},{1,0},{2,3},{3,2},{4,5},{5,4},{6,7},{7,6},{8,9},{9,8},{10,11... | collective-permute-start | bytes 9437192 | tf_op jit(solution)/shard_map/ppermute | solution.py:19
  9.9 21.3 %collective-permute-start.4 = (bf16[4096,384]{1,0:T(8,128)(2,1)}, bf16[4096,384]{1,0:T(8,128)(2,1)}, u32[]{:S(2)}, u32[]{:S(2)}) collective-permute-start(bf16[4096,384]{1,0:T(8,128)(2,1)} %bitcast.7), channel_id=1, source_target_pairs={{0,1},{1,0},{2,3},{3,2},{4,5},{5,4},{6,7},{7,6},{8,9},{9,8},{10,11... | collective-permute-start | bytes 9437192 | tf_op jit(solution)/shard_map/ppermute | solution.py:19
  16.4 14.9 %collective-permute-start.5 = (bf16[384,4096]{1,0:T(8,128)(2,1)}, bf16[384,4096]{1,0:T(8,128)(2,1)}, u32[]{:S(2)}, u32[]{:S(2)}) collective-permute-start(bf16[384,4096]{1,0:T(8,128)(2,1)} %bitcast.10), channel_id=1, source_target_pairs={{0,1},{1,0},{2,3},{3,2},{4,5},{5,4},{6,7},{7,6},{8,9},{9,8},{10,11... | collective-permute-start | bytes 9437192 | tf_op jit(solution)/shard_map/ppermute | solution.py:19
  16.4 1.9 %copy-start.6 = (bf16[16,6272]{1,0:T(8,128)(2,1)}, bf16[16,6272]{1,0:T(8,128)(2,1)S(1)}, u32[]{:S(2)}) copy-start(bf16[16,6272]{1,0:T(8,128)(2,1)S(1)} %constant_dynamic-update-slice_fusion.here) | copy-start | bytes 602116
  16.4 5.8 %collective-permute-start.10 = (bf16[16,6272]{1,0:T(8,128)(2,1)S(1)}, bf16[16,6272]{1,0:T(8,128)(2,1)S(1)}, u32[]{:S(2)}, u32[]{:S(2)}) collective-permute-start(bf16[16,6272]{1,0:T(8,128)(2,1)S(1)} %constant_dynamic-update-slice_fusion.here), channel_id=1, source_target_pairs={{0,2},{1,5},{2,0},{3,7},{4,6},{5,1},{6,4},{7,3},{8,10},{9,13},{10,... | collective-permute-start | bytes 602120 | tf_op jit(solution)/shard_map/ppermute | solution.py:19
  18.3 6.6 %collective-permute-start.1 = (bf16[16,6272]{1,0:T(8,128)(2,1)S(1)}, bf16[16,6272]{1,0:T(8,128)(2,1)S(1)}, u32[]{:S(2)}, u32[]{:S(2)}) collective-permute-start(bf16[16,6272]{1,0:T(8,128)(2,1)S(1)} %pad_maximum_fusion.2.here), channel_id=1, source_target_pairs={{0,2},{1,5},{2,0},{3,7},{4,6},{5,1},{6,4},{7,3},{8,10},{9,13},{10,... | collective-permute-start | bytes 602120 | tf_op jit(solution)/shard_map/ppermute | solution.py:19
  22.2 2.6 %copy-start.4 = (bf16[16,6272]{1,0:T(8,128)(2,1)}, bf16[16,6272]{1,0:T(8,128)(2,1)S(1)}, u32[]{:S(2)}) copy-start(bf16[16,6272]{1,0:T(8,128)(2,1)S(1)} %collective-permute-done.10.first) | copy-start | bytes 602116
  23.0 8.2 %collective-permute-start.11 = (bf16[32,6272]{1,0:T(8,128)(2,1)}, bf16[32,6272]{1,0:T(8,128)(2,1)}, u32[]{:S(2)}, u32[]{:S(2)}) collective-permute-start(bf16[32,6272]{1,0:T(8,128)(2,1)} %pad_maximum_fusion.1), channel_id=1, source_target_pairs={{0,4},{1,3},{2,6},{3,1},{4,0},{5,7},{6,2},{7,5},{8,12},{9,11},{10,... | collective-permute-start | bytes 1204232 | tf_op jit(solution)/shard_map/ppermute | solution.py:19
  26.5 20.8 %collective-permute-start.2 = (bf16[32,6272]{1,0:T(8,128)(2,1)}, bf16[32,6272]{1,0:T(8,128)(2,1)}, u32[]{:S(2)}, u32[]{:S(2)}) collective-permute-start(bf16[32,6272]{1,0:T(8,128)(2,1)} %pad_maximum_fusion), channel_id=1, source_target_pairs={{0,4},{1,3},{2,6},{3,1},{4,0},{5,7},{6,2},{7,5},{8,12},{9,11},{10,... | collective-permute-start | bytes 1204232 | tf_op jit(solution)/shard_map/ppermute | solution.py:19
  31.2 1.9 %copy-start = (bf16[1,4096,384]{2,1,0:T(8,128)(2,1)S(1)}, bf16[1,4096,384]{2,1,0:T(8,128)(2,1)}, u32[]{:S(2)}) copy-start(bf16[1,4096,384]{2,1,0:T(8,128)(2,1)} %param.9) | copy-start | bytes 9437188
  33.1 1.9 %copy-start.2 = (bf16[1,4096,384]{2,1,0:T(8,128)(2,1)S(1)}, bf16[1,4096,384]{2,1,0:T(8,128)(2,1)}, u32[]{:S(2)}) copy-start(bf16[1,4096,384]{2,1,0:T(8,128)(2,1)} %param.10) | copy-start | bytes 9437188
  35.0 1.9 %copy-start.3 = (bf16[1,384,4096]{2,1,0:T(8,128)(2,1)S(1)}, bf16[1,384,4096]{2,1,0:T(8,128)(2,1)}, u32[]{:S(2)}) copy-start(bf16[1,384,4096]{2,1,0:T(8,128)(2,1)} %param.11) | copy-start | bytes 9437188
  36.9 0.9 %copy-start.5 = (bf16[16,6272]{1,0:T(8,128)(2,1)S(1)}, bf16[16,6272]{1,0:T(8,128)(2,1)}, u32[]{:S(2)}) copy-start(bf16[16,6272]{1,0:T(8,128)(2,1)} %copy-done.4) | copy-start | bytes 602116
  37.8 0.9 %copy-start.7 = (bf16[16,6272]{1,0:T(8,128)(2,1)S(1)}, bf16[16,6272]{1,0:T(8,128)(2,1)}, u32[]{:S(2)}) copy-start(bf16[16,6272]{1,0:T(8,128)(2,1)} %copy-done.6) | copy-start | bytes 602116
  38.8 8.5 %copy-start.1 = (bf16[1,4096,384]{2,1,0:T(8,128)(2,1)S(1)}, bf16[1,4096,384]{2,1,0:T(8,128)(2,1)}, u32[]{:S(2)}) copy-start(bf16[1,4096,384]{2,1,0:T(8,128)(2,1)} %param.9) | copy-start | bytes 9437188
  45.4 8.7 %collective-permute-start.12 = (bf16[32,6144]{1,0:T(8,128)(2,1)S(1)}, bf16[32,6144]{1,0:T(8,128)(2,1)S(1)}, u32[]{:S(2)}, u32[]{:S(2)}) collective-permute-start(bf16[32,6144]{1,0:T(8,128)(2,1)S(1)} %get-tuple-element.12), channel_id=1, source_target_pairs={{0,4},{1,3},{2,6},{3,1},{4,0},{5,7},{6,2},{7,5},{8,12},{9,11},{10,... | collective-permute-start | bytes 1179656 | tf_op jit(solution)/shard_map/ppermute | solution.py:19
  53.8 7.8 %collective-permute-start.6 = (bf16[32,6144]{1,0:T(8,128)(2,1)S(1)}, bf16[32,6144]{1,0:T(8,128)(2,1)S(1)}, u32[]{:S(2)}, u32[]{:S(2)}) collective-permute-start(bf16[32,6144]{1,0:T(8,128)(2,1)S(1)} %get-tuple-element.10), channel_id=1, source_target_pairs={{0,4},{1,3},{2,6},{3,1},{4,0},{5,7},{6,2},{7,5},{8,12},{9,11},{10,... | collective-permute-start | bytes 1179656 | tf_op jit(solution)/shard_map/ppermute | solution.py:19
  54.3 9.5 %collective-permute-start.13 = (bf16[16,6144]{1,0:T(8,128)(2,1)S(1)}, bf16[16,6144]{1,0:T(8,128)(2,1)S(1)}, u32[]{:S(2)}, u32[]{:S(2)}) collective-permute-start(bf16[16,6144]{1,0:T(8,128)(2,1)S(1)} %slice.77), channel_id=1, source_target_pairs={{0,2},{1,5},{2,0},{3,7},{4,6},{5,1},{6,4},{7,3},{8,10},{9,13},{10,... | collective-permute-start | bytes 589832 | tf_op jit(solution)/shard_map/ppermute | solution.py:19
  61.8 6.4 %collective-permute-start.7 = (bf16[16,6144]{1,0:T(8,128)(2,1)S(1)}, bf16[16,6144]{1,0:T(8,128)(2,1)S(1)}, u32[]{:S(2)}, u32[]{:S(2)}) collective-permute-start(bf16[16,6144]{1,0:T(8,128)(2,1)S(1)} %slice.74), channel_id=1, source_target_pairs={{0,2},{1,5},{2,0},{3,7},{4,6},{5,1},{6,4},{7,3},{8,10},{9,13},{10,... | collective-permute-start | bytes 589832 | tf_op jit(solution)/shard_map/ppermute | solution.py:19
  63.8 7.0 %collective-permute-start.14 = (bf16[8,6144]{1,0:T(8,128)(2,1)S(1)}, bf16[8,6144]{1,0:T(8,128)(2,1)S(1)}, u32[]{:S(2)}, u32[]{:S(2)}) collective-permute-start(bf16[8,6144]{1,0:T(8,128)(2,1)S(1)} %get-tuple-element.13), channel_id=1, source_target_pairs={{0,24},{1,25},{2,26},{3,27},{4,28},{5,29},{6,30},{7,31},{8,16},{9,... | collective-permute-start | bytes 294920 | tf_op jit(solution)/shard_map/ppermute | solution.py:19
  66.7 7.3 %collective-permute-start.15 = (bf16[8,6144]{1,0:T(8,128)(2,1)S(1)}, bf16[8,6144]{1,0:T(8,128)(2,1)S(1)}, u32[]{:S(2)}, u32[]{:S(2)}) collective-permute-start(bf16[8,6144]{1,0:T(8,128)(2,1)S(1)} %get-tuple-element.14), channel_id=1, source_target_pairs={{0,16},{1,17},{2,18},{3,19},{4,20},{5,21},{6,22},{7,23},{8,24},{9,... | collective-permute-start | bytes 294920 | tf_op jit(solution)/shard_map/ppermute | solution.py:19
  68.3 5.7 %collective-permute-start.16 = (bf16[8,6144]{1,0:T(8,128)(2,1)S(1)}, bf16[8,6144]{1,0:T(8,128)(2,1)S(1)}, u32[]{:S(2)}, u32[]{:S(2)}) collective-permute-start(bf16[8,6144]{1,0:T(8,128)(2,1)S(1)} %slice.80), channel_id=1, source_target_pairs={{0,8},{1,9},{2,10},{3,11},{4,12},{5,13},{6,14},{7,15},{8,0},{9,1},... | collective-permute-start | bytes 294920 | tf_op jit(solution)/shard_map/ppermute | solution.py:19

commit v3 on v0

v3 whole, which is shorter than its diff:
```python
import functools

import jax
import jax.numpy as jnp
from jax import lax
from jax.experimental import pallas as pl
from jax.experimental.pallas import tpu as pltpu
from jax.sharding import PartitionSpec as P

BF16 = jnp.bfloat16
F32 = jnp.float32
TILE = 8
HALF_TILE = 4
LANES = 128
STEP = 512
PIECES = 4
COST = 4 << 20
VMEM = pl.BlockSpec(memory_space=pltpu.VMEM)
SMEM = pl.BlockSpec(memory_space=pltpu.SMEM)
HBM = pl.BlockSpec(memory_space=pltpu.HBM)


def call(kernel, out_shape, in_specs, args, scratch=(), limit=8, flops=0, moved=0):
    args = [
        pltpu.with_memory_space_constraint(arg, pltpu.HBM) if spec is HBM else arg
        for arg, spec in zip(args, in_specs)
    ]
    single = not isinstance(out_shape, tuple)
    return pl.pallas_call(
        kernel,
        out_shape=out_shape,
        in_specs=in_specs,
        out_specs=VMEM if single else (VMEM,) * len(out_shape),
        scratch_shapes=scratch,
        compiler_params=pltpu.CompilerParams(vmem_limit_bytes=limit << 20),
        cost_estimate=pl.CostEstimate(flops=flops, bytes_accessed=moved, transcendentals=0),
    )(*args)


def upper_rows(shape):
    return lax.broadcasted_iota(jnp.int32, shape, 0) < HALF_TILE


def swap(tile):
    return pltpu.roll(tile, HALF_TILE, 0)


def fold_kernel(experts, *refs):
    sources, out, (ids, gate, hidden, turned, sems) = refs[:3], refs[3], refs[4:]
    copies = [
        pltpu.make_async_copy(source, target, sems.at[i])
        for i, (source, target) in enumerate(zip(sources, (ids, gate, hidden)))
    ]
    for copy in copies:
        copy.start()
    copies[0].wait()
    copies[1].wait()
    rows, width = hidden.shape
    half = width // 2
    top = ids.shape[0]
    lanes = turned.shape[0]
    raw = gate[...]
    weight = raw / jnp.sum(raw, axis=0, keepdims=True)
    expert = lax.broadcasted_iota(jnp.int32, (lanes, rows), 0) % experts
    dense = jnp.zeros((lanes, rows), F32)
    for t in range(top):
        dense = jnp.where(ids[t : t + 1, :] == expert, weight[t : t + 1, :], dense)
    turned[:, :rows] = dense
    dense = turned[...].T
    high = dense.astype(BF16).astype(F32)
    first, last = high[:TILE], high[TILE : 2 * TILE]
    low_first, low_last = dense[:TILE] - first, dense[TILE : 2 * TILE] - last
    upper = upper_rows((TILE, lanes))
    last = jnp.where(upper, last, swap(last))
    low_last = jnp.where(upper, low_last, swap(low_last))
    role = lax.broadcasted_iota(jnp.int32, (TILE, lanes), 1) // experts
    side = jnp.where(
        role == 0,
        first,
        jnp.where(role == 1, low_first, jnp.where(role == 2, last, jnp.where(role == 3, low_last, 0.0))),
    )
    out[:, width + half :] = side.astype(BF16)
    copies[2].wait()
    out[:, :width] = hidden[:TILE, :]
    rest = hidden[TILE:, :].astype(F32)
    out[:, width : width + half] = jnp.concatenate([rest[:, :half], rest[:, half:]], axis=0).astype(BF16)


def fold_rows(hidden, expert_ids, gate_raw, experts):
    rows, width = hidden.shape
    lanes = -(-4 * experts // LANES) * LANES
    out = jax.ShapeDtypeStruct((TILE, width + width // 2 + lanes), BF16)
    return call(
        functools.partial(fold_kernel, experts),
        out,
        [HBM] * 3,
        (expert_ids.T, gate_raw.T, hidden),
        [
            pltpu.VMEM(expert_ids.T.shape, expert_ids.dtype),
            pltpu.VMEM(gate_raw.T.shape, F32),
            pltpu.VMEM(hidden.shape, BF16),
            pltpu.VMEM((lanes, LANES), F32),
            pltpu.SemaphoreType.DMA((3,)),
        ],
    )


def pair_kernel(experts, width, *refs):
    parts, out = refs[:-1], refs[-1]
    half = width // 2

    def tiles(start, size):
        values = [part[:, start : start + size].astype(F32) for part in parts]
        return [value[at : at + TILE] for value in values for at in range(0, value.shape[0], TILE)]

    lanes = out.shape[1] - width

    def put(at, size, firsts, lasts):
        rows = [row for a, b, last in zip(firsts[::2], firsts[1::2], lasts) for row in (a, b, last)]
        out[:, at : at + size] = jnp.concatenate(rows, axis=0).astype(BF16)

    upper = upper_rows((TILE, STEP))
    for start in range(0, half, STEP):
        rest = tiles(width + start, STEP)
        for at, turn in ((start, False), (half + start, True)):
            lasts = [
                jnp.where(upper, swap(a) if turn else a, b if turn else swap(b))
                for a, b in zip(rest[::2], rest[1::2])
            ]
            put(at, STEP, tiles(at, STEP), lasts)
    side = tiles(width + half, lanes)
    first = lax.broadcasted_iota(jnp.int32, (TILE, lanes), 1) < 2 * experts
    upper = upper_rows((TILE, lanes))
    put(
        width,
        lanes,
        [jnp.where(first, value, 0.0) for value in side],
        [jnp.where(first, 0.0, jnp.where(upper, a, b)) for a, b in zip(side[::2], side[1::2])],
    )


def pair_rows(parts, width, experts):
    lanes = parts[0].shape[1] - width - width // 2
    rows = sum(part.shape[0] for part in parts)
    out = jax.ShapeDtypeStruct((rows + rows // 2, width + lanes), BF16)
    return call(functools.partial(pair_kernel, experts, width), out, [VMEM] * len(parts), parts)


def split_kernel(order, *refs):
    parts, outs = refs[: -len(order)], refs[-len(order) :]
    rows, width = parts[0].shape
    half = width // 2
    upper = upper_rows((TILE, STEP))

    def tiles(at):
        total = sum(part[:, at : at + STEP].astype(F32)[:rows] for part in parts)
        return [total[row : row + TILE] for row in range(0, rows, TILE)]

    def put(at, values):
        for out, blocks in zip(outs, order):
            value = jnp.concatenate([values[block] for block in blocks], axis=0)
            out[:, at : at + STEP] = value.astype(BF16)

    for start in range(0, half, STEP):
        low, high = tiles(start), tiles(half + start)
        rest = []
        for a, b in zip(low[2::3], high[2::3]):
            rest += [jnp.where(upper, a, swap(b)), jnp.where(upper, swap(a), b)]
        put(start, [tile for i, tile in enumerate(low) if i % 3 < 2])
        put(half + start, [tile for i, tile in enumerate(high) if i % 3 < 2])
        put(width + start, rest)


def split_rows(parts, order, cost=0):
    width = parts[0].shape[1]
    shapes = tuple(jax.ShapeDtypeStruct((TILE * len(blocks), width + width // 2), BF16) for blocks in order)
    return call(functools.partial(split_kernel, order), shapes, [VMEM] * len(parts), parts, moved=cost)


def last_kernel(*refs):
    parts, out = refs[:-1], refs[-1]
    rows, width = out.shape
    half = width // 2
    for start in range(0, half, STEP):
        low, high, rest = (
            sum(part[:, at : at + STEP].astype(F32)[:TILE] for part in parts)
            for at in (start, half + start, width + start)
        )
        out[:, start : start + STEP] = jnp.concatenate([low, rest[:HALF_TILE]], axis=0).astype(BF16)
        out[:, half + start : half + start + STEP] = jnp.concatenate(
            [high, rest[HALF_TILE:]], axis=0
        ).astype(BF16)


def last_rows(parts, rows, width):
    return call(last_kernel, jax.ShapeDtypeStruct((rows, width), BF16), [VMEM] * len(parts), parts)


def fetch_kernel(*refs):
    count = len(refs) // 2
    sources, targets, sems = refs[:count], refs[count:-1], refs[-1]
    copies = []
    for i, (source, target) in enumerate(zip(sources, targets)):
        rows = source.shape[0] // PIECES
        for j in range(PIECES):
            at = pl.ds(j * rows, rows)
            copies.append(pltpu.make_async_copy(source.at[at], target.at[at], sems.at[i, j]))
    for copy in copies:
        copy.start()
    for copy in copies:
        copy.wait()


def fetch(arrays):
    return call(
        fetch_kernel,
        tuple(pltpu.VMEM(w.shape, w.dtype) for w in arrays),
        [HBM] * len(arrays),
        arrays,
        [pltpu.SemaphoreType.DMA((len(arrays), PIECES))],
    )


def expert_kernel(experts, count, mine, *refs):
    parts, own, others, source = refs[:count], refs[count : count + 3], refs[count + 3 : count + 5], refs[count + 5]
    outs, (xs, inner, last, sem) = refs[count + 6 : -4], refs[-4:]
    others += (last,)
    copy = pltpu.make_async_copy(source, last, sem)
    copy.start()
    width = outs[0].shape[1]
    units = own[0].shape[1]

    for start in range(0, width, STEP):
        xs[:, start : start + STEP] = jnp.concatenate(
            [part[:, start : start + STEP].astype(F32) for part in parts], axis=0
        ).astype(BF16)
    side = jnp.concatenate([part[:, width:].astype(F32) for part in parts], axis=0)
    lane = lax.broadcasted_iota(jnp.int32, side.shape, 1)
    scale = jnp.sum(jnp.where(lane % experts == mine[0], side, 0.0), axis=1, keepdims=True)

    for at, (gate, up, unused) in enumerate((own, others)):
        for tile in range(0, units, LANES):
            piece = slice(tile, tile + LANES)
            total = jnp.dot(
                xs[...],
                jnp.concatenate([gate[:, piece], up[:, piece]], axis=1),
                preferred_element_type=F32,
            )
            value = jax.nn.silu(total[:, :LANES]) * total[:, LANES:] * scale
            inner[:, at * units + tile : at * units + tile + LANES] = value.astype(BF16)

    copy.wait()
    for start in range(0, width, STEP):
        mat = jnp.concatenate([own[2][:, start : start + STEP], others[2][:, start : start + STEP]], axis=0)
        value = jnp.dot(inner[...], mat, preferred_element_type=F32)
        at = 0
        for out in outs:
            out[:, start : start + STEP] = value[at : at + out.shape[0]].astype(BF16)
            at += out.shape[0]


def expert_rows(parts, outs, width, mine, experts, weights):
    rows = sum(part.shape[0] for part in parts)
    units = weights[0].shape[1]
    *weights, last = weights
    weights = [pltpu.with_memory_space_constraint(w, pltpu.VMEM) for w in weights]
    return call(
        functools.partial(expert_kernel, experts, len(parts)),
        tuple(jax.ShapeDtypeStruct((n, width), BF16) for n in outs),
        [SMEM] + [VMEM] * (len(parts) + len(weights)) + [HBM],
        (mine, *parts, *weights, last),
        [
            pltpu.VMEM((rows, width), BF16),
            pltpu.VMEM((rows, 2 * units), BF16),
            pltpu.VMEM(last.shape, BF16),
            pltpu.SemaphoreType.DMA,
        ],
        limit=16,
        flops=6 * rows * width * 2 * units,
    )


def permute(value, devices, flip_of):
    pairs = [(device, device ^ flip_of(device)) for device in range(devices)]
    return lax.ppermute(value, "expert", pairs)


def level_flip(step, device):
    return 8 * (step + device % 2)


def first_flip(device):
    return 2 if device % 2 == 0 else 4


def second_flip(device):
    return 4 if device % 2 == 0 else 2


def join_kernel(a, b, out):
    for start in range(0, out.shape[1], LANES):
        at = pl.ds(start, LANES)
        out[:, at] = jnp.concatenate([a[:, at].astype(F32), b[:, at].astype(F32)], axis=0).astype(BF16)


def join(a, b):
    out = jax.ShapeDtypeStruct((2 * a.shape[0], a.shape[1]), BF16)
    return call(join_kernel, out, [VMEM] * 2, (a, b))


def add_kernel(a, b, out):
    rows, width = out.shape
    for start in range(0, width, STEP):
        at = pl.ds(start, STEP)
        out[:, at] = (a[:, at].astype(F32) + b[:, at].astype(F32)[-rows:]).astype(BF16)


def add(a, b, cost=0):
    return call(add_kernel, jax.ShapeDtypeStruct(a.shape, BF16), [VMEM] * 2, (a, b), moved=cost)


def per_device(hidden, expert_ids, gate_raw, w_gate, w_up, w_down):
    devices = lax.axis_size("expert")
    experts = devices // 2
    levels = devices // 8
    rows, width = hidden.shape
    mine = (lax.axis_index("expert") // 2).reshape(1)
    go = lambda value, flip: permute(value, devices, flip)

    own = fold_rows(hidden, expert_ids, gate_raw, experts)

    weights = [w_gate[0], w_up[0], w_down[0]]

    both = pair_rows((own, go(own, lambda device: 1)), width, experts)
    weights, both = lax.optimization_barrier((weights, both))
    others = [go(w, lambda device: 1) for w in weights]
    far = [go(both, lambda device, s=step: level_flip(s, device)) for step in range(2, levels, 2)]
    far = far[0] if len(far) == 1 else jnp.concatenate(far, axis=0)
    own_first = go(own, first_flip)
    own_second = go(join(own, own_first), second_flip)
    far, own_second = lax.optimization_barrier((far, own_second))
    far_first = go(far, first_flip)
    far_second = go(far, second_flip)
    near = pair_rows((own, own_first, own_second), width, experts)
    near_other = go(near, lambda device: 8)
    weights, far_first = lax.optimization_barrier((weights, far_first))
    far_third = go(far_first, second_flip)
    weights = list(fetch(weights + others[:2])) + others[2:]

    many, more = far.shape[0], near.shape[0]
    near, near_other, far, far_first, far_second, far_third = expert_rows(
        (near, near_other, far, far_first, far_second, far_third),
        (more, more, many, many, many, many),
        width,
        mine,
        experts,
        weights,
    )

    far_third = go(far_third, second_flip)
    far_second = go(far_second, second_flip)
    near_other = go(near_other, lambda device: 8)
    far_first = go(add(far_first, far_third, COST), first_flip)
    far = split_rows((far, far_second, far_first), [(block,) for block in range(levels - 2)], COST)
    far = [
        go(block, lambda device, s=step, twin=twin: level_flip(s, device) + twin)
        for block, (step, twin) in zip(far, [(s, t) for s in range(2, levels, 2) for t in range(2)])
    ]
    own, own_first, own_second = split_rows((near, near_other), ((0,), (1,), (2, 3)))
    own_second = go(own_second, second_flip)
    own_first = go(add(own_first, own_second), first_flip)
    return last_rows([own, own_first, own_second] + far, rows, width)


def solution(mesh):
    placed = (
        P(("groups", "expert"), None),
        P(("groups", "expert"), None),
        P(("groups", "expert"), None),
        P("expert", None, None),
        P("expert", None, None),
        P("expert", None, None),
    )
    return jax.shard_map(
        per_device,
        mesh=mesh,
        in_specs=placed,
        out_specs=P(("groups", "expert"), None),
        check_vma=False,
    )
```

time: 212 us -> 64.3 us (0.30)
  waiting for transfers between devices: 115 us -> 30.5 us
  blocking collectives: 44.1 us -> 0 us
  matrix products: 22.7 us -> 0 us
  starting transfers between devices: 3.7 us -> 19.4 us
  Pallas kernels: 0 us -> 13.6 us
  between operations: 13.5 us -> 0.09 us
  local copies, waits for them, and re-layouts: 10.3 us -> 0 us
    all_to_all x1 -> x0, waiting for transfers between devices: 93 us -> none  [expert_return(): lax.all_to_all(partial_value, 'expert', split_axis=0, concat_axis=0, tile...]
    all_gather x1 -> x0, blocking collectives: 44.1 us -> none  [per_device(): lax.all_gather(expert_ids, 'expert', axis=0, tiled=True)]
    ppermute x0 -> x19, waiting for transfers between devices: none -> 30.5 us  [permute(): return lax.ppermute(value, 'expert', pairs)]
    dot_general x5 -> x0, matrix products: 22.7 us -> none  [the longest x1 6.81 us: expert_return(): jnp.dot(inner, w_down[0], preferred_element_type=jnp.float32)]
    all_gather x1 -> x0, waiting for transfers between devices: 21.6 us -> none  [per_device(): lax.all_gather(hidden, 'expert', axis=0, tiled=True)]
    ppermute x0 -> x19, starting transfers between devices: none -> 19.4 us  [permute(): return lax.ppermute(value, 'expert', pairs)]
    pallas_call x0 -> x11, Pallas kernels: none -> 13.6 us  [call(): pl.pallas_call(kernel, out_shape=out_shape, in_specs=in_specs, out_specs=...]
    reshape x2 -> x0, local copies, waits for them, and re-layouts: 9.32 us -> none  [the longest x1 4.69 us: expert_return(): flat = buffer.reshape(count * slots, width)]
  transfers between devices with their start and end apart: 2 -> 19, of which waited for: 2 -> 9; matrix products, arithmetic and copies ran while one was open for 1% -> 0% of each run, Pallas kernels for 0% -> 10%
where the time goes in v3:
time: 64.3 us; the launch traced here: 63.7 us
  waiting for transfers between devices  30.5 us (47%)
  starting transfers between devices  19.4 us (30%)
  Pallas kernels  13.6 us (21%)
    ppermute x19, waiting for transfers between devices, permute(): return lax.ppermute(value, 'expert', pairs)  30.5 us
    ppermute x19, starting transfers between devices, permute(): return lax.ppermute(value, 'expert', pairs)  19.4 us
    pallas_call x11, Pallas kernels, call(): pl.pallas_call(kernel, out_shape=out_shape, in_specs=in_specs, out_specs=...  13.6 us
  transfers between devices with their start and end apart: 19, of which 9 were waited for; matrix products, arithmetic and copies ran while one was open for 0% of the time, Pallas kernels for 10%

profile of v3, /device:TPU:0, one launch (start us, length us, event | category | flops | bytes accessed | tf_op | source)
XLA Modules:
  0.0 63.7 jit_solution(16058523950909820693)
XLA Ops:
  0.0 1.0 %shard_map.64.refs_0_.a = bf16[8,6272]{1,0:T(8,128)(2,1)S(1)} custom-call(s32[8,12]{1,0:T(8,128)} %bitcast.12, f32[8,12]{1,0:T(8,128)} %bitcast.13, bf16[12,4096]{1,0:T(8,128)(2,1)} %refs_2_.1), custom_call_target="tpu_custom_call" | custom-call | tf_op jit(solution)/shard_map/pallas_call | solution.py:29
  1.0 0.5 collective-permute-start.1
  1.5 0.9 %collective-permute-done.1.refs_1_ = bf16[8,6272]{1,0:T(8,128)(2,1)S(1)} collective-permute-done((bf16[8,6272]{1,0:T(8,128)(2,1)S(1)}, bf16[8,6272]{1,0:T(8,128)(2,1)S(1)}, u32[]{:S(2)}, u32[]{:S(2)}) %collective-permute-start.1) | collective-permute-done | bytes 100384 | tf_op jit(solution)/shard_map/ppermute | solution.py:285
  2.5 0.4 collective-permute-start.8
  2.9 0.2 collective-permute-start.9
  3.1 0.4 collective-permute-start.10
  3.4 2.6 %collective-permute-start = (bf16[8,6272]{1,0:T(8,128)(2,1)S(1)}, bf16[8,6272]{1,0:T(8,128)(2,1)S(1)}, u32[]{:S(2)}, u32[]{:S(2)}) collective-permute-start(bf16[8,6272]{1,0:T(8,128)(2,1)S(1)} %shard_map.64.refs_0_.a), channel_id=1, source_target_pairs={{0,2},{1,5},{2,0},{3,7},{4,6},{5,1},{6,4},{7,3},{8,10},{9,13},{10,... | collective-permute-start | bytes 301064 | tf_op jit(solution)/shard_map/ppermute | solution.py:285
  6.0 2.6 %collective-permute-start.2 = (bf16[24,4224]{1,0:T(8,128)(2,1)S(1)}, bf16[24,4224]{1,0:T(8,128)(2,1)S(1)}, u32[]{:S(2)}, u32[]{:S(2)}) collective-permute-start(bf16[24,4224]{1,0:T(8,128)(2,1)S(1)} %shard_map.65), channel_id=1, source_target_pairs={{0,16},{1,25},{2,18},{3,27},{4,20},{5,29},{6,22},{7,31},{8,24},{9,... | collective-permute-start | bytes 608264 | tf_op jit(solution)/shard_map/ppermute | solution.py:285
  8.7 2.1 %collective-permute-start.3 = (bf16[16,6272]{1,0:T(8,128)(2,1)S(1)}, bf16[16,6272]{1,0:T(8,128)(2,1)S(1)}, u32[]{:S(2)}, u32[]{:S(2)}) collective-permute-start(bf16[16,6272]{1,0:T(8,128)(2,1)S(1)} %shard_map.66), channel_id=1, source_target_pairs={{0,4},{1,3},{2,6},{3,1},{4,0},{5,7},{6,2},{7,5},{8,12},{9,11},{10,... | collective-permute-start | bytes 602120 | tf_op jit(solution)/shard_map/ppermute | solution.py:285
  10.8 3.7 %collective-permute-done.3.refs_2_ = bf16[16,6272]{1,0:T(8,128)(2,1)S(1)} collective-permute-done((bf16[16,6272]{1,0:T(8,128)(2,1)S(1)}, bf16[16,6272]{1,0:T(8,128)(2,1)S(1)}, u32[]{:S(2)}, u32[]{:S(2)}) %collective-permute-start.3) | collective-permute-done | bytes 200736 | tf_op jit(solution)/shard_map/ppermute | solution.py:285
  14.5 3.9 %collective-permute-done.2.refs_2_ = bf16[24,4224]{1,0:T(8,128)(2,1)S(1)} collective-permute-done((bf16[24,4224]{1,0:T(8,128)(2,1)S(1)}, bf16[24,4224]{1,0:T(8,128)(2,1)S(1)}, u32[]{:S(2)}, u32[]{:S(2)}) %collective-permute-start.2) | collective-permute-done | bytes 202784 | tf_op jit(solution)/shard_map/ppermute | solution.py:285
  18.5 0.5 collective-permute-start.5
  19.0 0.7 %collective-permute-start.4 = (bf16[48,4224]{1,0:T(8,128)(2,1)S(1)}, bf16[48,4224]{1,0:T(8,128)(2,1)S(1)}, u32[]{:S(2)}, u32[]{:S(2)}) collective-permute-start(bf16[48,4224]{1,0:T(8,128)(2,1)S(1)} %shard_map.67.refs_0_), channel_id=1, source_target_pairs={{0,8},{1,9},{2,10},{3,11},{4,12},{5,13},{6,14},{7,15},{8,0},{9,1},... | collective-permute-start | bytes 1216520 | tf_op jit(solution)/shard_map/ppermute | solution.py:285
  19.7 6.6 %collective-permute-done.5.refs_3_ = bf16[24,4224]{1,0:T(8,128)(2,1)S(1)} collective-permute-done((bf16[24,4224]{1,0:T(8,128)(2,1)S(1)}, bf16[24,4224]{1,0:T(8,128)(2,1)S(1)}, u32[]{:S(2)}, u32[]{:S(2)}) %collective-permute-start.5) | collective-permute-done | bytes 202784 | tf_op jit(solution)/shard_map/ppermute | solution.py:285
  26.4 0.5 collective-permute-start.6
  26.9 1.5 %collective-permute-start.7 = (bf16[24,4224]{1,0:T(8,128)(2,1)S(1)}, bf16[24,4224]{1,0:T(8,128)(2,1)S(1)}, u32[]{:S(2)}, u32[]{:S(2)}) collective-permute-start(bf16[24,4224]{1,0:T(8,128)(2,1)S(1)} %collective-permute-done.5.refs_3_), channel_id=1, source_target_pairs={{0,4},{1,3},{2,6},{3,1},{4,0},{5,7},{6,2},{7,5},{8,12},{9,11},{10,... | collective-permute-start | bytes 608264 | tf_op jit(solution)/shard_map/ppermute | solution.py:285
  28.4 5.7 %shard_map.68 = (bf16[4096,384]{1,0:T(8,128)(2,1)S(1)}, bf16[4096,384]{1,0:T(8,128)(2,1)S(1)}, bf16[384,4096]{1,0:T(8,128)(2,1)S(1)}, bf16[4096,384]{1,0:T(8,128)(2,1)S(1)}, bf16[4096,384]{1,0:T(8,128)(2,1)S(1)}) custom-call(bf16[4096,384]{1,0:T(8,128)(2,1)} %bitcast.7, bf16[4096,384]{1,0:T(8,128)(2,1)} %bitcast.9, bf16[384,4096]{1,0:T(8,128)(2,1)} %bitcast.11, ...), custom_call_target="tpu_custom_call" | custom-call | tf_op jit(solution)/shard_map/pallas_call | solution.py:29
  34.1 0.1 collective-permute-done.7.refs_5_
  34.3 5.8 %shard_map.69 = (bf16[48,4096]{1,0:T(8,128)(2,1)S(1)}, bf16[48,4096]{1,0:T(8,128)(2,1)S(1)}, bf16[24,4096]{1,0:T(8,128)(2,1)S(1)}, bf16[24,4096]{1,0:T(8,128)(2,...) custom-call(s32[1]{0:T(128)} %bitcast.mine, bf16[48,4224]{1,0:T(8,128)(2,1)S(1)} %shard_map.67.refs_0_, ...), custom_call_target="tpu_custom_call" | custom-call | flops 3623878656 | tf_op jit(solution)/shard_map/pallas_call | solution.py:29
  40.1 0.1 collective-permute-start.11
  40.2 0.6 collective-permute-start.15
  40.7 1.5 %collective-permute-start.14 = (bf16[24,4096]{1,0:T(8,128)(2,1)S(1)}, bf16[24,4096]{1,0:T(8,128)(2,1)S(1)}, u32[]{:S(2)}, u32[]{:S(2)}) collective-permute-start(bf16[24,4096]{1,0:T(8,128)(2,1)S(1)} %get-tuple-element.52), channel_id=1, source_target_pairs={{0,4},{1,3},{2,6},{3,1},{4,0},{5,7},{6,2},{7,5},{8,12},{9,11},{10,... | collective-permute-start | bytes 589832 | tf_op jit(solution)/shard_map/ppermute | solution.py:285
  42.3 5.0 %collective-permute-done.15.b = bf16[24,4096]{1,0:T(8,128)(2,1)S(1)} collective-permute-done((bf16[24,4096]{1,0:T(8,128)(2,1)S(1)}, bf16[24,4096]{1,0:T(8,128)(2,1)S(1)}, u32[]{:S(2)}, u32[]{:S(2)}) %collective-permute-start.15) | collective-permute-done | bytes 196640 | tf_op jit(solution)/shard_map/ppermute | solution.py:285
  47.4 0.5 collective-permute-done.11.refs_1_
  47.9 0.1 shard_map.70
  48.1 2.0 %collective-permute-start.12 = (bf16[16,6144]{1,0:T(8,128)(2,1)S(1)}, bf16[16,6144]{1,0:T(8,128)(2,1)S(1)}, u32[]{:S(2)}, u32[]{:S(2)}) collective-permute-start(bf16[16,6144]{1,0:T(8,128)(2,1)S(1)} %get-tuple-element.50), channel_id=1, source_target_pairs={{0,4},{1,3},{2,6},{3,1},{4,0},{5,7},{6,2},{7,5},{8,12},{9,11},{10,... | collective-permute-start | bytes 589832 | tf_op jit(solution)/shard_map/ppermute | solution.py:285
  50.1 3.0 %collective-permute-done.16.refs_2_ = bf16[24,4096]{1,0:T(8,128)(2,1)S(1)} collective-permute-done((bf16[24,4096]{1,0:T(8,128)(2,1)S(1)}, bf16[24,4096]{1,0:T(8,128)(2,1)S(1)}, u32[]{:S(2)}, u32[]{:S(2)}) %collective-permute-start.16) | collective-permute-done | bytes 196640 | tf_op jit(solution)/shard_map/ppermute | solution.py:285
  53.1 0.1 shard_map.73
  53.2 1.2 %collective-permute-start.17 = (bf16[8,6144]{1,0:T(8,128)(2,1)S(1)}, bf16[8,6144]{1,0:T(8,128)(2,1)S(1)}, u32[]{:S(2)}, u32[]{:S(2)}) collective-permute-start(bf16[8,6144]{1,0:T(8,128)(2,1)S(1)} %get-tuple-element.55), channel_id=1, source_target_pairs={{0,16},{1,25},{2,18},{3,27},{4,20},{5,29},{6,22},{7,31},{8,24},{9,... | collective-permute-start | bytes 294920 | tf_op jit(solution)/shard_map/ppermute | solution.py:285
  54.4 2.0 %collective-permute-start.13 = (bf16[8,6144]{1,0:T(8,128)(2,1)S(1)}, bf16[8,6144]{1,0:T(8,128)(2,1)S(1)}, u32[]{:S(2)}, u32[]{:S(2)}) collective-permute-start(bf16[8,6144]{1,0:T(8,128)(2,1)S(1)} %shard_map.71), channel_id=1, source_target_pairs={{0,2},{1,5},{2,0},{3,7},{4,6},{5,1},{6,4},{7,3},{8,10},{9,13},{10,... | collective-permute-start | bytes 294920 | tf_op jit(solution)/shard_map/ppermute | solution.py:285
  56.4 6.5 %collective-permute-done.17.refs_3_ = bf16[8,6144]{1,0:T(8,128)(2,1)S(1)} collective-permute-done((bf16[8,6144]{1,0:T(8,128)(2,1)S(1)}, bf16[8,6144]{1,0:T(8,128)(2,1)S(1)}, u32[]{:S(2)}, u32[]{:S(2)}) %collective-permute-start.17) | collective-permute-done | bytes 98336 | tf_op jit(solution)/shard_map/ppermute | solution.py:285
  62.9 0.7 %shard_map.74 = bf16[12,4096]{1,0:T(8,128)(2,1)} custom-call(bf16[8,6144]{1,0:T(8,128)(2,1)S(1)} %get-tuple-element.48.refs_0_, bf16[8,6144]{1,0:T(8,128)(2,1)S(1)} %collective-permute-done.13.refs_1_, bf16[16,6144]{1,0:T(8,128)(2,1)S(1)} %collective-permute-done.12.b.refs_2_, bf16[8,6144]{1,0:T(8,128)(2,1)S(1)} %collective-permute-done.17.refs_3_, ...), custom_call_target="tpu_custom_call" | custom-call | tf_op jit(solution)/shard_map/pallas_call | solution.py:29
  (17 shorter events, 0.3 us)
Async XLA Ops:
  1.0 1.5 %collective-permute-start.1 = (bf16[8,6272]{1,0:T(8,128)(2,1)S(1)}, bf16[8,6272]{1,0:T(8,128)(2,1)S(1)}, u32[]{:S(2)}, u32[]{:S(2)}) collective-permute-start(bf16[8,6272]{1,0:T(8,128)(2,1)S(1)} %shard_map.64.refs_0_.a), channel_id=1, source_target_pairs={{0,1},{1,0},{2,3},{3,2},{4,5},{5,4},{6,7},{7,6},{8,9},{9,8},{10,11... | collective-permute-start | bytes 301064 | tf_op jit(solution)/shard_map/ppermute | solution.py:285
  2.5 24.4 %collective-permute-start.8 = (bf16[4096,384]{1,0:T(8,128)(2,1)}, bf16[4096,384]{1,0:T(8,128)(2,1)}, u32[]{:S(2)}, u32[]{:S(2)}) collective-permute-start(bf16[4096,384]{1,0:T(8,128)(2,1)} %bitcast.6), channel_id=1, source_target_pairs={{0,1},{1,0},{2,3},{3,2},{4,5},{5,4},{6,7},{7,6},{8,9},{9,8},{10,11... | collective-permute-start | bytes 9437192 | tf_op jit(solution)/shard_map/ppermute | solution.py:285
  2.9 25.5 %collective-permute-start.9 = (bf16[4096,384]{1,0:T(8,128)(2,1)}, bf16[4096,384]{1,0:T(8,128)(2,1)}, u32[]{:S(2)}, u32[]{:S(2)}) collective-permute-start(bf16[4096,384]{1,0:T(8,128)(2,1)} %bitcast.8), channel_id=1, source_target_pairs={{0,1},{1,0},{2,3},{3,2},{4,5},{5,4},{6,7},{7,6},{8,9},{9,8},{10,11... | collective-permute-start | bytes 9437192 | tf_op jit(solution)/shard_map/ppermute | solution.py:285
  3.1 31.2 %collective-permute-start.10 = (bf16[384,4096]{1,0:T(8,128)(2,1)}, bf16[384,4096]{1,0:T(8,128)(2,1)}, u32[]{:S(2)}, u32[]{:S(2)}) collective-permute-start(bf16[384,4096]{1,0:T(8,128)(2,1)} %bitcast.10), channel_id=1, source_target_pairs={{0,1},{1,0},{2,3},{3,2},{4,5},{5,4},{6,7},{7,6},{8,9},{9,8},{10,11... | collective-permute-start | bytes 9437192 | tf_op jit(solution)/shard_map/ppermute | solution.py:285
  3.4 5.3 %collective-permute-start = (bf16[8,6272]{1,0:T(8,128)(2,1)S(1)}, bf16[8,6272]{1,0:T(8,128)(2,1)S(1)}, u32[]{:S(2)}, u32[]{:S(2)}) collective-permute-start(bf16[8,6272]{1,0:T(8,128)(2,1)S(1)} %shard_map.64.refs_0_.a), channel_id=1, source_target_pairs={{0,2},{1,5},{2,0},{3,7},{4,6},{5,1},{6,4},{7,3},{8,10},{9,13},{10,... | collective-permute-start | bytes 301064 | tf_op jit(solution)/shard_map/ppermute | solution.py:285
  6.0 12.4 %collective-permute-start.2 = (bf16[24,4224]{1,0:T(8,128)(2,1)S(1)}, bf16[24,4224]{1,0:T(8,128)(2,1)S(1)}, u32[]{:S(2)}, u32[]{:S(2)}) collective-permute-start(bf16[24,4224]{1,0:T(8,128)(2,1)S(1)} %shard_map.65), channel_id=1, source_target_pairs={{0,16},{1,25},{2,18},{3,27},{4,20},{5,29},{6,22},{7,31},{8,24},{9,... | collective-permute-start | bytes 608264 | tf_op jit(solution)/shard_map/ppermute | solution.py:285
  8.7 5.8 %collective-permute-start.3 = (bf16[16,6272]{1,0:T(8,128)(2,1)S(1)}, bf16[16,6272]{1,0:T(8,128)(2,1)S(1)}, u32[]{:S(2)}, u32[]{:S(2)}) collective-permute-start(bf16[16,6272]{1,0:T(8,128)(2,1)S(1)} %shard_map.66), channel_id=1, source_target_pairs={{0,4},{1,3},{2,6},{3,1},{4,0},{5,7},{6,2},{7,5},{8,12},{9,11},{10,... | collective-permute-start | bytes 602120 | tf_op jit(solution)/shard_map/ppermute | solution.py:285
  18.5 7.9 %collective-permute-start.5 = (bf16[24,4224]{1,0:T(8,128)(2,1)S(1)}, bf16[24,4224]{1,0:T(8,128)(2,1)S(1)}, u32[]{:S(2)}, u32[]{:S(2)}) collective-permute-start(bf16[24,4224]{1,0:T(8,128)(2,1)S(1)} %collective-permute-done.2.refs_2_), channel_id=1, source_target_pairs={{0,2},{1,5},{2,0},{3,7},{4,6},{5,1},{6,4},{7,3},{8,10},{9,13},{10,... | collective-permute-start | bytes 608264 | tf_op jit(solution)/shard_map/ppermute | solution.py:285
  19.0 15.3 %collective-permute-start.4 = (bf16[48,4224]{1,0:T(8,128)(2,1)S(1)}, bf16[48,4224]{1,0:T(8,128)(2,1)S(1)}, u32[]{:S(2)}, u32[]{:S(2)}) collective-permute-start(bf16[48,4224]{1,0:T(8,128)(2,1)S(1)} %shard_map.67.refs_0_), channel_id=1, source_target_pairs={{0,8},{1,9},{2,10},{3,11},{4,12},{5,13},{6,14},{7,15},{8,0},{9,1},... | collective-permute-start | bytes 1216520 | tf_op jit(solution)/shard_map/ppermute | solution.py:285
  26.4 7.8 %collective-permute-start.6 = (bf16[24,4224]{1,0:T(8,128)(2,1)S(1)}, bf16[24,4224]{1,0:T(8,128)(2,1)S(1)}, u32[]{:S(2)}, u32[]{:S(2)}) collective-permute-start(bf16[24,4224]{1,0:T(8,128)(2,1)S(1)} %collective-permute-done.2.refs_2_), channel_id=1, source_target_pairs={{0,4},{1,3},{2,6},{3,1},{4,0},{5,7},{6,2},{7,5},{8,12},{9,11},{10,... | collective-permute-start | bytes 608264 | tf_op jit(solution)/shard_map/ppermute | solution.py:285
  26.9 7.4 %collective-permute-start.7 = (bf16[24,4224]{1,0:T(8,128)(2,1)S(1)}, bf16[24,4224]{1,0:T(8,128)(2,1)S(1)}, u32[]{:S(2)}, u32[]{:S(2)}) collective-permute-start(bf16[24,4224]{1,0:T(8,128)(2,1)S(1)} %collective-permute-done.5.refs_3_), channel_id=1, source_target_pairs={{0,4},{1,3},{2,6},{3,1},{4,0},{5,7},{6,2},{7,5},{8,12},{9,11},{10,... | collective-permute-start | bytes 608264 | tf_op jit(solution)/shard_map/ppermute | solution.py:285
  40.1 7.8 %collective-permute-start.11 = (bf16[48,4096]{1,0:T(8,128)(2,1)S(1)}, bf16[48,4096]{1,0:T(8,128)(2,1)S(1)}, u32[]{:S(2)}, u32[]{:S(2)}) collective-permute-start(bf16[48,4096]{1,0:T(8,128)(2,1)S(1)} %get-tuple-element.47), channel_id=1, source_target_pairs={{0,8},{1,9},{2,10},{3,11},{4,12},{5,13},{6,14},{7,15},{8,0},{9,1},... | collective-permute-start | bytes 1179656 | tf_op jit(solution)/shard_map/ppermute | solution.py:285
  40.2 7.1 %collective-permute-start.15 = (bf16[24,4096]{1,0:T(8,128)(2,1)S(1)}, bf16[24,4096]{1,0:T(8,128)(2,1)S(1)}, u32[]{:S(2)}, u32[]{:S(2)}) collective-permute-start(bf16[24,4096]{1,0:T(8,128)(2,1)S(1)} %get-tuple-element.54), channel_id=1, source_target_pairs={{0,4},{1,3},{2,6},{3,1},{4,0},{5,7},{6,2},{7,5},{8,12},{9,11},{10,... | collective-permute-start | bytes 589832 | tf_op jit(solution)/shard_map/ppermute | solution.py:285
  40.7 9.3 %collective-permute-start.14 = (bf16[24,4096]{1,0:T(8,128)(2,1)S(1)}, bf16[24,4096]{1,0:T(8,128)(2,1)S(1)}, u32[]{:S(2)}, u32[]{:S(2)}) collective-permute-start(bf16[24,4096]{1,0:T(8,128)(2,1)S(1)} %get-tuple-element.52), channel_id=1, source_target_pairs={{0,4},{1,3},{2,6},{3,1},{4,0},{5,7},{6,2},{7,5},{8,12},{9,11},{10,... | collective-permute-start | bytes 589832 | tf_op jit(solution)/shard_map/ppermute | solution.py:285
  47.4 5.7 %collective-permute-start.16 = (bf16[24,4096]{1,0:T(8,128)(2,1)S(1)}, bf16[24,4096]{1,0:T(8,128)(2,1)S(1)}, u32[]{:S(2)}, u32[]{:S(2)}) collective-permute-start(bf16[24,4096]{1,0:T(8,128)(2,1)S(1)} %shard_map.72), channel_id=1, source_target_pairs={{0,2},{1,5},{2,0},{3,7},{4,6},{5,1},{6,4},{7,3},{8,10},{9,13},{10,... | collective-permute-start | bytes 589832 | tf_op jit(solution)/shard_map/ppermute | solution.py:285
  48.1 6.3 %collective-permute-start.12 = (bf16[16,6144]{1,0:T(8,128)(2,1)S(1)}, bf16[16,6144]{1,0:T(8,128)(2,1)S(1)}, u32[]{:S(2)}, u32[]{:S(2)}) collective-permute-start(bf16[16,6144]{1,0:T(8,128)(2,1)S(1)} %get-tuple-element.50), channel_id=1, source_target_pairs={{0,4},{1,3},{2,6},{3,1},{4,0},{5,7},{6,2},{7,5},{8,12},{9,11},{10,... | collective-permute-start | bytes 589832 | tf_op jit(solution)/shard_map/ppermute | solution.py:285
  53.2 9.7 %collective-permute-start.17 = (bf16[8,6144]{1,0:T(8,128)(2,1)S(1)}, bf16[8,6144]{1,0:T(8,128)(2,1)S(1)}, u32[]{:S(2)}, u32[]{:S(2)}) collective-permute-start(bf16[8,6144]{1,0:T(8,128)(2,1)S(1)} %get-tuple-element.55), channel_id=1, source_target_pairs={{0,16},{1,25},{2,18},{3,27},{4,20},{5,29},{6,22},{7,31},{8,24},{9,... | collective-permute-start | bytes 294920 | tf_op jit(solution)/shard_map/ppermute | solution.py:285
  54.4 8.5 %collective-permute-start.18 = (bf16[8,6144]{1,0:T(8,128)(2,1)S(1)}, bf16[8,6144]{1,0:T(8,128)(2,1)S(1)}, u32[]{:S(2)}, u32[]{:S(2)}) collective-permute-start(bf16[8,6144]{1,0:T(8,128)(2,1)S(1)} %get-tuple-element.56), channel_id=1, source_target_pairs={{0,17},{1,24},{2,19},{3,26},{4,21},{5,28},{6,23},{7,30},{8,25},{9,... | collective-permute-start | bytes 294920 | tf_op jit(solution)/shard_map/ppermute | solution.py:285
  54.4 8.5 %collective-permute-start.13 = (bf16[8,6144]{1,0:T(8,128)(2,1)S(1)}, bf16[8,6144]{1,0:T(8,128)(2,1)S(1)}, u32[]{:S(2)}, u32[]{:S(2)}) collective-permute-start(bf16[8,6144]{1,0:T(8,128)(2,1)S(1)} %shard_map.71), channel_id=1, source_target_pairs={{0,2},{1,5},{2,0},{3,7},{4,6},{5,1},{6,4},{7,3},{8,10},{9,13},{10,... | collective-permute-start | bytes 294920 | tf_op jit(solution)/shard_map/ppermute | solution.py:285

commit v4 on v3

--- a/solution.py
+++ b/solution.py
@@ -1,4 +1,5 @@
 import functools
+import math
 
 import jax
 import jax.numpy as jnp
@@ -14,27 +15,34 @@
 LANES = 128
 STEP = 512
 PIECES = 4
-COST = 4 << 20
+ROOM = 3
 VMEM = pl.BlockSpec(memory_space=pltpu.VMEM)
 SMEM = pl.BlockSpec(memory_space=pltpu.SMEM)
 HBM = pl.BlockSpec(memory_space=pltpu.HBM)
 
 
-def call(kernel, out_shape, in_specs, args, scratch=(), limit=8, flops=0, moved=0):
+def call(kernel, out_shape, in_specs, args, scratch=(), room=1, held=0, flops=0):
     args = [
         pltpu.with_memory_space_constraint(arg, pltpu.HBM) if spec is HBM else arg
         for arg, spec in zip(args, in_specs)
     ]
     single = not isinstance(out_shape, tuple)
+    outs = (out_shape,) if single else out_shape
+    arrays = [arg for arg, spec in zip(args, in_specs) if spec is VMEM] + [*outs, *scratch]
+    size = sum(math.prod(array.shape) * array.dtype.itemsize for array in arrays if hasattr(array.dtype, "itemsize"))
     return pl.pallas_call(
         kernel,
         out_shape=out_shape,
         in_specs=in_specs,
         out_specs=VMEM if single else (VMEM,) * len(out_shape),
         scratch_shapes=scratch,
-        compiler_params=pltpu.CompilerParams(vmem_limit_bytes=limit << 20),
-        cost_estimate=pl.CostEstimate(flops=flops, bytes_accessed=moved, transcendentals=0),
+        compiler_params=pltpu.CompilerParams(vmem_limit_bytes=size - held + (room << 20)),
+        cost_estimate=pl.CostEstimate(flops=flops, bytes_accessed=0, transcendentals=0),
     )(*args)
+
+
+def size_of(arrays):
+    return sum(math.prod(array.shape) * array.dtype.itemsize for array in arrays)
 
 
 def upper_rows(shape):
@@ -171,10 +179,10 @@
         put(width + start, rest)
 
 
-def split_rows(parts, order, cost=0):
+def split_rows(parts, order):
     width = parts[0].shape[1]
     shapes = tuple(jax.ShapeDtypeStruct((TILE * len(blocks), width + width // 2), BF16) for blocks in order)
-    return call(functools.partial(split_kernel, order), shapes, [VMEM] * len(parts), parts, moved=cost)
+    return call(functools.partial(split_kernel, order), shapes, [VMEM] * len(parts), parts)
 
 
 def last_kernel(*refs):
@@ -218,15 +226,13 @@
         [HBM] * len(arrays),
         arrays,
         [pltpu.SemaphoreType.DMA((len(arrays), PIECES))],
+        held=size_of(arrays),
     )
 
 
 def expert_kernel(experts, count, mine, *refs):
-    parts, own, others, source = refs[:count], refs[count : count + 3], refs[count + 3 : count + 5], refs[count + 5]
-    outs, (xs, inner, last, sem) = refs[count + 6 : -4], refs[-4:]
-    others += (last,)
-    copy = pltpu.make_async_copy(source, last, sem)
-    copy.start()
+    parts, own, others = refs[:count], refs[count : count + 3], refs[count + 3 : count + 6]
+    outs, (xs, inner) = refs[count + 6 : -2], refs[-2:]
     width = outs[0].shape[1]
     units = own[0].shape[1]
 
@@ -249,7 +255,6 @@
             value = jax.nn.silu(total[:, :LANES]) * total[:, LANES:] * scale
             inner[:, at * units + tile : at * units + tile + LANES] = value.astype(BF16)
 
-    copy.wait()
     for start in range(0, width, STEP):
         mat = jnp.concatenate([own[2][:, start : start + STEP], others[2][:, start : start + STEP]], axis=0)
         value = jnp.dot(inner[...], mat, preferred_element_type=F32)
@@ -262,20 +267,18 @@
 def expert_rows(parts, outs, width, mine, experts, weights):
     rows = sum(part.shape[0] for part in parts)
     units = weights[0].shape[1]
-    *weights, last = weights
     weights = [pltpu.with_memory_space_constraint(w, pltpu.VMEM) for w in weights]
     return call(
         functools.partial(expert_kernel, experts, len(parts)),
         tuple(jax.ShapeDtypeStruct((n, width), BF16) for n in outs),
-        [SMEM] + [VMEM] * (len(parts) + len(weights)) + [HBM],
-        (mine, *parts, *weights, last),
+        [SMEM] + [VMEM] * (len(parts) + len(weights)),
+        (mine, *parts, *weights),
         [
             pltpu.VMEM((rows, width), BF16),
             pltpu.VMEM((rows, 2 * units), BF16),
-            pltpu.VMEM(last.shape, BF16),
-            pltpu.SemaphoreType.DMA,
         ],
-        limit=16,
+        room=ROOM,
+        held=size_of(weights),
         flops=6 * rows * width * 2 * units,
     )
 
@@ -315,8 +318,8 @@
         out[:, at] = (a[:, at].astype(F32) + b[:, at].astype(F32)[-rows:]).astype(BF16)
 
 
-def add(a, b, cost=0):
-    return call(add_kernel, jax.ShapeDtypeStruct(a.shape, BF16), [VMEM] * 2, (a, b), moved=cost)
+def add(a, b):
+    return call(add_kernel, jax.ShapeDtypeStruct(a.shape, BF16), [VMEM] * 2, (a, b))
 
 
 def per_device(hidden, expert_ids, gate_raw, w_gate, w_up, w_down):
@@ -333,19 +336,22 @@
 
     both = pair_rows((own, go(own, lambda device: 1)), width, experts)
     weights, both = lax.optimization_barrier((weights, both))
-    others = [go(w, lambda device: 1) for w in weights]
+    others = [go(w, lambda device: 1) for w in weights[:2]]
     far = [go(both, lambda device, s=step: level_flip(s, device)) for step in range(2, levels, 2)]
     far = far[0] if len(far) == 1 else jnp.concatenate(far, axis=0)
     own_first = go(own, first_flip)
-    own_second = go(join(own, own_first), second_flip)
-    far, own_second = lax.optimization_barrier((far, own_second))
+    plane = (own, own_first, go(join(own, own_first), second_flip))
+    weights, own_first = lax.optimization_barrier((weights, own_first))
+    weights = list(fetch(weights[:1])) + weights[1:]
+    far, plane, weights = lax.optimization_barrier((far, plane, weights))
+    others.append(go(weights[2], lambda device: 1))
     far_first = go(far, first_flip)
     far_second = go(far, second_flip)
-    near = pair_rows((own, own_first, own_second), width, experts)
+    near = pair_rows(plane, width, experts)
     near_other = go(near, lambda device: 8)
-    weights, far_first = lax.optimization_barrier((weights, far_first))
+    others, far_first = lax.optimization_barrier((others, far_first))
     far_third = go(far_first, second_flip)
-    weights = list(fetch(weights + others[:2])) + others[2:]
+    weights = weights[:1] + list(fetch(weights[1:] + others))
 
     many, more = far.shape[0], near.shape[0]
     near, near_other, far, far_first, far_second, far_third = expert_rows(
@@ -360,8 +366,8 @@
     far_third = go(far_third, second_flip)
     far_second = go(far_second, second_flip)
     near_other = go(near_other, lambda device: 8)
-    far_first = go(add(far_first, far_third, COST), first_flip)
-    far = split_rows((far, far_second, far_first), [(block,) for block in range(levels - 2)], COST)
+    far_first = go(add(far_first, far_third), first_flip)
+    far = split_rows((far, far_second, far_first), [(block,) for block in range(levels - 2)])
     far = [
         go(block, lambda device, s=step, twin=twin: level_flip(s, device) + twin)
         for block, (step, twin) in zip(far, [(s, t) for s in range(2, levels, 2) for t in range(2)])

time: 64.3 us -> 62.6 us (0.974)
  waiting for transfers between devices: 30.5 us -> 21.5 us
  local copies, waits for them, and re-layouts: 0 us -> 2.85 us
  starting transfers between devices: 19.4 us -> 21.9 us
  Pallas kernels: 13.6 us -> 15 us
    ppermute x19, waiting for transfers between devices: 30.5 us -> 21.5 us  [permute(): return lax.ppermute(value, 'expert', pairs)]
    unnamed x0 -> x8, local copies, waits for them, and re-layouts: none -> 2.85 us
    ppermute x19, starting transfers between devices: 19.4 us -> 21.9 us  [permute(): return lax.ppermute(value, 'expert', pairs)]
    pallas_call x11 -> x12, Pallas kernels: 13.6 us -> 15 us  [call(): pl.pallas_call(kernel, out_shape=out_shape, in_specs=in_specs, out_specs=...]
  transfers between devices with their start and end apart: 19 -> 19, of which waited for: 9 -> 7; matrix products, arithmetic and copies ran while one was open for 0% -> 0% of each run, Pallas kernels for 10% -> 13%
where the time goes in v4:
time: 62.6 us; the launch traced here: 61.4 us
  starting transfers between devices  21.9 us (35%)
  waiting for transfers between devices  21.5 us (34%)
  Pallas kernels  15 us (24%)
  local copies, waits for them, and re-layouts  2.85 us (5%)
    ppermute x19, starting transfers between devices, permute(): return lax.ppermute(value, 'expert', pairs)  21.9 us
    ppermute x19, waiting for transfers between devices, permute(): return lax.ppermute(value, 'expert', pairs)  21.5 us
    pallas_call x12, Pallas kernels, call(): pl.pallas_call(kernel, out_shape=out_shape, in_specs=in_specs, out_specs=...  15 us
    unnamed x8, local copies, waits for them, and re-layouts  2.85 us
  transfers between devices with their start and end apart: 19, of which 7 were waited for; matrix products, arithmetic and copies ran while one was open for 0% of the time, Pallas kernels for 13%

profile of v4, /device:TPU:0, one launch (start us, length us, event | category | flops | bytes accessed | tf_op | source)
XLA Modules:
  0.0 61.4 jit_solution(7835603740109425764)
XLA Ops:
  0.0 1.0 %shard_map.64.refs_0_.a = bf16[8,6272]{1,0:T(8,128)(2,1)S(1)} custom-call(s32[8,12]{1,0:T(8,128)} %bitcast.12, f32[8,12]{1,0:T(8,128)} %bitcast.13, bf16[12,4096]{1,0:T(8,128)(2,1)} %refs_2_.1), custom_call_target="tpu_custom_call" | custom-call | tf_op jit(solution)/shard_map/pallas_call | solution.py:33
  1.0 0.5 collective-permute-start
  1.5 2.6 %collective-permute-start.2 = (bf16[8,6272]{1,0:T(8,128)(2,1)S(1)}, bf16[8,6272]{1,0:T(8,128)(2,1)S(1)}, u32[]{:S(2)}, u32[]{:S(2)}) collective-permute-start(bf16[8,6272]{1,0:T(8,128)(2,1)S(1)} %shard_map.64.refs_0_.a), channel_id=1, source_target_pairs={{0,2},{1,5},{2,0},{3,7},{4,6},{5,1},{6,4},{7,3},{8,10},{9,13},{10,... | collective-permute-start | bytes 301064 | tf_op jit(solution)/shard_map/ppermute | solution.py:288
  4.1 2.7 %collective-permute-start.1 = (bf16[24,4224]{1,0:T(8,128)(2,1)S(1)}, bf16[24,4224]{1,0:T(8,128)(2,1)}, u32[]{:S(2)}, u32[]{:S(2)}) collective-permute-start(bf16[24,4224]{1,0:T(8,128)(2,1)S(1)} %shard_map.65), channel_id=1, source_target_pairs={{0,16},{1,25},{2,18},{3,27},{4,20},{5,29},{6,22},{7,31},{8,24},{9,... | collective-permute-start | bytes 608264 | tf_op jit(solution)/shard_map/ppermute | solution.py:288
  6.8 2.0 %collective-permute-start.3 = (bf16[16,6272]{1,0:T(8,128)(2,1)S(1)}, bf16[16,6272]{1,0:T(8,128)(2,1)S(1)}, u32[]{:S(2)}, u32[]{:S(2)}) collective-permute-start(bf16[16,6272]{1,0:T(8,128)(2,1)S(1)} %shard_map.66), channel_id=1, source_target_pairs={{0,4},{1,3},{2,6},{3,1},{4,0},{5,7},{6,2},{7,5},{8,12},{9,11},{10,... | collective-permute-start | bytes 602120 | tf_op jit(solution)/shard_map/ppermute | solution.py:288
  8.9 0.1 collective-permute-start.5
  9.0 0.4 collective-permute-start.6
  9.4 1.9 %shard_map.67.refs_6_ = bf16[4096,384]{1,0:T(8,128)(2,1)S(1)} custom-call(bf16[4096,384]{1,0:T(8,128)(2,1)} %bitcast.7), custom_call_target="tpu_custom_call" | custom-call | tf_op jit(solution)/shard_map/pallas_call | solution.py:33
  11.2 1.3 %collective-permute-done.3.refs_2_ = bf16[16,6272]{1,0:T(8,128)(2,1)S(1)} collective-permute-done((bf16[16,6272]{1,0:T(8,128)(2,1)S(1)}, bf16[16,6272]{1,0:T(8,128)(2,1)S(1)}, u32[]{:S(2)}, u32[]{:S(2)}) %collective-permute-start.3) | collective-permute-done | bytes 200736 | tf_op jit(solution)/shard_map/ppermute | solution.py:288
  12.6 4.2 %collective-permute-done.1.refs_2_ = bf16[24,4224]{1,0:T(8,128)(2,1)} collective-permute-done((bf16[24,4224]{1,0:T(8,128)(2,1)S(1)}, bf16[24,4224]{1,0:T(8,128)(2,1)}, u32[]{:S(2)}, u32[]{:S(2)}) %collective-permute-start.1) | collective-permute-done | bytes 202784 | tf_op jit(solution)/shard_map/ppermute | solution.py:288
  16.8 1.5 %collective-permute-start.8 = (bf16[24,4224]{1,0:T(8,128)(2,1)}, bf16[24,4224]{1,0:T(8,128)(2,1)}, u32[]{:S(2)}, u32[]{:S(2)}) collective-permute-start(bf16[24,4224]{1,0:T(8,128)(2,1)} %collective-permute-done.1.refs_2_), channel_id=1, source_target_pairs={{0,2},{1,5},{2,0},{3,7},{4,6},{5,1},{6,4},{7,3},{8,10},{9,13},{10,... | collective-permute-start | bytes 608264 | tf_op jit(solution)/shard_map/ppermute | solution.py:288
  18.3 0.1 collective-permute-start.4
  18.4 4.4 %collective-permute-done.8.refs_3_ = bf16[24,4224]{1,0:T(8,128)(2,1)} collective-permute-done((bf16[24,4224]{1,0:T(8,128)(2,1)}, bf16[24,4224]{1,0:T(8,128)(2,1)}, u32[]{:S(2)}, u32[]{:S(2)}) %collective-permute-start.8) | collective-permute-done | bytes 202784 | tf_op jit(solution)/shard_map/ppermute | solution.py:288
  22.8 1.2 %collective-permute-start.9 = (bf16[24,4224]{1,0:T(8,128)(2,1)}, bf16[24,4224]{1,0:T(8,128)(2,1)}, u32[]{:S(2)}, u32[]{:S(2)}) collective-permute-start(bf16[24,4224]{1,0:T(8,128)(2,1)} %collective-permute-done.1.refs_2_), channel_id=1, source_target_pairs={{0,4},{1,3},{2,6},{3,1},{4,0},{5,7},{6,2},{7,5},{8,12},{9,11},{10,... | collective-permute-start | bytes 608264 | tf_op jit(solution)/shard_map/ppermute | solution.py:288
  24.1 1.6 %copy-done.1 = bf16[4096,384]{1,0:T(8,128)(2,1)} copy-done((bf16[4096,384]{1,0:T(8,128)(2,1)}, bf16[4096,384]{1,0:T(8,128)(2,1)S(1)}, u32[]{:S(2)}) %copy-start.1) | copy-done | bytes 3145752
  25.7 0.8 %collective-permute-start.10 = (bf16[24,4224]{1,0:T(8,128)(2,1)}, bf16[24,4224]{1,0:T(8,128)(2,1)}, u32[]{:S(2)}, u32[]{:S(2)}) collective-permute-start(bf16[24,4224]{1,0:T(8,128)(2,1)} %collective-permute-done.8.refs_3_), channel_id=1, source_target_pairs={{0,4},{1,3},{2,6},{3,1},{4,0},{5,7},{6,2},{7,5},{8,12},{9,11},{10,... | collective-permute-start | bytes 608264 | tf_op jit(solution)/shard_map/ppermute | solution.py:288
  26.5 0.2 copy-done.2
  26.7 1.0 %copy-done.3 = bf16[384,4096]{1,0:T(8,128)(2,1)} copy-done((bf16[384,4096]{1,0:T(8,128)(2,1)}, bf16[384,4096]{1,0:T(8,128)(2,1)S(1)}, u32[]{:S(2)}) %copy-start.3) | copy-done | bytes 3145752
  27.7 5.7 %shard_map.69 = (bf16[4096,384]{1,0:T(8,128)(2,1)S(1)}, bf16[384,4096]{1,0:T(8,128)(2,1)S(1)}, bf16[4096,384]{1,0:T(8,128)(2,1)S(1)}, bf16[4096,384]{1,0:T(8,128)(2,1)S(1)}, bf16[384,4096]{1,0:T(8,128)(2,1)S(1)}) custom-call(bf16[4096,384]{1,0:T(8,128)(2,1)} %bitcast.9, bf16[384,4096]{1,0:T(8,128)(2,1)} %bitcast.10, bf16[4096,384]{1,0:T(8,128)(2,1)} %copy-done.1, ...), custom_call_target="tpu_custom_call" | custom-call | tf_op jit(solution)/shard_map/pallas_call | solution.py:33
  33.4 5.3 %shard_map.70 = (bf16[48,4096]{1,0:T(8,128)(2,1)S(1)}, bf16[48,4096]{1,0:T(8,128)(2,1)S(1)}, bf16[24,4096]{1,0:T(8,128)(2,1)S(1)}, bf16[24,4096]{1,0:T(8,128)(2,...) custom-call(s32[1]{0:T(128)} %bitcast.mine, bf16[48,4224]{1,0:T(8,128)(2,1)S(1)} %shard_map.68.refs_0_, ...), custom_call_target="tpu_custom_call" | custom-call | flops 3623878656 | tf_op jit(solution)/shard_map/pallas_call | solution.py:33
  38.8 0.9 %collective-permute-start.15 = (bf16[24,4096]{1,0:T(8,128)(2,1)S(1)}, bf16[24,4096]{1,0:T(8,128)(2,1)S(1)}, u32[]{:S(2)}, u32[]{:S(2)}) collective-permute-start(bf16[24,4096]{1,0:T(8,128)(2,1)S(1)} %get-tuple-element.70), channel_id=1, source_target_pairs={{0,4},{1,3},{2,6},{3,1},{4,0},{5,7},{6,2},{7,5},{8,12},{9,11},{10,... | collective-permute-start | bytes 589832 | tf_op jit(solution)/shard_map/ppermute | solution.py:288
  39.7 1.2 %collective-permute-start.14 = (bf16[24,4096]{1,0:T(8,128)(2,1)S(1)}, bf16[24,4096]{1,0:T(8,128)(2,1)S(1)}, u32[]{:S(2)}, u32[]{:S(2)}) collective-permute-start(bf16[24,4096]{1,0:T(8,128)(2,1)S(1)} %get-tuple-element.68), channel_id=1, source_target_pairs={{0,4},{1,3},{2,6},{3,1},{4,0},{5,7},{6,2},{7,5},{8,12},{9,11},{10,... | collective-permute-start | bytes 589832 | tf_op jit(solution)/shard_map/ppermute | solution.py:288
  40.9 3.6 %collective-permute-done.15.b = bf16[24,4096]{1,0:T(8,128)(2,1)S(1)} collective-permute-done((bf16[24,4096]{1,0:T(8,128)(2,1)S(1)}, bf16[24,4096]{1,0:T(8,128)(2,1)S(1)}, u32[]{:S(2)}, u32[]{:S(2)}) %collective-permute-start.15) | collective-permute-done | bytes 196640 | tf_op jit(solution)/shard_map/ppermute | solution.py:288
  44.6 1.6 %collective-permute-start.16 = (bf16[24,4096]{1,0:T(8,128)(2,1)S(1)}, bf16[24,4096]{1,0:T(8,128)(2,1)S(1)}, u32[]{:S(2)}, u32[]{:S(2)}) collective-permute-start(bf16[24,4096]{1,0:T(8,128)(2,1)S(1)} %shard_map.73), channel_id=1, source_target_pairs={{0,2},{1,5},{2,0},{3,7},{4,6},{5,1},{6,4},{7,3},{8,10},{9,13},{10,... | collective-permute-start | bytes 589832 | tf_op jit(solution)/shard_map/ppermute | solution.py:288
  46.2 3.3 %collective-permute-done.11.refs_1_ = bf16[48,4096]{1,0:T(8,128)(2,1)S(1)} collective-permute-done((bf16[48,4096]{1,0:T(8,128)(2,1)S(1)}, bf16[48,4096]{1,0:T(8,128)(2,1)S(1)}, u32[]{:S(2)}, u32[]{:S(2)}) %collective-permute-start.11) | collective-permute-done | bytes 393248 | tf_op jit(solution)/shard_map/ppermute | solution.py:288
  49.5 0.1 shard_map.71
  49.6 1.3 %collective-permute-start.12 = (bf16[16,6144]{1,0:T(8,128)(2,1)S(1)}, bf16[16,6144]{1,0:T(8,128)(2,1)S(1)}, u32[]{:S(2)}, u32[]{:S(2)}) collective-permute-start(bf16[16,6144]{1,0:T(8,128)(2,1)S(1)} %get-tuple-element.66), channel_id=1, source_target_pairs={{0,4},{1,3},{2,6},{3,1},{4,0},{5,7},{6,2},{7,5},{8,12},{9,11},{10,... | collective-permute-start | bytes 589832 | tf_op jit(solution)/shard_map/ppermute | solution.py:288
  51.0 3.4 %collective-permute-start.17 = (bf16[8,6144]{1,0:T(8,128)(2,1)S(1)}, bf16[8,6144]{1,0:T(8,128)(2,1)S(1)}, u32[]{:S(2)}, u32[]{:S(2)}) collective-permute-start(bf16[8,6144]{1,0:T(8,128)(2,1)S(1)} %get-tuple-element.71), channel_id=1, source_target_pairs={{0,16},{1,25},{2,18},{3,27},{4,20},{5,29},{6,22},{7,31},{8,24},{9,... | collective-permute-start | bytes 294920 | tf_op jit(solution)/shard_map/ppermute | solution.py:288
  54.4 0.9 %collective-permute-done.12.b.refs_2_ = bf16[16,6144]{1,0:T(8,128)(2,1)S(1)} collective-permute-done((bf16[16,6144]{1,0:T(8,128)(2,1)S(1)}, bf16[16,6144]{1,0:T(8,128)(2,1)S(1)}, u32[]{:S(2)}, u32[]{:S(2)}) %collective-permute-start.12) | collective-permute-done | bytes 196640 | tf_op jit(solution)/shard_map/ppermute | solution.py:288
  55.4 1.6 %collective-permute-start.13 = (bf16[8,6144]{1,0:T(8,128)(2,1)S(1)}, bf16[8,6144]{1,0:T(8,128)(2,1)S(1)}, u32[]{:S(2)}, u32[]{:S(2)}) collective-permute-start(bf16[8,6144]{1,0:T(8,128)(2,1)S(1)} %shard_map.72), channel_id=1, source_target_pairs={{0,2},{1,5},{2,0},{3,7},{4,6},{5,1},{6,4},{7,3},{8,10},{9,13},{10,... | collective-permute-start | bytes 294920 | tf_op jit(solution)/shard_map/ppermute | solution.py:288
  57.0 3.7 %collective-permute-done.17.refs_3_ = bf16[8,6144]{1,0:T(8,128)(2,1)S(1)} collective-permute-done((bf16[8,6144]{1,0:T(8,128)(2,1)S(1)}, bf16[8,6144]{1,0:T(8,128)(2,1)S(1)}, u32[]{:S(2)}, u32[]{:S(2)}) %collective-permute-start.17) | collective-permute-done | bytes 98336 | tf_op jit(solution)/shard_map/ppermute | solution.py:288
  60.7 0.7 %shard_map.75 = bf16[12,4096]{1,0:T(8,128)(2,1)} custom-call(bf16[8,6144]{1,0:T(8,128)(2,1)S(1)} %get-tuple-element.64.refs_0_, bf16[8,6144]{1,0:T(8,128)(2,1)S(1)} %collective-permute-done.13.refs_1_, bf16[16,6144]{1,0:T(8,128)(2,1)S(1)} %collective-permute-done.12.b.refs_2_, bf16[8,6144]{1,0:T(8,128)(2,1)S(1)} %collective-permute-done.17.refs_3_, ...), custom_call_target="tpu_custom_call" | custom-call | tf_op jit(solution)/shard_map/pallas_call | solution.py:33
  (26 shorter events, 0.4 us)
Async XLA Ops:
  1.0 3.1 %collective-permute-start = (bf16[8,6272]{1,0:T(8,128)(2,1)S(1)}, bf16[8,6272]{1,0:T(8,128)(2,1)S(1)}, u32[]{:S(2)}, u32[]{:S(2)}) collective-permute-start(bf16[8,6272]{1,0:T(8,128)(2,1)S(1)} %shard_map.64.refs_0_.a), channel_id=1, source_target_pairs={{0,1},{1,0},{2,3},{3,2},{4,5},{5,4},{6,7},{7,6},{8,9},{9,8},{10,11... | collective-permute-start | bytes 301064 | tf_op jit(solution)/shard_map/ppermute | solution.py:288
  1.5 5.3 %collective-permute-start.2 = (bf16[8,6272]{1,0:T(8,128)(2,1)S(1)}, bf16[8,6272]{1,0:T(8,128)(2,1)S(1)}, u32[]{:S(2)}, u32[]{:S(2)}) collective-permute-start(bf16[8,6272]{1,0:T(8,128)(2,1)S(1)} %shard_map.64.refs_0_.a), channel_id=1, source_target_pairs={{0,2},{1,5},{2,0},{3,7},{4,6},{5,1},{6,4},{7,3},{8,10},{9,13},{10,... | collective-permute-start | bytes 301064 | tf_op jit(solution)/shard_map/ppermute | solution.py:288
  4.1 12.6 %collective-permute-start.1 = (bf16[24,4224]{1,0:T(8,128)(2,1)S(1)}, bf16[24,4224]{1,0:T(8,128)(2,1)}, u32[]{:S(2)}, u32[]{:S(2)}) collective-permute-start(bf16[24,4224]{1,0:T(8,128)(2,1)S(1)} %shard_map.65), channel_id=1, source_target_pairs={{0,16},{1,25},{2,18},{3,27},{4,20},{5,29},{6,22},{7,31},{8,24},{9,... | collective-permute-start | bytes 608264 | tf_op jit(solution)/shard_map/ppermute | solution.py:288
  6.8 10.0 %copy-start = (bf16[1,384,4096]{2,1,0:T(8,128)(2,1)S(1)}, bf16[1,384,4096]{2,1,0:T(8,128)(2,1)}, u32[]{:S(2)}) copy-start(bf16[1,384,4096]{2,1,0:T(8,128)(2,1)} %param.11) | copy-start | bytes 9437188
  6.8 5.8 %collective-permute-start.3 = (bf16[16,6272]{1,0:T(8,128)(2,1)S(1)}, bf16[16,6272]{1,0:T(8,128)(2,1)S(1)}, u32[]{:S(2)}, u32[]{:S(2)}) collective-permute-start(bf16[16,6272]{1,0:T(8,128)(2,1)S(1)} %shard_map.66), channel_id=1, source_target_pairs={{0,4},{1,3},{2,6},{3,1},{4,0},{5,7},{6,2},{7,5},{8,12},{9,11},{10,... | collective-permute-start | bytes 602120 | tf_op jit(solution)/shard_map/ppermute | solution.py:288
  8.9 15.2 %collective-permute-start.5 = (bf16[4096,384]{1,0:T(8,128)(2,1)}, bf16[4096,384]{1,0:T(8,128)(2,1)S(1)}, u32[]{:S(2)}, u32[]{:S(2)}) collective-permute-start(bf16[4096,384]{1,0:T(8,128)(2,1)} %bitcast.6), channel_id=1, source_target_pairs={{0,1},{1,0},{2,3},{3,2},{4,5},{5,4},{6,7},{7,6},{8,9},{9,8},{10,11... | collective-permute-start | bytes 9437192 | tf_op jit(solution)/shard_map/ppermute | solution.py:288
  9.0 15.0 %collective-permute-start.6 = (bf16[4096,384]{1,0:T(8,128)(2,1)}, bf16[4096,384]{1,0:T(8,128)(2,1)S(1)}, u32[]{:S(2)}, u32[]{:S(2)}) collective-permute-start(bf16[4096,384]{1,0:T(8,128)(2,1)} %bitcast.8), channel_id=1, source_target_pairs={{0,1},{1,0},{2,3},{3,2},{4,5},{5,4},{6,7},{7,6},{8,9},{9,8},{10,11... | collective-permute-start | bytes 9437192 | tf_op jit(solution)/shard_map/ppermute | solution.py:288
  16.7 7.3 %collective-permute-start.7 = (bf16[384,4096]{1,0:T(8,128)(2,1)S(1)}, bf16[384,4096]{1,0:T(8,128)(2,1)S(1)}, u32[]{:S(2)}, u32[]{:S(2)}) collective-permute-start(bf16[384,4096]{1,0:T(8,128)(2,1)S(1)} %bitcast.11), channel_id=1, source_target_pairs={{0,1},{1,0},{2,3},{3,2},{4,5},{5,4},{6,7},{7,6},{8,9},{9,8},{10,11... | collective-permute-start | bytes 9437192 | tf_op jit(solution)/shard_map/ppermute | solution.py:288
  16.8 6.1 %collective-permute-start.8 = (bf16[24,4224]{1,0:T(8,128)(2,1)}, bf16[24,4224]{1,0:T(8,128)(2,1)}, u32[]{:S(2)}, u32[]{:S(2)}) collective-permute-start(bf16[24,4224]{1,0:T(8,128)(2,1)} %collective-permute-done.1.refs_2_), channel_id=1, source_target_pairs={{0,2},{1,5},{2,0},{3,7},{4,6},{5,1},{6,4},{7,3},{8,10},{9,13},{10,... | collective-permute-start | bytes 608264 | tf_op jit(solution)/shard_map/ppermute | solution.py:288
  18.3 15.1 %collective-permute-start.4 = (bf16[48,4224]{1,0:T(8,128)(2,1)S(1)}, bf16[48,4224]{1,0:T(8,128)(2,1)}, u32[]{:S(2)}, u32[]{:S(2)}) collective-permute-start(bf16[48,4224]{1,0:T(8,128)(2,1)S(1)} %shard_map.68.refs_0_), channel_id=1, source_target_pairs={{0,8},{1,9},{2,10},{3,11},{4,12},{5,13},{6,14},{7,15},{8,0},{9,1},... | collective-permute-start | bytes 1216520 | tf_op jit(solution)/shard_map/ppermute | solution.py:288
  22.8 10.6 %collective-permute-start.9 = (bf16[24,4224]{1,0:T(8,128)(2,1)}, bf16[24,4224]{1,0:T(8,128)(2,1)}, u32[]{:S(2)}, u32[]{:S(2)}) collective-permute-start(bf16[24,4224]{1,0:T(8,128)(2,1)} %collective-permute-done.1.refs_2_), channel_id=1, source_target_pairs={{0,4},{1,3},{2,6},{3,1},{4,0},{5,7},{6,2},{7,5},{8,12},{9,11},{10,... | collective-permute-start | bytes 608264 | tf_op jit(solution)/shard_map/ppermute | solution.py:288
  24.0 1.6 %copy-start.1 = (bf16[4096,384]{1,0:T(8,128)(2,1)}, bf16[4096,384]{1,0:T(8,128)(2,1)S(1)}, u32[]{:S(2)}) copy-start(bf16[4096,384]{1,0:T(8,128)(2,1)S(1)} %collective-permute-done.5.refs_2_) | copy-start | bytes 9437188
  24.0 2.6 %copy-start.2 = (bf16[4096,384]{1,0:T(8,128)(2,1)}, bf16[4096,384]{1,0:T(8,128)(2,1)S(1)}, u32[]{:S(2)}) copy-start(bf16[4096,384]{1,0:T(8,128)(2,1)S(1)} %collective-permute-done.6.refs_3_) | copy-start | bytes 9437188
  25.7 2.0 %copy-start.3 = (bf16[384,4096]{1,0:T(8,128)(2,1)}, bf16[384,4096]{1,0:T(8,128)(2,1)S(1)}, u32[]{:S(2)}) copy-start(bf16[384,4096]{1,0:T(8,128)(2,1)S(1)} %collective-permute-done.7.refs_4_) | copy-start | bytes 9437188
  25.7 7.8 %collective-permute-start.10 = (bf16[24,4224]{1,0:T(8,128)(2,1)}, bf16[24,4224]{1,0:T(8,128)(2,1)}, u32[]{:S(2)}, u32[]{:S(2)}) collective-permute-start(bf16[24,4224]{1,0:T(8,128)(2,1)} %collective-permute-done.8.refs_3_), channel_id=1, source_target_pairs={{0,4},{1,3},{2,6},{3,1},{4,0},{5,7},{6,2},{7,5},{8,12},{9,11},{10,... | collective-permute-start | bytes 608264 | tf_op jit(solution)/shard_map/ppermute | solution.py:288
  38.8 10.7 %collective-permute-start.11 = (bf16[48,4096]{1,0:T(8,128)(2,1)S(1)}, bf16[48,4096]{1,0:T(8,128)(2,1)S(1)}, u32[]{:S(2)}, u32[]{:S(2)}) collective-permute-start(bf16[48,4096]{1,0:T(8,128)(2,1)S(1)} %get-tuple-element.63), channel_id=1, source_target_pairs={{0,8},{1,9},{2,10},{3,11},{4,12},{5,13},{6,14},{7,15},{8,0},{9,1},... | collective-permute-start | bytes 1179656 | tf_op jit(solution)/shard_map/ppermute | solution.py:288
  38.8 5.7 %collective-permute-start.15 = (bf16[24,4096]{1,0:T(8,128)(2,1)S(1)}, bf16[24,4096]{1,0:T(8,128)(2,1)S(1)}, u32[]{:S(2)}, u32[]{:S(2)}) collective-permute-start(bf16[24,4096]{1,0:T(8,128)(2,1)S(1)} %get-tuple-element.70), channel_id=1, source_target_pairs={{0,4},{1,3},{2,6},{3,1},{4,0},{5,7},{6,2},{7,5},{8,12},{9,11},{10,... | collective-permute-start | bytes 589832 | tf_op jit(solution)/shard_map/ppermute | solution.py:288
  39.7 11.2 %collective-permute-start.14 = (bf16[24,4096]{1,0:T(8,128)(2,1)S(1)}, bf16[24,4096]{1,0:T(8,128)(2,1)S(1)}, u32[]{:S(2)}, u32[]{:S(2)}) collective-permute-start(bf16[24,4096]{1,0:T(8,128)(2,1)S(1)} %get-tuple-element.68), channel_id=1, source_target_pairs={{0,4},{1,3},{2,6},{3,1},{4,0},{5,7},{6,2},{7,5},{8,12},{9,11},{10,... | collective-permute-start | bytes 589832 | tf_op jit(solution)/shard_map/ppermute | solution.py:288
  44.6 6.3 %collective-permute-start.16 = (bf16[24,4096]{1,0:T(8,128)(2,1)S(1)}, bf16[24,4096]{1,0:T(8,128)(2,1)S(1)}, u32[]{:S(2)}, u32[]{:S(2)}) collective-permute-start(bf16[24,4096]{1,0:T(8,128)(2,1)S(1)} %shard_map.73), channel_id=1, source_target_pairs={{0,2},{1,5},{2,0},{3,7},{4,6},{5,1},{6,4},{7,3},{8,10},{9,13},{10,... | collective-permute-start | bytes 589832 | tf_op jit(solution)/shard_map/ppermute | solution.py:288
  49.6 5.7 %collective-permute-start.12 = (bf16[16,6144]{1,0:T(8,128)(2,1)S(1)}, bf16[16,6144]{1,0:T(8,128)(2,1)S(1)}, u32[]{:S(2)}, u32[]{:S(2)}) collective-permute-start(bf16[16,6144]{1,0:T(8,128)(2,1)S(1)} %get-tuple-element.66), channel_id=1, source_target_pairs={{0,4},{1,3},{2,6},{3,1},{4,0},{5,7},{6,2},{7,5},{8,12},{9,11},{10,... | collective-permute-start | bytes 589832 | tf_op jit(solution)/shard_map/ppermute | solution.py:288
  51.0 9.7 %collective-permute-start.17 = (bf16[8,6144]{1,0:T(8,128)(2,1)S(1)}, bf16[8,6144]{1,0:T(8,128)(2,1)S(1)}, u32[]{:S(2)}, u32[]{:S(2)}) collective-permute-start(bf16[8,6144]{1,0:T(8,128)(2,1)S(1)} %get-tuple-element.71), channel_id=1, source_target_pairs={{0,16},{1,25},{2,18},{3,27},{4,20},{5,29},{6,22},{7,31},{8,24},{9,... | collective-permute-start | bytes 294920 | tf_op jit(solution)/shard_map/ppermute | solution.py:288
  54.4 6.3 %collective-permute-start.18 = (bf16[8,6144]{1,0:T(8,128)(2,1)S(1)}, bf16[8,6144]{1,0:T(8,128)(2,1)S(1)}, u32[]{:S(2)}, u32[]{:S(2)}) collective-permute-start(bf16[8,6144]{1,0:T(8,128)(2,1)S(1)} %get-tuple-element.72), channel_id=1, source_target_pairs={{0,17},{1,24},{2,19},{3,26},{4,21},{5,28},{6,23},{7,30},{8,25},{9,... | collective-permute-start | bytes 294920 | tf_op jit(solution)/shard_map/ppermute | solution.py:288
  55.4 5.3 %collective-permute-start.13 = (bf16[8,6144]{1,0:T(8,128)(2,1)S(1)}, bf16[8,6144]{1,0:T(8,128)(2,1)S(1)}, u32[]{:S(2)}, u32[]{:S(2)}) collective-permute-start(bf16[8,6144]{1,0:T(8,128)(2,1)S(1)} %shard_map.72), channel_id=1, source_target_pairs={{0,2},{1,5},{2,0},{3,7},{4,6},{5,1},{6,4},{7,3},{8,10},{9,13},{10,... | collective-permute-start | bytes 294920 | tf_op jit(solution)/shard_map/ppermute | solution.py:288

commit v5 on v4

--- a/solution.py
+++ b/solution.py
@@ -349,7 +349,7 @@
     far_second = go(far, second_flip)
     near = pair_rows(plane, width, experts)
     near_other = go(near, lambda device: 8)
-    others, far_first = lax.optimization_barrier((others, far_first))
+    weights, far_first = lax.optimization_barrier((weights, far_first))
     far_third = go(far_first, second_flip)
     weights = weights[:1] + list(fetch(weights[1:] + others))
 

time: 62.6 us -> 61 us (0.974)
  local copies, waits for them, and re-layouts: 2.85 us -> 0 us
  waiting for transfers between devices: 21.5 us -> 23.1 us
    unnamed x8 -> x0, local copies, waits for them, and re-layouts: 2.85 us -> none
    ppermute x19, waiting for transfers between devices: 21.5 us -> 23.1 us  [permute(): return lax.ppermute(value, 'expert', pairs)]
  transfers between devices with their start and end apart: 19 -> 19, of which waited for: 7 -> 8; matrix products, arithmetic and copies ran while one was open for 0% -> 0% of each run, Pallas kernels for 13% -> 13%
where the time goes in v5:
time: 61 us; the launch traced here: 60.1 us
  waiting for transfers between devices  23.1 us (38%)
  starting transfers between devices  21.9 us (36%)
  Pallas kernels  14.9 us (24%)
    ppermute x19, waiting for transfers between devices, permute(): return lax.ppermute(value, 'expert', pairs)  23.1 us
    ppermute x19, starting transfers between devices, permute(): return lax.ppermute(value, 'expert', pairs)  21.9 us
    pallas_call x12, Pallas kernels, call(): pl.pallas_call(kernel, out_shape=out_shape, in_specs=in_specs, out_specs=...  14.9 us
  transfers between devices with their start and end apart: 19, of which 8 were waited for; matrix products, arithmetic and copies ran while one was open for 0% of the time, Pallas kernels for 13%

profile of v5, /device:TPU:0, one launch (start us, length us, event | category | flops | bytes accessed | tf_op | source)
XLA Modules:
  0.0 60.1 jit_solution(8225568723160866096)
XLA Ops:
  0.0 1.0 %shard_map.64.refs_0_.a = bf16[8,6272]{1,0:T(8,128)(2,1)S(1)} custom-call(s32[8,12]{1,0:T(8,128)} %bitcast.10, f32[8,12]{1,0:T(8,128)} %bitcast.11, bf16[12,4096]{1,0:T(8,128)(2,1)} %refs_2_.1), custom_call_target="tpu_custom_call" | custom-call | tf_op jit(solution)/shard_map/pallas_call | solution.py:33
  1.0 0.5 collective-permute-start
  1.5 2.6 %collective-permute-start.2 = (bf16[8,6272]{1,0:T(8,128)(2,1)S(1)}, bf16[8,6272]{1,0:T(8,128)(2,1)S(1)}, u32[]{:S(2)}, u32[]{:S(2)}) collective-permute-start(bf16[8,6272]{1,0:T(8,128)(2,1)S(1)} %shard_map.64.refs_0_.a), channel_id=1, source_target_pairs={{0,2},{1,5},{2,0},{3,7},{4,6},{5,1},{6,4},{7,3},{8,10},{9,13},{10,... | collective-permute-start | bytes 301064 | tf_op jit(solution)/shard_map/ppermute | solution.py:288
  4.1 2.7 %collective-permute-start.1 = (bf16[24,4224]{1,0:T(8,128)(2,1)S(1)}, bf16[24,4224]{1,0:T(8,128)(2,1)}, u32[]{:S(2)}, u32[]{:S(2)}) collective-permute-start(bf16[24,4224]{1,0:T(8,128)(2,1)S(1)} %shard_map.65), channel_id=1, source_target_pairs={{0,16},{1,25},{2,18},{3,27},{4,20},{5,29},{6,22},{7,31},{8,24},{9,... | collective-permute-start | bytes 608264 | tf_op jit(solution)/shard_map/ppermute | solution.py:288
  6.8 0.9 %collective-permute-start.8 = (bf16[4096,384]{1,0:T(8,128)(2,1)}, bf16[4096,384]{1,0:T(8,128)(2,1)}, u32[]{:S(2)}, u32[]{:S(2)}) collective-permute-start(bf16[4096,384]{1,0:T(8,128)(2,1)} %bitcast.6), channel_id=1, source_target_pairs={{0,1},{1,0},{2,3},{3,2},{4,5},{5,4},{6,7},{7,6},{8,9},{9,8},{10,11... | collective-permute-start | bytes 9437192 | tf_op jit(solution)/shard_map/ppermute | solution.py:288
  7.7 1.3 %collective-permute-start.3 = (bf16[16,6272]{1,0:T(8,128)(2,1)S(1)}, bf16[16,6272]{1,0:T(8,128)(2,1)S(1)}, u32[]{:S(2)}, u32[]{:S(2)}) collective-permute-start(bf16[16,6272]{1,0:T(8,128)(2,1)S(1)} %shard_map.66), channel_id=1, source_target_pairs={{0,4},{1,3},{2,6},{3,1},{4,0},{5,7},{6,2},{7,5},{8,12},{9,11},{10,... | collective-permute-start | bytes 602120 | tf_op jit(solution)/shard_map/ppermute | solution.py:288
  9.0 1.9 %shard_map.67.refs_6_ = bf16[4096,384]{1,0:T(8,128)(2,1)S(1)} custom-call(bf16[4096,384]{1,0:T(8,128)(2,1)} %bitcast.7), custom_call_target="tpu_custom_call" | custom-call | tf_op jit(solution)/shard_map/pallas_call | solution.py:33
  10.9 2.6 %collective-permute-done.3.refs_2_ = bf16[16,6272]{1,0:T(8,128)(2,1)S(1)} collective-permute-done((bf16[16,6272]{1,0:T(8,128)(2,1)S(1)}, bf16[16,6272]{1,0:T(8,128)(2,1)S(1)}, u32[]{:S(2)}, u32[]{:S(2)}) %collective-permute-start.3) | collective-permute-done | bytes 200736 | tf_op jit(solution)/shard_map/ppermute | solution.py:288
  13.5 3.3 %collective-permute-done.1.refs_2_ = bf16[24,4224]{1,0:T(8,128)(2,1)} collective-permute-done((bf16[24,4224]{1,0:T(8,128)(2,1)S(1)}, bf16[24,4224]{1,0:T(8,128)(2,1)}, u32[]{:S(2)}, u32[]{:S(2)}) %collective-permute-start.1) | collective-permute-done | bytes 202784 | tf_op jit(solution)/shard_map/ppermute | solution.py:288
  16.7 1.5 %collective-permute-start.5 = (bf16[24,4224]{1,0:T(8,128)(2,1)}, bf16[24,4224]{1,0:T(8,128)(2,1)}, u32[]{:S(2)}, u32[]{:S(2)}) collective-permute-start(bf16[24,4224]{1,0:T(8,128)(2,1)} %collective-permute-done.1.refs_2_), channel_id=1, source_target_pairs={{0,2},{1,5},{2,0},{3,7},{4,6},{5,1},{6,4},{7,3},{8,10},{9,13},{10,... | collective-permute-start | bytes 608264 | tf_op jit(solution)/shard_map/ppermute | solution.py:288
  18.3 0.1 collective-permute-start.4
  18.4 4.4 %collective-permute-done.5.refs_3_ = bf16[24,4224]{1,0:T(8,128)(2,1)} collective-permute-done((bf16[24,4224]{1,0:T(8,128)(2,1)}, bf16[24,4224]{1,0:T(8,128)(2,1)}, u32[]{:S(2)}, u32[]{:S(2)}) %collective-permute-start.5) | collective-permute-done | bytes 202784 | tf_op jit(solution)/shard_map/ppermute | solution.py:288
  22.8 1.2 %collective-permute-start.6 = (bf16[24,4224]{1,0:T(8,128)(2,1)}, bf16[24,4224]{1,0:T(8,128)(2,1)}, u32[]{:S(2)}, u32[]{:S(2)}) collective-permute-start(bf16[24,4224]{1,0:T(8,128)(2,1)} %collective-permute-done.1.refs_2_), channel_id=1, source_target_pairs={{0,4},{1,3},{2,6},{3,1},{4,0},{5,7},{6,2},{7,5},{8,12},{9,11},{10,... | collective-permute-start | bytes 608264 | tf_op jit(solution)/shard_map/ppermute | solution.py:288
  24.0 0.8 %collective-permute-start.7 = (bf16[24,4224]{1,0:T(8,128)(2,1)}, bf16[24,4224]{1,0:T(8,128)(2,1)}, u32[]{:S(2)}, u32[]{:S(2)}) collective-permute-start(bf16[24,4224]{1,0:T(8,128)(2,1)} %collective-permute-done.5.refs_3_), channel_id=1, source_target_pairs={{0,4},{1,3},{2,6},{3,1},{4,0},{5,7},{6,2},{7,5},{8,12},{9,11},{10,... | collective-permute-start | bytes 608264 | tf_op jit(solution)/shard_map/ppermute | solution.py:288
  24.8 5.7 %shard_map.69 = (bf16[4096,384]{1,0:T(8,128)(2,1)S(1)}, bf16[384,4096]{1,0:T(8,128)(2,1)S(1)}, bf16[4096,384]{1,0:T(8,128)(2,1)S(1)}, bf16[4096,384]{1,0:T(8,128)(2,1)S(1)}, bf16[384,4096]{1,0:T(8,128)(2,1)S(1)}) custom-call(bf16[4096,384]{1,0:T(8,128)(2,1)} %bitcast.9, bf16[384,4096]{1,0:T(8,128)(2,1)} %bitcast.3.refs_1_, ...), custom_call_target="tpu_custom_call" | custom-call | tf_op jit(solution)/shard_map/pallas_call | solution.py:33
  30.5 0.5 collective-permute-done.7.refs_5_
  31.0 5.3 %shard_map.70 = (bf16[48,4096]{1,0:T(8,128)(2,1)S(1)}, bf16[48,4096]{1,0:T(8,128)(2,1)S(1)}, bf16[24,4096]{1,0:T(8,128)(2,1)S(1)}, bf16[24,4096]{1,0:T(8,128)(2,...) custom-call(s32[1]{0:T(128)} %bitcast.mine, bf16[48,4224]{1,0:T(8,128)(2,1)S(1)} %shard_map.68.refs_0_, ...), custom_call_target="tpu_custom_call" | custom-call | flops 3623878656 | tf_op jit(solution)/shard_map/pallas_call | solution.py:33
  36.3 0.1 collective-permute-start.11
  36.4 1.3 %collective-permute-start.15 = (bf16[24,4096]{1,0:T(8,128)(2,1)S(1)}, bf16[24,4096]{1,0:T(8,128)(2,1)S(1)}, u32[]{:S(2)}, u32[]{:S(2)}) collective-permute-start(bf16[24,4096]{1,0:T(8,128)(2,1)S(1)} %get-tuple-element.70), channel_id=1, source_target_pairs={{0,4},{1,3},{2,6},{3,1},{4,0},{5,7},{6,2},{7,5},{8,12},{9,11},{10,... | collective-permute-start | bytes 589832 | tf_op jit(solution)/shard_map/ppermute | solution.py:288
  37.7 0.8 %collective-permute-start.14 = (bf16[24,4096]{1,0:T(8,128)(2,1)S(1)}, bf16[24,4096]{1,0:T(8,128)(2,1)S(1)}, u32[]{:S(2)}, u32[]{:S(2)}) collective-permute-start(bf16[24,4096]{1,0:T(8,128)(2,1)S(1)} %get-tuple-element.68), channel_id=1, source_target_pairs={{0,4},{1,3},{2,6},{3,1},{4,0},{5,7},{6,2},{7,5},{8,12},{9,11},{10,... | collective-permute-start | bytes 589832 | tf_op jit(solution)/shard_map/ppermute | solution.py:288
  38.5 3.6 %collective-permute-done.15.b = bf16[24,4096]{1,0:T(8,128)(2,1)S(1)} collective-permute-done((bf16[24,4096]{1,0:T(8,128)(2,1)S(1)}, bf16[24,4096]{1,0:T(8,128)(2,1)S(1)}, u32[]{:S(2)}, u32[]{:S(2)}) %collective-permute-start.15) | collective-permute-done | bytes 196640 | tf_op jit(solution)/shard_map/ppermute | solution.py:288
  42.1 0.1 shard_map.73
  42.2 1.6 %collective-permute-start.16 = (bf16[24,4096]{1,0:T(8,128)(2,1)S(1)}, bf16[24,4096]{1,0:T(8,128)(2,1)S(1)}, u32[]{:S(2)}, u32[]{:S(2)}) collective-permute-start(bf16[24,4096]{1,0:T(8,128)(2,1)S(1)} %shard_map.73), channel_id=1, source_target_pairs={{0,2},{1,5},{2,0},{3,7},{4,6},{5,1},{6,4},{7,3},{8,10},{9,13},{10,... | collective-permute-start | bytes 589832 | tf_op jit(solution)/shard_map/ppermute | solution.py:288
  43.8 2.5 %collective-permute-done.11.refs_1_ = bf16[48,4096]{1,0:T(8,128)(2,1)S(1)} collective-permute-done((bf16[48,4096]{1,0:T(8,128)(2,1)S(1)}, bf16[48,4096]{1,0:T(8,128)(2,1)S(1)}, u32[]{:S(2)}, u32[]{:S(2)}) %collective-permute-start.11) | collective-permute-done | bytes 393248 | tf_op jit(solution)/shard_map/ppermute | solution.py:288
  46.2 0.1 shard_map.71
  46.3 1.3 %collective-permute-start.12 = (bf16[16,6144]{1,0:T(8,128)(2,1)S(1)}, bf16[16,6144]{1,0:T(8,128)(2,1)S(1)}, u32[]{:S(2)}, u32[]{:S(2)}) collective-permute-start(bf16[16,6144]{1,0:T(8,128)(2,1)S(1)} %get-tuple-element.66), channel_id=1, source_target_pairs={{0,4},{1,3},{2,6},{3,1},{4,0},{5,7},{6,2},{7,5},{8,12},{9,11},{10,... | collective-permute-start | bytes 589832 | tf_op jit(solution)/shard_map/ppermute | solution.py:288
  47.6 1.3 %collective-permute-done.16.refs_2_ = bf16[24,4096]{1,0:T(8,128)(2,1)S(1)} collective-permute-done((bf16[24,4096]{1,0:T(8,128)(2,1)S(1)}, bf16[24,4096]{1,0:T(8,128)(2,1)S(1)}, u32[]{:S(2)}, u32[]{:S(2)}) %collective-permute-start.16) | collective-permute-done | bytes 196640 | tf_op jit(solution)/shard_map/ppermute | solution.py:288
  49.0 0.1 shard_map.74
  49.1 3.8 %collective-permute-start.17 = (bf16[8,6144]{1,0:T(8,128)(2,1)S(1)}, bf16[8,6144]{1,0:T(8,128)(2,1)S(1)}, u32[]{:S(2)}, u32[]{:S(2)}) collective-permute-start(bf16[8,6144]{1,0:T(8,128)(2,1)S(1)} %get-tuple-element.71), channel_id=1, source_target_pairs={{0,16},{1,25},{2,18},{3,27},{4,20},{5,29},{6,22},{7,31},{8,24},{9,... | collective-permute-start | bytes 294920 | tf_op jit(solution)/shard_map/ppermute | solution.py:288
  52.9 1.6 %collective-permute-start.13 = (bf16[8,6144]{1,0:T(8,128)(2,1)S(1)}, bf16[8,6144]{1,0:T(8,128)(2,1)S(1)}, u32[]{:S(2)}, u32[]{:S(2)}) collective-permute-start(bf16[8,6144]{1,0:T(8,128)(2,1)S(1)} %shard_map.72), channel_id=1, source_target_pairs={{0,2},{1,5},{2,0},{3,7},{4,6},{5,1},{6,4},{7,3},{8,10},{9,13},{10,... | collective-permute-start | bytes 294920 | tf_op jit(solution)/shard_map/ppermute | solution.py:288
  54.4 4.9 %collective-permute-done.17.refs_3_ = bf16[8,6144]{1,0:T(8,128)(2,1)S(1)} collective-permute-done((bf16[8,6144]{1,0:T(8,128)(2,1)S(1)}, bf16[8,6144]{1,0:T(8,128)(2,1)S(1)}, u32[]{:S(2)}, u32[]{:S(2)}) %collective-permute-start.17) | collective-permute-done | bytes 98336 | tf_op jit(solution)/shard_map/ppermute | solution.py:288
  59.4 0.7 %shard_map.75 = bf16[12,4096]{1,0:T(8,128)(2,1)} custom-call(bf16[8,6144]{1,0:T(8,128)(2,1)S(1)} %get-tuple-element.64.refs_0_, bf16[8,6144]{1,0:T(8,128)(2,1)S(1)} %collective-permute-done.13.refs_1_, bf16[16,6144]{1,0:T(8,128)(2,1)S(1)} %collective-permute-done.12.b.refs_2_, bf16[8,6144]{1,0:T(8,128)(2,1)S(1)} %collective-permute-done.17.refs_3_, ...), custom_call_target="tpu_custom_call" | custom-call | tf_op jit(solution)/shard_map/pallas_call | solution.py:33
  (18 shorter events, 0.2 us)
Async XLA Ops:
  1.0 3.1 %collective-permute-start = (bf16[8,6272]{1,0:T(8,128)(2,1)S(1)}, bf16[8,6272]{1,0:T(8,128)(2,1)S(1)}, u32[]{:S(2)}, u32[]{:S(2)}) collective-permute-start(bf16[8,6272]{1,0:T(8,128)(2,1)S(1)} %shard_map.64.refs_0_.a), channel_id=1, source_target_pairs={{0,1},{1,0},{2,3},{3,2},{4,5},{5,4},{6,7},{7,6},{8,9},{9,8},{10,11... | collective-permute-start | bytes 301064 | tf_op jit(solution)/shard_map/ppermute | solution.py:288
  1.5 6.2 %collective-permute-start.2 = (bf16[8,6272]{1,0:T(8,128)(2,1)S(1)}, bf16[8,6272]{1,0:T(8,128)(2,1)S(1)}, u32[]{:S(2)}, u32[]{:S(2)}) collective-permute-start(bf16[8,6272]{1,0:T(8,128)(2,1)S(1)} %shard_map.64.refs_0_.a), channel_id=1, source_target_pairs={{0,2},{1,5},{2,0},{3,7},{4,6},{5,1},{6,4},{7,3},{8,10},{9,13},{10,... | collective-permute-start | bytes 301064 | tf_op jit(solution)/shard_map/ppermute | solution.py:288
  4.1 12.6 %collective-permute-start.1 = (bf16[24,4224]{1,0:T(8,128)(2,1)S(1)}, bf16[24,4224]{1,0:T(8,128)(2,1)}, u32[]{:S(2)}, u32[]{:S(2)}) collective-permute-start(bf16[24,4224]{1,0:T(8,128)(2,1)S(1)} %shard_map.65), channel_id=1, source_target_pairs={{0,16},{1,25},{2,18},{3,27},{4,20},{5,29},{6,22},{7,31},{8,24},{9,... | collective-permute-start | bytes 608264 | tf_op jit(solution)/shard_map/ppermute | solution.py:288
  6.8 17.3 %collective-permute-start.8 = (bf16[4096,384]{1,0:T(8,128)(2,1)}, bf16[4096,384]{1,0:T(8,128)(2,1)}, u32[]{:S(2)}, u32[]{:S(2)}) collective-permute-start(bf16[4096,384]{1,0:T(8,128)(2,1)} %bitcast.6), channel_id=1, source_target_pairs={{0,1},{1,0},{2,3},{3,2},{4,5},{5,4},{6,7},{7,6},{8,9},{9,8},{10,11... | collective-permute-start | bytes 9437192 | tf_op jit(solution)/shard_map/ppermute | solution.py:288
  7.7 5.8 %collective-permute-start.3 = (bf16[16,6272]{1,0:T(8,128)(2,1)S(1)}, bf16[16,6272]{1,0:T(8,128)(2,1)S(1)}, u32[]{:S(2)}, u32[]{:S(2)}) collective-permute-start(bf16[16,6272]{1,0:T(8,128)(2,1)S(1)} %shard_map.66), channel_id=1, source_target_pairs={{0,4},{1,3},{2,6},{3,1},{4,0},{5,7},{6,2},{7,5},{8,12},{9,11},{10,... | collective-permute-start | bytes 602120 | tf_op jit(solution)/shard_map/ppermute | solution.py:288
  9.0 15.8 %collective-permute-start.9 = (bf16[4096,384]{1,0:T(8,128)(2,1)}, bf16[4096,384]{1,0:T(8,128)(2,1)}, u32[]{:S(2)}, u32[]{:S(2)}) collective-permute-start(bf16[4096,384]{1,0:T(8,128)(2,1)} %bitcast.8), channel_id=1, source_target_pairs={{0,1},{1,0},{2,3},{3,2},{4,5},{5,4},{6,7},{7,6},{8,9},{9,8},{10,11... | collective-permute-start | bytes 9437192 | tf_op jit(solution)/shard_map/ppermute | solution.py:288
  16.7 8.1 %collective-permute-start.10 = (bf16[384,4096]{1,0:T(8,128)(2,1)}, bf16[384,4096]{1,0:T(8,128)(2,1)}, u32[]{:S(2)}, u32[]{:S(2)}) collective-permute-start(bf16[384,4096]{1,0:T(8,128)(2,1)} %bitcast.3.refs_1_), channel_id=1, source_target_pairs={{0,1},{1,0},{2,3},{3,2},{4,5},{5,4},{6,7},{7,6},{8,9},{9,8},{10,11... | collective-permute-start | bytes 9437192 | tf_op jit(solution)/shard_map/ppermute | solution.py:288
  16.7 6.1 %collective-permute-start.5 = (bf16[24,4224]{1,0:T(8,128)(2,1)}, bf16[24,4224]{1,0:T(8,128)(2,1)}, u32[]{:S(2)}, u32[]{:S(2)}) collective-permute-start(bf16[24,4224]{1,0:T(8,128)(2,1)} %collective-permute-done.1.refs_2_), channel_id=1, source_target_pairs={{0,2},{1,5},{2,0},{3,7},{4,6},{5,1},{6,4},{7,3},{8,10},{9,13},{10,... | collective-permute-start | bytes 608264 | tf_op jit(solution)/shard_map/ppermute | solution.py:288
  18.3 12.7 %collective-permute-start.4 = (bf16[48,4224]{1,0:T(8,128)(2,1)S(1)}, bf16[48,4224]{1,0:T(8,128)(2,1)}, u32[]{:S(2)}, u32[]{:S(2)}) collective-permute-start(bf16[48,4224]{1,0:T(8,128)(2,1)S(1)} %shard_map.68.refs_0_), channel_id=1, source_target_pairs={{0,8},{1,9},{2,10},{3,11},{4,12},{5,13},{6,14},{7,15},{8,0},{9,1},... | collective-permute-start | bytes 1216520 | tf_op jit(solution)/shard_map/ppermute | solution.py:288
  22.8 7.7 %collective-permute-start.6 = (bf16[24,4224]{1,0:T(8,128)(2,1)}, bf16[24,4224]{1,0:T(8,128)(2,1)}, u32[]{:S(2)}, u32[]{:S(2)}) collective-permute-start(bf16[24,4224]{1,0:T(8,128)(2,1)} %collective-permute-done.1.refs_2_), channel_id=1, source_target_pairs={{0,4},{1,3},{2,6},{3,1},{4,0},{5,7},{6,2},{7,5},{8,12},{9,11},{10,... | collective-permute-start | bytes 608264 | tf_op jit(solution)/shard_map/ppermute | solution.py:288
  24.0 7.0 %collective-permute-start.7 = (bf16[24,4224]{1,0:T(8,128)(2,1)}, bf16[24,4224]{1,0:T(8,128)(2,1)}, u32[]{:S(2)}, u32[]{:S(2)}) collective-permute-start(bf16[24,4224]{1,0:T(8,128)(2,1)} %collective-permute-done.5.refs_3_), channel_id=1, source_target_pairs={{0,4},{1,3},{2,6},{3,1},{4,0},{5,7},{6,2},{7,5},{8,12},{9,11},{10,... | collective-permute-start | bytes 608264 | tf_op jit(solution)/shard_map/ppermute | solution.py:288
  36.3 9.9 %collective-permute-start.11 = (bf16[48,4096]{1,0:T(8,128)(2,1)S(1)}, bf16[48,4096]{1,0:T(8,128)(2,1)S(1)}, u32[]{:S(2)}, u32[]{:S(2)}) collective-permute-start(bf16[48,4096]{1,0:T(8,128)(2,1)S(1)} %get-tuple-element.63), channel_id=1, source_target_pairs={{0,8},{1,9},{2,10},{3,11},{4,12},{5,13},{6,14},{7,15},{8,0},{9,1},... | collective-permute-start | bytes 1179656 | tf_op jit(solution)/shard_map/ppermute | solution.py:288
  36.4 5.7 %collective-permute-start.15 = (bf16[24,4096]{1,0:T(8,128)(2,1)S(1)}, bf16[24,4096]{1,0:T(8,128)(2,1)S(1)}, u32[]{:S(2)}, u32[]{:S(2)}) collective-permute-start(bf16[24,4096]{1,0:T(8,128)(2,1)S(1)} %get-tuple-element.70), channel_id=1, source_target_pairs={{0,4},{1,3},{2,6},{3,1},{4,0},{5,7},{6,2},{7,5},{8,12},{9,11},{10,... | collective-permute-start | bytes 589832 | tf_op jit(solution)/shard_map/ppermute | solution.py:288
  37.7 9.9 %collective-permute-start.14 = (bf16[24,4096]{1,0:T(8,128)(2,1)S(1)}, bf16[24,4096]{1,0:T(8,128)(2,1)S(1)}, u32[]{:S(2)}, u32[]{:S(2)}) collective-permute-start(bf16[24,4096]{1,0:T(8,128)(2,1)S(1)} %get-tuple-element.68), channel_id=1, source_target_pairs={{0,4},{1,3},{2,6},{3,1},{4,0},{5,7},{6,2},{7,5},{8,12},{9,11},{10,... | collective-permute-start | bytes 589832 | tf_op jit(solution)/shard_map/ppermute | solution.py:288
  42.2 6.8 %collective-permute-start.16 = (bf16[24,4096]{1,0:T(8,128)(2,1)S(1)}, bf16[24,4096]{1,0:T(8,128)(2,1)S(1)}, u32[]{:S(2)}, u32[]{:S(2)}) collective-permute-start(bf16[24,4096]{1,0:T(8,128)(2,1)S(1)} %shard_map.73), channel_id=1, source_target_pairs={{0,2},{1,5},{2,0},{3,7},{4,6},{5,1},{6,4},{7,3},{8,10},{9,13},{10,... | collective-permute-start | bytes 589832 | tf_op jit(solution)/shard_map/ppermute | solution.py:288
  46.3 6.5 %collective-permute-start.12 = (bf16[16,6144]{1,0:T(8,128)(2,1)S(1)}, bf16[16,6144]{1,0:T(8,128)(2,1)S(1)}, u32[]{:S(2)}, u32[]{:S(2)}) collective-permute-start(bf16[16,6144]{1,0:T(8,128)(2,1)S(1)} %get-tuple-element.66), channel_id=1, source_target_pairs={{0,4},{1,3},{2,6},{3,1},{4,0},{5,7},{6,2},{7,5},{8,12},{9,11},{10,... | collective-permute-start | bytes 589832 | tf_op jit(solution)/shard_map/ppermute | solution.py:288
  49.1 10.3 %collective-permute-start.17 = (bf16[8,6144]{1,0:T(8,128)(2,1)S(1)}, bf16[8,6144]{1,0:T(8,128)(2,1)S(1)}, u32[]{:S(2)}, u32[]{:S(2)}) collective-permute-start(bf16[8,6144]{1,0:T(8,128)(2,1)S(1)} %get-tuple-element.71), channel_id=1, source_target_pairs={{0,16},{1,25},{2,18},{3,27},{4,20},{5,29},{6,22},{7,31},{8,24},{9,... | collective-permute-start | bytes 294920 | tf_op jit(solution)/shard_map/ppermute | solution.py:288
  52.8 6.6 %collective-permute-start.18 = (bf16[8,6144]{1,0:T(8,128)(2,1)S(1)}, bf16[8,6144]{1,0:T(8,128)(2,1)S(1)}, u32[]{:S(2)}, u32[]{:S(2)}) collective-permute-start(bf16[8,6144]{1,0:T(8,128)(2,1)S(1)} %get-tuple-element.72), channel_id=1, source_target_pairs={{0,17},{1,24},{2,19},{3,26},{4,21},{5,28},{6,23},{7,30},{8,25},{9,... | collective-permute-start | bytes 294920 | tf_op jit(solution)/shard_map/ppermute | solution.py:288
  52.9 6.5 %collective-permute-start.13 = (bf16[8,6144]{1,0:T(8,128)(2,1)S(1)}, bf16[8,6144]{1,0:T(8,128)(2,1)S(1)}, u32[]{:S(2)}, u32[]{:S(2)}) collective-permute-start(bf16[8,6144]{1,0:T(8,128)(2,1)S(1)} %shard_map.72), channel_id=1, source_target_pairs={{0,2},{1,5},{2,0},{3,7},{4,6},{5,1},{6,4},{7,3},{8,10},{9,13},{10,... | collective-permute-start | bytes 294920 | tf_op jit(solution)/shard_map/ppermute | solution.py:288

commit v6 on v5

--- a/solution.py
+++ b/solution.py
@@ -341,8 +341,6 @@
     far = far[0] if len(far) == 1 else jnp.concatenate(far, axis=0)
     own_first = go(own, first_flip)
     plane = (own, own_first, go(join(own, own_first), second_flip))
-    weights, own_first = lax.optimization_barrier((weights, own_first))
-    weights = list(fetch(weights[:1])) + weights[1:]
     far, plane, weights = lax.optimization_barrier((far, plane, weights))
     others.append(go(weights[2], lambda device: 1))
     far_first = go(far, first_flip)
@@ -351,7 +349,7 @@
     near_other = go(near, lambda device: 8)
     weights, far_first = lax.optimization_barrier((weights, far_first))
     far_third = go(far_first, second_flip)
-    weights = weights[:1] + list(fetch(weights[1:] + others))
+    weights = list(fetch(weights + others))
 
     many, more = far.shape[0], near.shape[0]
     near, near_other, far, far_first, far_second, far_third = expert_rows(

time: 61 us -> 59.8 us (0.980)
  Pallas kernels: 14.9 us -> 12.7 us
  starting transfers between devices: 21.9 us -> 22.6 us
    pallas_call x12 -> x11, Pallas kernels: 14.9 us -> 12.7 us  [call(): pl.pallas_call(kernel, out_shape=out_shape, in_specs=in_specs, out_specs=...]
    ppermute x19, starting transfers between devices: 21.9 us -> 22.6 us  [permute(): return lax.ppermute(value, 'expert', pairs)]
  transfers between devices with their start and end apart: 19 -> 19, of which waited for: 8 -> 7; matrix products, arithmetic and copies ran while one was open for 0% -> 0% of each run, Pallas kernels for 13% -> 12%
where the time goes in v6:
time: 59.8 us; the launch traced here: 59.2 us
  waiting for transfers between devices  23.7 us (40%)
  starting transfers between devices  22.6 us (38%)
  Pallas kernels  12.7 us (21%)
    ppermute x19, waiting for transfers between devices, permute(): return lax.ppermute(value, 'expert', pairs)  23.7 us
    ppermute x19, starting transfers between devices, permute(): return lax.ppermute(value, 'expert', pairs)  22.6 us
    pallas_call x11, Pallas kernels, call(): pl.pallas_call(kernel, out_shape=out_shape, in_specs=in_specs, out_specs=...  12.7 us
  transfers between devices with their start and end apart: 19, of which 7 were waited for; matrix products, arithmetic and copies ran while one was open for 0% of the time, Pallas kernels for 12%

profile of v6, /device:TPU:0, one launch (start us, length us, event | category | flops | bytes accessed | tf_op | source)
XLA Modules:
  0.0 59.2 jit_solution(8905865737898068887)
XLA Ops:
  0.0 1.0 %shard_map.64.refs_0_.a = bf16[8,6272]{1,0:T(8,128)(2,1)S(1)} custom-call(s32[8,12]{1,0:T(8,128)} %bitcast.12, f32[8,12]{1,0:T(8,128)} %bitcast.13, bf16[12,4096]{1,0:T(8,128)(2,1)} %refs_2_.1), custom_call_target="tpu_custom_call" | custom-call | tf_op jit(solution)/shard_map/pallas_call | solution.py:33
  1.0 0.5 collective-permute-start
  1.5 2.6 %collective-permute-start.2 = (bf16[8,6272]{1,0:T(8,128)(2,1)S(1)}, bf16[8,6272]{1,0:T(8,128)(2,1)S(1)}, u32[]{:S(2)}, u32[]{:S(2)}) collective-permute-start(bf16[8,6272]{1,0:T(8,128)(2,1)S(1)} %shard_map.64.refs_0_.a), channel_id=1, source_target_pairs={{0,2},{1,5},{2,0},{3,7},{4,6},{5,1},{6,4},{7,3},{8,10},{9,13},{10,... | collective-permute-start | bytes 301064 | tf_op jit(solution)/shard_map/ppermute | solution.py:288
  4.1 0.0 collective-permute-done.refs_1_
  4.1 2.7 %collective-permute-start.1 = (bf16[24,4224]{1,0:T(8,128)(2,1)S(1)}, bf16[24,4224]{1,0:T(8,128)(2,1)S(1)}, u32[]{:S(2)}, u32[]{:S(2)}) collective-permute-start(bf16[24,4224]{1,0:T(8,128)(2,1)S(1)} %shard_map.65), channel_id=1, source_target_pairs={{0,16},{1,25},{2,18},{3,27},{4,20},{5,29},{6,22},{7,31},{8,24},{9,... | collective-permute-start | bytes 608264 | tf_op jit(solution)/shard_map/ppermute | solution.py:288
  6.8 0.9 %collective-permute-start.8 = (bf16[4096,384]{1,0:T(8,128)(2,1)}, bf16[4096,384]{1,0:T(8,128)(2,1)}, u32[]{:S(2)}, u32[]{:S(2)}) collective-permute-start(bf16[4096,384]{1,0:T(8,128)(2,1)} %bitcast.6), channel_id=1, source_target_pairs={{0,1},{1,0},{2,3},{3,2},{4,5},{5,4},{6,7},{7,6},{8,9},{9,8},{10,11... | collective-permute-start | bytes 9437192 | tf_op jit(solution)/shard_map/ppermute | solution.py:288
  7.7 0.0 collective-permute-done.2.b.refs_1_
  7.7 1.3 %collective-permute-start.3 = (bf16[16,6272]{1,0:T(8,128)(2,1)S(1)}, bf16[16,6272]{1,0:T(8,128)(2,1)S(1)}, u32[]{:S(2)}, u32[]{:S(2)}) collective-permute-start(bf16[16,6272]{1,0:T(8,128)(2,1)S(1)} %shard_map.66), channel_id=1, source_target_pairs={{0,4},{1,3},{2,6},{3,1},{4,0},{5,7},{6,2},{7,5},{8,12},{9,11},{10,... | collective-permute-start | bytes 602120 | tf_op jit(solution)/shard_map/ppermute | solution.py:288
  9.0 4.5 %collective-permute-done.3.refs_2_ = bf16[16,6272]{1,0:T(8,128)(2,1)S(1)} collective-permute-done((bf16[16,6272]{1,0:T(8,128)(2,1)S(1)}, bf16[16,6272]{1,0:T(8,128)(2,1)S(1)}, u32[]{:S(2)}, u32[]{:S(2)}) %collective-permute-start.3) | collective-permute-done | bytes 200736 | tf_op jit(solution)/shard_map/ppermute | solution.py:288
  13.5 3.2 %collective-permute-done.1.refs_2_ = bf16[24,4224]{1,0:T(8,128)(2,1)S(1)} collective-permute-done((bf16[24,4224]{1,0:T(8,128)(2,1)S(1)}, bf16[24,4224]{1,0:T(8,128)(2,1)S(1)}, u32[]{:S(2)}, u32[]{:S(2)}) %collective-permute-start.1) | collective-permute-done | bytes 202784 | tf_op jit(solution)/shard_map/ppermute | solution.py:288
  16.6 1.5 %collective-permute-start.5 = (bf16[24,4224]{1,0:T(8,128)(2,1)S(1)}, bf16[24,4224]{1,0:T(8,128)(2,1)S(1)}, u32[]{:S(2)}, u32[]{:S(2)}) collective-permute-start(bf16[24,4224]{1,0:T(8,128)(2,1)S(1)} %collective-permute-done.1.refs_2_), channel_id=1, source_target_pairs={{0,2},{1,5},{2,0},{3,7},{4,6},{5,1},{6,4},{7,3},{8,10},{9,13},{10,... | collective-permute-start | bytes 608264 | tf_op jit(solution)/shard_map/ppermute | solution.py:288
  18.2 0.1 collective-permute-start.4
  18.3 4.1 %collective-permute-done.5.refs_3_ = bf16[24,4224]{1,0:T(8,128)(2,1)S(1)} collective-permute-done((bf16[24,4224]{1,0:T(8,128)(2,1)S(1)}, bf16[24,4224]{1,0:T(8,128)(2,1)S(1)}, u32[]{:S(2)}, u32[]{:S(2)}) %collective-permute-start.5) | collective-permute-done | bytes 202784 | tf_op jit(solution)/shard_map/ppermute | solution.py:288
  22.4 1.2 %collective-permute-start.6 = (bf16[24,4224]{1,0:T(8,128)(2,1)S(1)}, bf16[24,4224]{1,0:T(8,128)(2,1)S(1)}, u32[]{:S(2)}, u32[]{:S(2)}) collective-permute-start(bf16[24,4224]{1,0:T(8,128)(2,1)S(1)} %collective-permute-done.1.refs_2_), channel_id=1, source_target_pairs={{0,4},{1,3},{2,6},{3,1},{4,0},{5,7},{6,2},{7,5},{8,12},{9,11},{10,... | collective-permute-start | bytes 608264 | tf_op jit(solution)/shard_map/ppermute | solution.py:288
  23.6 0.8 %collective-permute-start.7 = (bf16[24,4224]{1,0:T(8,128)(2,1)S(1)}, bf16[24,4224]{1,0:T(8,128)(2,1)S(1)}, u32[]{:S(2)}, u32[]{:S(2)}) collective-permute-start(bf16[24,4224]{1,0:T(8,128)(2,1)S(1)} %collective-permute-done.5.refs_3_), channel_id=1, source_target_pairs={{0,4},{1,3},{2,6},{3,1},{4,0},{5,7},{6,2},{7,5},{8,12},{9,11},{10,... | collective-permute-start | bytes 608264 | tf_op jit(solution)/shard_map/ppermute | solution.py:288
  24.4 6.6 %shard_map.68 = (bf16[4096,384]{1,0:T(8,128)(2,1)S(1)}, bf16[4096,384]{1,0:T(8,128)(2,1)S(1)}, bf16[384,4096]{1,0:T(8,128)(2,1)S(1)}, bf16[4096,384]{1,0:T(8,128...) custom-call(bf16[4096,384]{1,0:T(8,128)(2,1)} %bitcast.7, bf16[4096,384]{1,0:T(8,128)(2,1)} %bitcast.9, ...), custom_call_target="tpu_custom_call" | custom-call | tf_op jit(solution)/shard_map/pallas_call | solution.py:33
  31.1 4.0 %shard_map.69 = (bf16[48,4096]{1,0:T(8,128)(2,1)S(1)}, bf16[48,4096]{1,0:T(8,128)(2,1)S(1)}, bf16[24,4096]{1,0:T(8,128)(2,1)S(1)}, bf16[24,4096]{1,0:T(8,128)(2,...) custom-call(s32[1]{0:T(128)} %bitcast.mine, bf16[48,4224]{1,0:T(8,128)(2,1)S(1)} %shard_map.67.refs_0_, ...), custom_call_target="tpu_custom_call" | custom-call | flops 3623878656 | tf_op jit(solution)/shard_map/pallas_call | solution.py:33
  35.1 0.1 collective-permute-start.11
  35.2 1.3 %collective-permute-start.15 = (bf16[24,4096]{1,0:T(8,128)(2,1)S(1)}, bf16[24,4096]{1,0:T(8,128)(2,1)S(1)}, u32[]{:S(2)}, u32[]{:S(2)}) collective-permute-start(bf16[24,4096]{1,0:T(8,128)(2,1)S(1)} %get-tuple-element.66), channel_id=1, source_target_pairs={{0,4},{1,3},{2,6},{3,1},{4,0},{5,7},{6,2},{7,5},{8,12},{9,11},{10,... | collective-permute-start | bytes 589832 | tf_op jit(solution)/shard_map/ppermute | solution.py:288
  36.5 0.8 %collective-permute-start.14 = (bf16[24,4096]{1,0:T(8,128)(2,1)S(1)}, bf16[24,4096]{1,0:T(8,128)(2,1)S(1)}, u32[]{:S(2)}, u32[]{:S(2)}) collective-permute-start(bf16[24,4096]{1,0:T(8,128)(2,1)S(1)} %get-tuple-element.64), channel_id=1, source_target_pairs={{0,4},{1,3},{2,6},{3,1},{4,0},{5,7},{6,2},{7,5},{8,12},{9,11},{10,... | collective-permute-start | bytes 589832 | tf_op jit(solution)/shard_map/ppermute | solution.py:288
  37.3 3.6 %collective-permute-done.15.b = bf16[24,4096]{1,0:T(8,128)(2,1)S(1)} collective-permute-done((bf16[24,4096]{1,0:T(8,128)(2,1)S(1)}, bf16[24,4096]{1,0:T(8,128)(2,1)S(1)}, u32[]{:S(2)}, u32[]{:S(2)}) %collective-permute-start.15) | collective-permute-done | bytes 196640 | tf_op jit(solution)/shard_map/ppermute | solution.py:288
  40.9 0.1 shard_map.72
  41.0 1.6 %collective-permute-start.16 = (bf16[24,4096]{1,0:T(8,128)(2,1)S(1)}, bf16[24,4096]{1,0:T(8,128)(2,1)S(1)}, u32[]{:S(2)}, u32[]{:S(2)}) collective-permute-start(bf16[24,4096]{1,0:T(8,128)(2,1)S(1)} %shard_map.72), channel_id=1, source_target_pairs={{0,2},{1,5},{2,0},{3,7},{4,6},{5,1},{6,4},{7,3},{8,10},{9,13},{10,... | collective-permute-start | bytes 589832 | tf_op jit(solution)/shard_map/ppermute | solution.py:288
  42.5 2.7 %collective-permute-done.11.refs_1_ = bf16[48,4096]{1,0:T(8,128)(2,1)S(1)} collective-permute-done((bf16[48,4096]{1,0:T(8,128)(2,1)S(1)}, bf16[48,4096]{1,0:T(8,128)(2,1)S(1)}, u32[]{:S(2)}, u32[]{:S(2)}) %collective-permute-start.11) | collective-permute-done | bytes 393248 | tf_op jit(solution)/shard_map/ppermute | solution.py:288
  45.3 0.1 shard_map.70
  45.4 1.3 %collective-permute-start.12 = (bf16[16,6144]{1,0:T(8,128)(2,1)S(1)}, bf16[16,6144]{1,0:T(8,128)(2,1)S(1)}, u32[]{:S(2)}, u32[]{:S(2)}) collective-permute-start(bf16[16,6144]{1,0:T(8,128)(2,1)S(1)} %get-tuple-element.62), channel_id=1, source_target_pairs={{0,4},{1,3},{2,6},{3,1},{4,0},{5,7},{6,2},{7,5},{8,12},{9,11},{10,... | collective-permute-start | bytes 589832 | tf_op jit(solution)/shard_map/ppermute | solution.py:288
  46.7 0.4 collective-permute-done.16.refs_2_
  47.1 0.1 shard_map.73
  47.2 4.5 %collective-permute-start.17 = (bf16[8,6144]{1,0:T(8,128)(2,1)S(1)}, bf16[8,6144]{1,0:T(8,128)(2,1)S(1)}, u32[]{:S(2)}, u32[]{:S(2)}) collective-permute-start(bf16[8,6144]{1,0:T(8,128)(2,1)S(1)} %get-tuple-element.67), channel_id=1, source_target_pairs={{0,16},{1,25},{2,18},{3,27},{4,20},{5,29},{6,22},{7,31},{8,24},{9,... | collective-permute-start | bytes 294920 | tf_op jit(solution)/shard_map/ppermute | solution.py:288
  51.7 1.6 %collective-permute-start.13 = (bf16[8,6144]{1,0:T(8,128)(2,1)S(1)}, bf16[8,6144]{1,0:T(8,128)(2,1)S(1)}, u32[]{:S(2)}, u32[]{:S(2)}) collective-permute-start(bf16[8,6144]{1,0:T(8,128)(2,1)S(1)} %shard_map.71), channel_id=1, source_target_pairs={{0,2},{1,5},{2,0},{3,7},{4,6},{5,1},{6,4},{7,3},{8,10},{9,13},{10,... | collective-permute-start | bytes 294920 | tf_op jit(solution)/shard_map/ppermute | solution.py:288
  53.3 5.2 %collective-permute-done.17.refs_3_ = bf16[8,6144]{1,0:T(8,128)(2,1)S(1)} collective-permute-done((bf16[8,6144]{1,0:T(8,128)(2,1)S(1)}, bf16[8,6144]{1,0:T(8,128)(2,1)S(1)}, u32[]{:S(2)}, u32[]{:S(2)}) %collective-permute-start.17) | collective-permute-done | bytes 98336 | tf_op jit(solution)/shard_map/ppermute | solution.py:288
  58.4 0.7 %shard_map.74 = bf16[12,4096]{1,0:T(8,128)(2,1)} custom-call(bf16[8,6144]{1,0:T(8,128)(2,1)S(1)} %get-tuple-element.60.refs_0_, bf16[8,6144]{1,0:T(8,128)(2,1)S(1)} %collective-permute-done.13.refs_1_, bf16[16,6144]{1,0:T(8,128)(2,1)S(1)} %collective-permute-done.12.b.refs_2_, bf16[8,6144]{1,0:T(8,128)(2,1)S(1)} %collective-permute-done.17.refs_3_, ...), custom_call_target="tpu_custom_call" | custom-call | tf_op jit(solution)/shard_map/pallas_call | solution.py:33
  (17 shorter events, 0.2 us)
Async XLA Ops:
  1.0 3.1 %collective-permute-start = (bf16[8,6272]{1,0:T(8,128)(2,1)S(1)}, bf16[8,6272]{1,0:T(8,128)(2,1)S(1)}, u32[]{:S(2)}, u32[]{:S(2)}) collective-permute-start(bf16[8,6272]{1,0:T(8,128)(2,1)S(1)} %shard_map.64.refs_0_.a), channel_id=1, source_target_pairs={{0,1},{1,0},{2,3},{3,2},{4,5},{5,4},{6,7},{7,6},{8,9},{9,8},{10,11... | collective-permute-start | bytes 301064 | tf_op jit(solution)/shard_map/ppermute | solution.py:288
  1.5 6.2 %collective-permute-start.2 = (bf16[8,6272]{1,0:T(8,128)(2,1)S(1)}, bf16[8,6272]{1,0:T(8,128)(2,1)S(1)}, u32[]{:S(2)}, u32[]{:S(2)}) collective-permute-start(bf16[8,6272]{1,0:T(8,128)(2,1)S(1)} %shard_map.64.refs_0_.a), channel_id=1, source_target_pairs={{0,2},{1,5},{2,0},{3,7},{4,6},{5,1},{6,4},{7,3},{8,10},{9,13},{10,... | collective-permute-start | bytes 301064 | tf_op jit(solution)/shard_map/ppermute | solution.py:288
  4.1 12.5 %collective-permute-start.1 = (bf16[24,4224]{1,0:T(8,128)(2,1)S(1)}, bf16[24,4224]{1,0:T(8,128)(2,1)S(1)}, u32[]{:S(2)}, u32[]{:S(2)}) collective-permute-start(bf16[24,4224]{1,0:T(8,128)(2,1)S(1)} %shard_map.65), channel_id=1, source_target_pairs={{0,16},{1,25},{2,18},{3,27},{4,20},{5,29},{6,22},{7,31},{8,24},{9,... | collective-permute-start | bytes 608264 | tf_op jit(solution)/shard_map/ppermute | solution.py:288
  6.8 16.9 %collective-permute-start.8 = (bf16[4096,384]{1,0:T(8,128)(2,1)}, bf16[4096,384]{1,0:T(8,128)(2,1)}, u32[]{:S(2)}, u32[]{:S(2)}) collective-permute-start(bf16[4096,384]{1,0:T(8,128)(2,1)} %bitcast.6), channel_id=1, source_target_pairs={{0,1},{1,0},{2,3},{3,2},{4,5},{5,4},{6,7},{7,6},{8,9},{9,8},{10,11... | collective-permute-start | bytes 9437192 | tf_op jit(solution)/shard_map/ppermute | solution.py:288
  7.7 5.8 %collective-permute-start.3 = (bf16[16,6272]{1,0:T(8,128)(2,1)S(1)}, bf16[16,6272]{1,0:T(8,128)(2,1)S(1)}, u32[]{:S(2)}, u32[]{:S(2)}) collective-permute-start(bf16[16,6272]{1,0:T(8,128)(2,1)S(1)} %shard_map.66), channel_id=1, source_target_pairs={{0,4},{1,3},{2,6},{3,1},{4,0},{5,7},{6,2},{7,5},{8,12},{9,11},{10,... | collective-permute-start | bytes 602120 | tf_op jit(solution)/shard_map/ppermute | solution.py:288
  9.0 15.4 %collective-permute-start.9 = (bf16[4096,384]{1,0:T(8,128)(2,1)}, bf16[4096,384]{1,0:T(8,128)(2,1)}, u32[]{:S(2)}, u32[]{:S(2)}) collective-permute-start(bf16[4096,384]{1,0:T(8,128)(2,1)} %bitcast.8), channel_id=1, source_target_pairs={{0,1},{1,0},{2,3},{3,2},{4,5},{5,4},{6,7},{7,6},{8,9},{9,8},{10,11... | collective-permute-start | bytes 9437192 | tf_op jit(solution)/shard_map/ppermute | solution.py:288
  16.6 7.8 %collective-permute-start.10 = (bf16[384,4096]{1,0:T(8,128)(2,1)}, bf16[384,4096]{1,0:T(8,128)(2,1)}, u32[]{:S(2)}, u32[]{:S(2)}) collective-permute-start(bf16[384,4096]{1,0:T(8,128)(2,1)} %bitcast.10), channel_id=1, source_target_pairs={{0,1},{1,0},{2,3},{3,2},{4,5},{5,4},{6,7},{7,6},{8,9},{9,8},{10,11... | collective-permute-start | bytes 9437192 | tf_op jit(solution)/shard_map/ppermute | solution.py:288
  16.6 5.7 %collective-permute-start.5 = (bf16[24,4224]{1,0:T(8,128)(2,1)S(1)}, bf16[24,4224]{1,0:T(8,128)(2,1)S(1)}, u32[]{:S(2)}, u32[]{:S(2)}) collective-permute-start(bf16[24,4224]{1,0:T(8,128)(2,1)S(1)} %collective-permute-done.1.refs_2_), channel_id=1, source_target_pairs={{0,2},{1,5},{2,0},{3,7},{4,6},{5,1},{6,4},{7,3},{8,10},{9,13},{10,... | collective-permute-start | bytes 608264 | tf_op jit(solution)/shard_map/ppermute | solution.py:288
  18.2 12.9 %collective-permute-start.4 = (bf16[48,4224]{1,0:T(8,128)(2,1)S(1)}, bf16[48,4224]{1,0:T(8,128)(2,1)S(1)}, u32[]{:S(2)}, u32[]{:S(2)}) collective-permute-start(bf16[48,4224]{1,0:T(8,128)(2,1)S(1)} %shard_map.67.refs_0_), channel_id=1, source_target_pairs={{0,8},{1,9},{2,10},{3,11},{4,12},{5,13},{6,14},{7,15},{8,0},{9,1},... | collective-permute-start | bytes 1216520 | tf_op jit(solution)/shard_map/ppermute | solution.py:288
  22.4 8.7 %collective-permute-start.6 = (bf16[24,4224]{1,0:T(8,128)(2,1)S(1)}, bf16[24,4224]{1,0:T(8,128)(2,1)S(1)}, u32[]{:S(2)}, u32[]{:S(2)}) collective-permute-start(bf16[24,4224]{1,0:T(8,128)(2,1)S(1)} %collective-permute-done.1.refs_2_), channel_id=1, source_target_pairs={{0,4},{1,3},{2,6},{3,1},{4,0},{5,7},{6,2},{7,5},{8,12},{9,11},{10,... | collective-permute-start | bytes 608264 | tf_op jit(solution)/shard_map/ppermute | solution.py:288
  23.6 7.5 %collective-permute-start.7 = (bf16[24,4224]{1,0:T(8,128)(2,1)S(1)}, bf16[24,4224]{1,0:T(8,128)(2,1)S(1)}, u32[]{:S(2)}, u32[]{:S(2)}) collective-permute-start(bf16[24,4224]{1,0:T(8,128)(2,1)S(1)} %collective-permute-done.5.refs_3_), channel_id=1, source_target_pairs={{0,4},{1,3},{2,6},{3,1},{4,0},{5,7},{6,2},{7,5},{8,12},{9,11},{10,... | collective-permute-start | bytes 608264 | tf_op jit(solution)/shard_map/ppermute | solution.py:288
  35.1 10.2 %collective-permute-start.11 = (bf16[48,4096]{1,0:T(8,128)(2,1)S(1)}, bf16[48,4096]{1,0:T(8,128)(2,1)S(1)}, u32[]{:S(2)}, u32[]{:S(2)}) collective-permute-start(bf16[48,4096]{1,0:T(8,128)(2,1)S(1)} %get-tuple-element.59), channel_id=1, source_target_pairs={{0,8},{1,9},{2,10},{3,11},{4,12},{5,13},{6,14},{7,15},{8,0},{9,1},... | collective-permute-start | bytes 1179656 | tf_op jit(solution)/shard_map/ppermute | solution.py:288
  35.2 5.7 %collective-permute-start.15 = (bf16[24,4096]{1,0:T(8,128)(2,1)S(1)}, bf16[24,4096]{1,0:T(8,128)(2,1)S(1)}, u32[]{:S(2)}, u32[]{:S(2)}) collective-permute-start(bf16[24,4096]{1,0:T(8,128)(2,1)S(1)} %get-tuple-element.66), channel_id=1, source_target_pairs={{0,4},{1,3},{2,6},{3,1},{4,0},{5,7},{6,2},{7,5},{8,12},{9,11},{10,... | collective-permute-start | bytes 589832 | tf_op jit(solution)/shard_map/ppermute | solution.py:288
  36.5 10.2 %collective-permute-start.14 = (bf16[24,4096]{1,0:T(8,128)(2,1)S(1)}, bf16[24,4096]{1,0:T(8,128)(2,1)S(1)}, u32[]{:S(2)}, u32[]{:S(2)}) collective-permute-start(bf16[24,4096]{1,0:T(8,128)(2,1)S(1)} %get-tuple-element.64), channel_id=1, source_target_pairs={{0,4},{1,3},{2,6},{3,1},{4,0},{5,7},{6,2},{7,5},{8,12},{9,11},{10,... | collective-permute-start | bytes 589832 | tf_op jit(solution)/shard_map/ppermute | solution.py:288
  41.0 6.1 %collective-permute-start.16 = (bf16[24,4096]{1,0:T(8,128)(2,1)S(1)}, bf16[24,4096]{1,0:T(8,128)(2,1)S(1)}, u32[]{:S(2)}, u32[]{:S(2)}) collective-permute-start(bf16[24,4096]{1,0:T(8,128)(2,1)S(1)} %shard_map.72), channel_id=1, source_target_pairs={{0,2},{1,5},{2,0},{3,7},{4,6},{5,1},{6,4},{7,3},{8,10},{9,13},{10,... | collective-permute-start | bytes 589832 | tf_op jit(solution)/shard_map/ppermute | solution.py:288
  45.4 6.3 %collective-permute-start.12 = (bf16[16,6144]{1,0:T(8,128)(2,1)S(1)}, bf16[16,6144]{1,0:T(8,128)(2,1)S(1)}, u32[]{:S(2)}, u32[]{:S(2)}) collective-permute-start(bf16[16,6144]{1,0:T(8,128)(2,1)S(1)} %get-tuple-element.62), channel_id=1, source_target_pairs={{0,4},{1,3},{2,6},{3,1},{4,0},{5,7},{6,2},{7,5},{8,12},{9,11},{10,... | collective-permute-start | bytes 589832 | tf_op jit(solution)/shard_map/ppermute | solution.py:288
  47.2 11.2 %collective-permute-start.17 = (bf16[8,6144]{1,0:T(8,128)(2,1)S(1)}, bf16[8,6144]{1,0:T(8,128)(2,1)S(1)}, u32[]{:S(2)}, u32[]{:S(2)}) collective-permute-start(bf16[8,6144]{1,0:T(8,128)(2,1)S(1)} %get-tuple-element.67), channel_id=1, source_target_pairs={{0,16},{1,25},{2,18},{3,27},{4,20},{5,29},{6,22},{7,31},{8,24},{9,... | collective-permute-start | bytes 294920 | tf_op jit(solution)/shard_map/ppermute | solution.py:288
  51.7 6.7 %collective-permute-start.18 = (bf16[8,6144]{1,0:T(8,128)(2,1)S(1)}, bf16[8,6144]{1,0:T(8,128)(2,1)S(1)}, u32[]{:S(2)}, u32[]{:S(2)}) collective-permute-start(bf16[8,6144]{1,0:T(8,128)(2,1)S(1)} %get-tuple-element.68), channel_id=1, source_target_pairs={{0,17},{1,24},{2,19},{3,26},{4,21},{5,28},{6,23},{7,30},{8,25},{9,... | collective-permute-start | bytes 294920 | tf_op jit(solution)/shard_map/ppermute | solution.py:288
  51.7 6.7 %collective-permute-start.13 = (bf16[8,6144]{1,0:T(8,128)(2,1)S(1)}, bf16[8,6144]{1,0:T(8,128)(2,1)S(1)}, u32[]{:S(2)}, u32[]{:S(2)}) collective-permute-start(bf16[8,6144]{1,0:T(8,128)(2,1)S(1)} %shard_map.71), channel_id=1, source_target_pairs={{0,2},{1,5},{2,0},{3,7},{4,6},{5,1},{6,4},{7,3},{8,10},{9,13},{10,... | collective-permute-start | bytes 294920 | tf_op jit(solution)/shard_map/ppermute | solution.py:288
